TPU v7x, 32 devices: a whole 2x2x4 slice. The times are simulated.
32 devices in a mesh: replica: 1, expert: 16 (over z, y, x), tensor: 2 (over core).
Axes of the slice: x: 2, y: 2, z: 4, core: 2. Of those that a mesh axis runs over, the one named last changes fastest.
Arguments:
- token_values: bfloat16 [1024, 4096], P(('replica', 'expert'), 'tensor'), may hold values from -6 to 6
- token_scales: bfloat16 [1024, 32], P(('replica', 'expert'), 'tensor'), may hold values from 0.19921875 to 2.5
- expert_ids: int32 [1024, 8], P(('replica', 'expert')), may hold values from 0 to 15, all different within a row; in each aligned block of 64 rows (0 to 63, 64 to 127, ...) at most 40 rows name the same one
- route_weights: int32 [1024, 8], P(('replica', 'expert')), may hold values from 1 to 4095
- gate_weight: bfloat16 [16, 4096, 768], P('expert', None, 'tensor'), may hold values from -0.09375 to 0.09375
- up_weight: bfloat16 [16, 4096, 768], P('expert', None, 'tensor'), may hold values from -0.09375 to 0.09375
- down_weight: bfloat16 [16, 768, 4096], P('expert', 'tensor'), may hold values from -0.21875 to 0.21875
Outputs:
- mixed: bfloat16 [1024, 4096], P(('replica', 'expert'), 'tensor')
Inputs may be any that keep to these rules, and one draw needn't show every extreme that they name: `expert_ids`: each row names 8 different experts. In each aligned block of 64 rows (the tokens of one index of expert) no expert is named by more than 40 rows, a bound that some block reaches.
All inputs are finite; a program needn't handle non-finite values.
Results may differ from a plain program's by a relative error of at most 0.0076.
Values may be sent and summed in bfloat16 or wider, within the bound.
No kernel may reach another device: no remote copies, remote signals or barrier semaphores. Data moves between devices by JAX's collectives and lax.ppermute only.
A program may use at most 128 MiB of HBM per device.

v0:
```python
import math

import jax
import jax.numpy as jnp
from jax import lax
from jax.sharding import PartitionSpec as P

WALSH = 128


def partner_2(array, axis, bit):
    return lax.ppermute(array, axis, [(i, i ^ 1 << bit) for i in range(lax.axis_size(axis))])


def walsh_signs(length):
    indices = jnp.arange(length, dtype=jnp.int32)
    parity = jnp.zeros((length, length), jnp.int32)
    for bit_index in range(length.bit_length() - 1):
        parity = parity + jnp.bitwise_and(
            jnp.bitwise_and(
                jnp.right_shift(indices[:, None], bit_index),
                jnp.right_shift(indices[None, :], bit_index),
            ),
            1,
        )
    return (1 - 2 * (parity % 2)).astype(jnp.float32)


def shards(
    token_values, token_scales, expert_ids, route_weights, gate_weight, up_weight, down_weight
):
    tok_rows, top_count = expert_ids.shape
    experts = lax.axis_size("expert")
    capacity = min(tok_rows, 5 * tok_rows * top_count // (4 * experts))
    flat_ids = expert_ids.reshape(-1)
    onehot = (flat_ids[:, None] == jnp.arange(experts, dtype=jnp.int32)[None, :]).astype(jnp.int32)
    slot_index = jnp.sum(jnp.cumsum(onehot, axis=0) * onehot, axis=1) - 1
    target = flat_ids * capacity + slot_index
    owner_token = jnp.arange(tok_rows * top_count, dtype=jnp.int32) // top_count
    source = jnp.full((experts * capacity,), tok_rows, jnp.int32).at[target].set(owner_token)
    padded_values = jnp.concatenate(
        [token_values, jnp.zeros((1, token_values.shape[1]), token_values.dtype)], axis=0
    )
    padded_scales = jnp.concatenate(
        [token_scales, jnp.zeros((1, token_scales.shape[1]), token_scales.dtype)], axis=0
    )
    send_values = padded_values[source].reshape(experts, capacity, -1)
    send_scales = padded_scales[source].reshape(experts, capacity, -1)
    arrived_values, arrived_scales = (
        lax.all_to_all(send_values, "expert", split_axis=0, concat_axis=0, tiled=True),
        lax.all_to_all(send_scales, "expert", split_axis=0, concat_axis=0, tiled=True),
    )
    joined_values, joined_scales = (
        lax.all_gather(arrived_values, "tensor", axis=2, tiled=True),
        lax.all_gather(arrived_scales, "tensor", axis=2, tiled=True),
    )
    row_count = experts * capacity
    feature_count = joined_values.shape[2]
    scale_count = joined_scales.shape[2]
    dequant = (
        (
            joined_values.astype(jnp.float32).reshape(
                row_count, scale_count, feature_count // scale_count
            )
            * joined_scales.astype(jnp.float32).reshape(row_count, scale_count, 1)
        )
        .reshape(row_count, feature_count)
        .astype(jnp.bfloat16)
    )
    gate_out = jnp.dot(dequant, gate_weight[0], preferred_element_type=jnp.float32)
    up_out = jnp.dot(dequant, up_weight[0], preferred_element_type=jnp.float32)
    hidden = (jax.nn.silu(gate_out) * up_out).astype(jnp.bfloat16)
    partner = partner_2(hidden, "tensor", 0)
    own_part = hidden.astype(jnp.float32)
    theirs = partner.astype(jnp.float32)
    combined = jnp.where(lax.axis_index("tensor") == 0, own_part + theirs, theirs - own_part)
    groups = hidden.shape[1] // WALSH
    norm_factor = 1.0 / math.sqrt(2 * WALSH)
    turned = (
        jnp.einsum(
            "rgj,kj->rgk",
            combined.reshape(row_count, groups, WALSH),
            walsh_signs(WALSH),
            precision=lax.Precision.HIGHEST,
        )
        * norm_factor
    )
    rotated = turned.reshape(row_count, -1).astype(jnp.bfloat16)
    partial_value = jnp.dot(rotated, down_weight[0], preferred_element_type=jnp.float32)
    summed = lax.psum_scatter(partial_value, "tensor", scatter_dimension=1, tiled=True).astype(
        jnp.bfloat16
    )
    returned = lax.all_to_all(
        summed.reshape(experts, capacity, -1), "expert", split_axis=0, concat_axis=0, tiled=True
    )
    picked = (
        returned.reshape(experts * capacity, -1)[target]
        .astype(jnp.float32)
        .reshape(tok_rows, top_count, -1)
    )
    route = route_weights.astype(jnp.float32)
    route = route / jnp.sum(route, axis=1, keepdims=True)
    return jnp.sum(picked * route[:, :, None], axis=1).astype(jnp.bfloat16)


def solution(mesh):
    return jax.shard_map(
        shards,
        mesh=mesh,
        in_specs=(
            P(("replica", "expert"), "tensor"),
            P(("replica", "expert"), "tensor"),
            P(("replica", "expert"), None),
            P(("replica", "expert"), None),
            P("expert", None, "tensor"),
            P("expert", None, "tensor"),
            P("expert", "tensor", None),
        ),
        out_specs=P(("replica", "expert"), "tensor"),
        check_vma=False,
    )
```

profile of v0, /device:TPU:8, one launch (start us, length us, event | category | flops | bytes accessed | tf_op | source)
XLA Modules:
  0.0 253.4 jit_solution(2727329423750854163)
XLA Ops:
  6.5 0.0 copy-start
  6.5 0.0 all-gather.2.cloned.1.call-start
  6.5 0.9 copy.19
  7.5 0.1 eq.35
  7.6 0.1 eq.31
  7.6 0.7 broadcast_multiply_fusion
  8.3 1.2 reduce-window.6
  9.5 0.2 slice_reduce_fusion
  9.8 0.1 fusion.25
  9.9 0.1 copy.18
  10.0 0.1 mul.64
  10.1 2.4 scatter_custom_fusion
  12.5 1.0 concatenate.6
  13.5 4.1 %gather_fusion = bf16[640,2048]{1,0:T(8,128)(2,1)} fusion(bf16[65,2048]{1,0:T(8,128)(2,1)S(1)} %concatenate.6, s32[1024]{0:T(1024)S(1)} %pad_clamp_fusion.1), kind=kCustom, calls=%fused_computation | custom fusion | bytes 5245440 | tf_op jit(solution)/shard_map/gather | solution.py:47
  17.6 0.0 copy-start.3
  17.6 66.9 %all_to_all.15 = bf16[16,40,2048]{2,1,0:T(8,128)(2,1)} all-to-all(bf16[16,40,2048]{2,1,0:T(8,128)(2,1)} %bitcast.50), channel_id=1, replica_groups=mesh['replica'=1,'expert'=16,'tensor'=2] {'expert'}, dimensions={0} | all-to-all | bytes 5242880 | tf_op jit(solution)/shard_map/all_to_all | solution.py:50
  84.5 0.0 all-gather.2.cloned.1.call-update
  84.5 0.0 reduce-scatter.2.cloned.1.call-start
  84.5 0.0 copy-done.3
  84.6 0.1 copy.22
  84.7 2.0 gather_fusion.1
  86.7 0.1 copy.23
  86.8 0.1 reshape.200
  86.9 10.4 %all_to_all.16 = bf16[16,2,320]{2,1,0:T(2,128)(2,1)S(1)} all-to-all(bf16[16,2,320]{2,1,0:T(2,128)(2,1)S(1)} %reshape.200), channel_id=1, replica_groups=mesh['replica'=1,'expert'=16,'tensor'=2] {'expert'}, dimensions={0} | all-to-all | bytes 40960 | tf_op jit(solution)/shard_map/all_to_all | solution.py:51
  97.3 0.1 reshape.201
  97.5 2.2 all_gather.7
  99.7 1.1 copy.29
  100.8 6.4 %mul.68 = f32[640,32,128]{2,1,0:T(8,128)} broadcast(f32[640,32]{1,0:T(8,128)S(1)} %bitcast.56), dimensions={0,1} | broadcast | bytes 10567680 | tf_op jit(solution)/shard_map/mul | solution.py:62
  107.1 11.6 %mul.69 = f32[16,40,4096]{2,1,0:T(8,128)} reshape(f32[640,32,128]{2,1,0:T(8,128)} %mul.68) | data formatting | bytes 20971520 | tf_op jit(solution)/shard_map/mul | solution.py:62
  118.8 0.0 all-gather.2.cloned.1.call-done
  118.8 9.8 %multiply_convert_fusion = bf16[16,40,4096]{2,1,0:T(8,128)(2,1)} fusion(f32[16,40,4096]{2,1,0:T(8,128)} %mul.69, bf16[16,40,4096]{2,1,0:T(8,128)(2,1)} %all-gather.2.cloned.1.call-done), kind=kLoop, calls=%fused_computation.4 | loop fusion | flops 7864320 | bytes 20971520 | tf_op jit(solution)/shard_map/convert_element_type | solution.py:68
  128.6 0.0 copy-start.1
  128.6 0.0 copy-start.4
  128.6 6.2 %fusion.5 = f32[640,384]{0,1:T(8,128)S(1)} fusion(bf16[640,4096]{1,0:T(8,128)(2,1)} %bitcast.52, bf16[1,4096,384]{2,1,0:T(8,128)(2,1)} %param.11), kind=kOutput, calls=%fused_computation.11 | convolution fusion | flops 2013265920 | bytes 9371648 | tf_op jit(solution)/shard_map/dot_general | solution.py:70
  134.8 0.0 copy-done.1
  134.9 0.0 copy-done.4
  134.9 3.7 %fusion.10 = bf16[640,384]{0,1:T(8,128)(2,1)} fusion(bf16[640,4096]{1,0:T(8,128)(2,1)S(1)} %bitcast.53, bf16[1,4096,384]{2,1,0:T(8,128)(2,1)S(1)} %copy-done.4, f32[640,384]{0,1:T(8,128)S(1)} %fusion.5), kind=kOutput, calls=%fused_computation.15 | convolution fusion | flops 2014740480 | bytes 9863168 | tf_op jit(solution)/shard_map/dot_general | solution.py:71
  138.5 0.2 collective-permute-start
  138.7 2.0 collective-permute-done
  140.8 1.3 fusion.14
  142.1 1.1 fusion.13
  143.2 0.0 copy-done
  143.2 5.5 %fusion.1 = f32[640,4096]{1,0:T(8,128)} fusion(bf16[640,384]{0,1:T(8,128)(2,1)S(1)} %bitcast.55, bf16[1,384,4096]{2,1,0:T(8,128)(2,1)S(1)} %copy-done), kind=kOutput, calls=%fused_computation.7 | convolution fusion | flops 2013265920 | bytes 14123008 | tf_op jit(solution)/shard_map/dot_general | solution.py:89
  148.7 0.0 reduce-scatter.2.cloned.1.call-update
  148.8 17.0 %reduce-scatter.2.cloned.1.call-done = f32[640,2048]{1,0:T(8,128)} async-done(((f32[640,4096]{1,0:T(8,128)}), f32[640,2048]{1,0:T(8,128)}) %reduce-scatter.2.cloned.1.call-update) | async-done | bytes 5242896 | tf_op jit(solution)/shard_map/reduce_scatter | solution.py:90
  165.8 4.4 %convert_element_type.60 = bf16[640,2048]{1,0:T(8,128)(2,1)} convert(f32[640,2048]{1,0:T(8,128)} %reduce-scatter.2.cloned.1.call-done) | non-fusion elementwise | flops 1310720 | bytes 7864320 | tf_op jit(solution)/shard_map/convert_element_type | solution.py:90
  170.2 0.0 copy-start.2
  170.2 7.1 %all-to-all-start.2 = ((bf16[16,40,2048]{2,1,0:T(8,128)(2,1)}), bf16[16,40,2048]{2,1,0:T(8,128)(2,1)}, u32[]{:S(2)}, u32[]{:S(2)}) async-start(bf16[16,40,2048]{2,1,0:T(8,128)(2,1)} %bitcast.51), calls=%async_computation.3 | async-start | bytes 5242880 | tf_op jit(solution)/shard_map/all_to_all | solution.py:93
  177.3 0.0 copy-done.2
  177.3 0.1 copy.27
  177.4 57.7 %all-to-all-done.2 = bf16[16,40,2048]{2,1,0:T(8,128)(2,1)} async-done(((bf16[16,40,2048]{2,1,0:T(8,128)(2,1)}), bf16[16,40,2048]{2,1,0:T(8,128)(2,1)}, u32[]{:S(2)}, u32[]{:S(2)}) %all-to-all-start.2) | async-done | bytes 2621472 | tf_op jit(solution)/shard_map/all_to_all | solution.py:93
  235.1 7.3 %gather_fusion.2 = bf16[512,2048]{1,0:T(8,128)(2,1)} fusion(bf16[640,2048]{1,0:T(8,128)(2,1)} %bitcast.14, s32[1024]{0:T(1024)S(1)} %pad_clamp_fusion), kind=kCustom, calls=%fused_computation.2 | custom fusion | bytes 4196352 | tf_op jit(solution)/shard_map/gather | solution.py:97
  242.4 4.1 %fusion = bf16[64,2048]{1,0:T(8,128)(2,1)} fusion(bf16[512,2048]{1,0:T(8,128)(2,1)} %gather_fusion.2, f32[64,8]{1,0:T(8,128)S(1)} %copy.27), kind=kLoop, calls=%fused_computation.6 | loop fusion | flops 3014656 | bytes 2361344 | tf_op jit(solution)/shard_map/reduce_sum | solution.py:103
  (17 shorter events, 0.1 us)
Async XLA Ops:
  6.5 136.7 %copy-start = (bf16[1,384,4096]{2,1,0:T(8,128)(2,1)S(1)}, bf16[1,384,4096]{2,1,0:T(8,128)(2,1)}, u32[]{:S(2)}) copy-start(bf16[1,384,4096]{2,1,0:T(8,128)(2,1)} %param.13) | copy-start | bytes 9437188
  6.5 112.2 %all-gather.2.cloned.1.call-start = ((), (), s32[]{:S(2)}) async-start(), calls=%async_computation.4 | async-start | bytes 7864320 | tf_op jit(solution)/shard_map/all_gather | solution.py:54
  17.6 66.9 %copy-start.3 = (bf16[64,16]{0,1:T(8,128)(2,1)S(1)}, bf16[64,16]{0,1:T(8,128)(2,1)}, u32[]{:S(2)}) copy-start(bf16[64,16]{0,1:T(8,128)(2,1)} %param.8) | copy-start | bytes 6148
  84.5 81.3 %reduce-scatter.2.cloned.1.call-start = ((), (), s32[]{:S(2)}) async-start(), calls=%async_computation.5 | async-start | bytes 15728640 | tf_op jit(solution)/shard_map/reduce_scatter | solution.py:90
  128.6 6.2 %copy-start.1 = (bf16[16,40,4096]{2,1,0:T(8,128)(2,1)S(1)}, bf16[16,40,4096]{2,1,0:T(8,128)(2,1)}, u32[]{:S(2)}) copy-start(bf16[16,40,4096]{2,1,0:T(8,128)(2,1)} %multiply_convert_fusion) | copy-start | bytes 15728644
  128.6 6.3 %copy-start.4 = (bf16[1,4096,384]{2,1,0:T(8,128)(2,1)S(1)}, bf16[1,4096,384]{2,1,0:T(8,128)(2,1)}, u32[]{:S(2)}) copy-start(bf16[1,4096,384]{2,1,0:T(8,128)(2,1)} %param.12) | copy-start | bytes 9437188
  138.5 2.2 collective-permute-start
  170.2 7.1 %copy-start.2 = (s32[64,8]{0,1:T(8,128)S(1)}, s32[64,8]{0,1:T(8,128)}, u32[]{:S(2)}) copy-start(s32[64,8]{0,1:T(8,128)} %param.10) | copy-start | bytes 6148
  170.2 65.0 %all-to-all-start.2 = ((bf16[16,40,2048]{2,1,0:T(8,128)(2,1)}), bf16[16,40,2048]{2,1,0:T(8,128)(2,1)}, u32[]{:S(2)}, u32[]{:S(2)}) async-start(bf16[16,40,2048]{2,1,0:T(8,128)(2,1)} %bitcast.51), calls=%async_computation.3 | async-start | bytes 5242880 | tf_op jit(solution)/shard_map/all_to_all | solution.py:93
Sparse Core Ops, SparseCore 0:
  84.6 13.9 all-gather.1
  148.9 16.8 reduce-scatter.1
where the time goes:
time: 256 us; the launch traced here: 253 us
  blocking collectives  79.5 us (31%)
  waiting for transfers between devices  76.8 us (30%)
  local copies, waits for them, and re-layouts  38 us (15%)
  other arithmetic  21.8 us (9%)
  matrix products  16.5 us (6%)
  between operations  13.6 us (5%)
  starting transfers between devices  7.3 us (3%)
    all_to_all x1, blocking collectives, shards(): lax.all_to_all(send_values, 'expert', split_axis=0, concat_axis=0, tiled=...  66.9 us
    all_to_all x1, waiting for transfers between devices, shards(): lax.all_to_all(summed.reshape(experts, capacity, -1), 'expert', split_axi...  57.7 us
    mul x3, local copies, waits for them, and re-layouts, shards(): joined_values.astype(jnp.float32)  19.1 us
    reduce_scatter x1, waiting for transfers between devices, shards(): lax.psum_scatter(partial_value, 'tensor', scatter_dimension=1, tiled=True)  17 us
    all_to_all x1, blocking collectives, shards(): lax.all_to_all(send_scales, 'expert', split_axis=0, concat_axis=0, tiled=...  10.4 us
    convert_element_type x1, other arithmetic, shards(): dequant = (joined_values.astype(jnp.float32).reshape(row_count, scale_cou...  9.83 us
    gather x1, local copies, waits for them, and re-layouts, shards(): returned.reshape(experts * capacity, -1)[target].astype(jnp.float32)  7.29 us
    all_to_all x1, starting transfers between devices, shards(): lax.all_to_all(summed.reshape(experts, capacity, -1), 'expert', split_axi...  7.1 us
  transfers between devices with their start and end apart: 4, of which 3 were waited for; matrix products, arithmetic and copies ran while one was open for 9% of the time, Pallas kernels for 0%

commit v1 on v0

--- a/solution.py
+++ b/solution.py
@@ -1,15 +1,15 @@
+import functools
 import math
 
 import jax
 import jax.numpy as jnp
 from jax import lax
+from jax.experimental import pallas as pl
+from jax.experimental.pallas import tpu as pltpu
 from jax.sharding import PartitionSpec as P
 
 WALSH = 128
-
-
-def partner_2(array, axis, bit):
-    return lax.ppermute(array, axis, [(i, i ^ 1 << bit) for i in range(lax.axis_size(axis))])
+LANES = 128
 
 
 def walsh_signs(length):
@@ -26,7 +26,232 @@
     return (1 - 2 * (parity % 2)).astype(jnp.float32)
 
 
-def shards(
+def swap(array, masks, core=0):
+    experts = lax.axis_size("expert")
+    pairs = [
+        (e * 2 + t, (e ^ masks[t]) * 2 + (t ^ core)) for e in range(experts) for t in range(2)
+    ]
+    return lax.ppermute(array, ("expert", "tensor"), pairs)
+
+
+def cost(flops, *arrays):
+    size = sum(math.prod(a.shape) * a.dtype.itemsize for a in arrays)
+    return pl.CostEstimate(flops=flops, bytes_accessed=size, transcendentals=0)
+
+
+def scaled_tokens(values, scales, ids, route_weights, experts):
+    rows, features = values.shape
+    top = ids.shape[1]
+    width = features // scales.shape[1]
+
+    def kernel(values_ref, scales_ref, ids_ref, weights_ref, out_ref):
+        factor = scales_ref[...].astype(jnp.float32)
+        for block in range(scales.shape[1]):
+            cols = slice(block * width, (block + 1) * width)
+            out_ref[:, cols] = (
+                values_ref[:, cols].astype(jnp.float32) * factor[:, block : block + 1]
+            ).astype(jnp.bfloat16)
+        weights = weights_ref[...].astype(jnp.float32)
+        route = weights / jnp.sum(weights, axis=1, keepdims=True)
+        lane = lax.broadcasted_iota(jnp.int32, (rows, LANES), 1)
+        expert = lax.rem(lane, experts)
+        table = jnp.zeros((rows, LANES), jnp.float32)
+        for k in range(top):
+            table = table + jnp.where(ids_ref[:, k : k + 1] == expert, route[:, k : k + 1], 0.0)
+        high = table.astype(jnp.bfloat16).astype(jnp.float32)
+        tail = jnp.where(lane < experts, high, jnp.where(lane < 2 * experts, table - high, 0.0))
+        out_ref[:, features:] = tail.astype(jnp.bfloat16)
+
+    return pl.pallas_call(
+        kernel,
+        out_shape=jax.ShapeDtypeStruct((rows, features + LANES), jnp.bfloat16),
+        name="scaled_tokens",
+    )(values, scales, ids, route_weights)
+
+
+def hidden_units(core, near, near_pair, far, far_pair, gate, up):
+    rows_near, wide = near.shape
+    rows_far = far.shape[0]
+    rows = rows_near + rows_far
+    block = rows_near // 2
+    features, units = gate.shape
+    half = features // 2
+    step = LANES
+
+    def kernel(core_ref, near_ref, near_pair_ref, far_ref, far_pair_ref, gate_ref, up_ref, out_ref):
+        own = pl.multiple_of(core_ref[0] * half, half)
+        other = pl.multiple_of((1 - core_ref[0]) * half, half)
+        x_own = jnp.concatenate([near_ref[:, :half], far_ref[:, :half]], axis=0)
+        x_other = jnp.concatenate(
+            [
+                near_pair_ref[:block, :half],
+                far_pair_ref[:block, :half],
+                near_pair_ref[block:, :half],
+                far_pair_ref[block:, :half],
+            ],
+            axis=0,
+        )
+        w_own = jnp.concatenate([gate_ref[pl.ds(own, half), :], up_ref[pl.ds(own, half), :]], axis=1)
+        w_other = jnp.concatenate(
+            [gate_ref[pl.ds(other, half), :], up_ref[pl.ds(other, half), :]], axis=1
+        )
+        both = jnp.dot(x_own, w_own, preferred_element_type=jnp.float32) + jnp.dot(
+            x_other, w_other, preferred_element_type=jnp.float32
+        )
+        gate_out, up_out = both[:, :step], both[:, step:]
+        out_ref[...] = (gate_out / (1.0 + jnp.exp(-gate_out)) * up_out).astype(jnp.bfloat16)
+
+    whole = lambda n: pl.BlockSpec((n, wide), lambda j, core: (0, 0))
+    return pl.pallas_call(
+        kernel,
+        grid_spec=pltpu.PrefetchScalarGridSpec(
+            num_scalar_prefetch=1,
+            grid=(units // step,),
+            in_specs=[
+                whole(rows_near),
+                whole(rows_near),
+                whole(rows_far),
+                whole(rows_far),
+                pl.BlockSpec((features, step), lambda j, core: (0, j)),
+                pl.BlockSpec((features, step), lambda j, core: (0, j)),
+            ],
+            out_specs=pl.BlockSpec((rows, step), lambda j, core: (0, j)),
+        ),
+        out_shape=jax.ShapeDtypeStruct((rows, units), jnp.bfloat16),
+        compiler_params=pltpu.CompilerParams(vmem_limit_bytes=32 << 20),
+        cost_estimate=cost(4 * rows * features * units, near, near, far, far, gate, up),
+        name="hidden_units",
+    )(core, near, near_pair, far, far_pair, gate, up)
+
+
+def routed_outputs(core, mine, theirs, mix, down, down_pair, near, far, lanes):
+    rows, units = mine.shape
+    features = down_pair.shape[1]
+    groups = units // WALSH
+    split = near.shape[0]
+    block = split // 2
+    step = min(512, features)
+    steps = features // step
+
+    def kernel(core_ref, mine_ref, theirs_ref, mix_ref, down_ref, pair_ref, near_ref, far_ref,
+               lanes_ref, near_out, far_out, turned, route):
+        @pl.when(pl.program_id(0) == 0)
+        def _():
+            for g in range(groups):
+                cols = slice(g * WALSH, (g + 1) * WALSH)
+                other = theirs_ref[:, cols]
+                other = jnp.concatenate(
+                    [other[:block], other[split : split + block], other[block:split],
+                     other[split + block :]],
+                    axis=0,
+                )
+                both = jnp.dot(
+                    jnp.concatenate([mine_ref[:, cols], other], axis=1),
+                    mix_ref[...],
+                    preferred_element_type=jnp.float32,
+                ).astype(jnp.bfloat16)
+                turned[:, cols] = both[:, :WALSH]
+                turned[:, units + g * WALSH : units + (g + 1) * WALSH] = both[:, WALSH:]
+            tails = jnp.concatenate([near_ref[...], far_ref[...]], axis=0).astype(jnp.float32)
+            weight = jnp.sum(tails * lanes_ref[...], axis=1, keepdims=True)
+            route[...] = jnp.broadcast_to(weight, route.shape)
+
+        out = jnp.dot(
+            turned[...],
+            jnp.concatenate([down_ref[...], pair_ref[...]], axis=0),
+            preferred_element_type=jnp.float32,
+        )
+        scaled = (out * route[:, :1]).astype(jnp.bfloat16)
+        near_out[...] = scaled[:split]
+        far_out[...] = scaled[split:]
+
+    tail = features // LANES
+    return pl.pallas_call(
+        kernel,
+        grid_spec=pltpu.PrefetchScalarGridSpec(
+            num_scalar_prefetch=1,
+            grid=(steps,),
+            in_specs=[
+                pl.BlockSpec((rows, units), lambda j, core: (0, 0)),
+                pl.BlockSpec((rows, units), lambda j, core: (0, 0)),
+                pl.BlockSpec(mix.shape, lambda j, core: (0, 0)),
+                pl.BlockSpec((units, step), lambda j, core: (0, core[0] * steps + j)),
+                pl.BlockSpec((units, step), lambda j, core: (0, j)),
+                pl.BlockSpec((split, LANES), lambda j, core: (0, tail)),
+                pl.BlockSpec((rows - split, LANES), lambda j, core: (0, tail)),
+                pl.BlockSpec((1, LANES), lambda j, core: (0, 0)),
+            ],
+            out_specs=[
+                pl.BlockSpec((split, step), lambda j, core: (0, j)),
+                pl.BlockSpec((rows - split, step), lambda j, core: (0, j)),
+            ],
+            scratch_shapes=[
+                pltpu.VMEM((rows, 2 * units), jnp.bfloat16),
+                pltpu.VMEM((rows, LANES), jnp.float32),
+            ],
+        ),
+        out_shape=[
+            jax.ShapeDtypeStruct((split, features), jnp.bfloat16),
+            jax.ShapeDtypeStruct((rows - split, features), jnp.bfloat16),
+        ],
+        compiler_params=pltpu.CompilerParams(vmem_limit_bytes=32 << 20),
+        cost_estimate=cost(4 * rows * units * features, mine, theirs, down_pair, down_pair, near, far),
+        name="routed_outputs",
+    )(core, mine, theirs, mix, down, down_pair, near, far, lanes)
+
+
+def every_expert(
+    token_values, token_scales, expert_ids, route_weights, gate_weight, up_weight, down_weight
+):
+    experts = lax.axis_size("expert")
+    core_index = lax.axis_index("tensor")
+    core = core_index.astype(jnp.int32).reshape(1)
+    expert = lax.axis_index("expert")
+    rows, features = token_values.shape
+    gate, up, down = gate_weight[0], up_weight[0], down_weight[0]
+    first, second = (1, 2), (2, 1)
+
+    block = scaled_tokens(token_values, token_scales, expert_ids, route_weights, experts)
+    blocks = [block] + [swap(block, (m, m)) for m in range(4, experts, 4)]
+
+    other_columns = lax.dynamic_slice(
+        down, (0, (1 - core_index) * features), (down.shape[0], features)
+    )
+    down_pair = swap(other_columns, (0, 0), 1)
+
+    signs = walsh_signs(WALSH) / math.sqrt(2 * WALSH)
+    sign = jnp.where(core_index == 0, 1.0, -1.0)
+    mix = jnp.concatenate(
+        [
+            jnp.concatenate([signs * sign, signs], axis=1),
+            jnp.concatenate([signs, -signs * sign], axis=1),
+        ],
+        axis=0,
+    ).astype(jnp.bfloat16)
+    lane = jnp.arange(LANES, dtype=jnp.int32)[None, :]
+    lanes = ((lane % experts == expert) & (lane < 2 * experts)).astype(jnp.float32)
+
+    total = None
+    for index, block in enumerate(blocks):
+        near = jnp.concatenate([block, swap(block, first)], axis=0)
+        far = swap(near, second)
+        near_pair = swap(near, (0, 0), 1)
+        far_pair = swap(far, (0, 0), 1)
+        mine = hidden_units(core, near, near_pair, far, far_pair, gate, up)
+        theirs = swap(mine, (0, 0), 1)
+        near_out, far_out = routed_outputs(
+            core, mine, theirs, mix, down, down_pair, near, far, lanes
+        )
+        summed = near_out.astype(jnp.float32) + swap(far_out, second).astype(jnp.float32)
+        back = swap(summed[rows:].astype(jnp.bfloat16), first).astype(jnp.float32)
+        part = summed[:rows] + back
+        if index > 0:
+            part = swap(part.astype(jnp.bfloat16), (4 * index, 4 * index)).astype(jnp.float32)
+        total = part if total is None else total + part
+    return total.astype(jnp.bfloat16)
+
+
+def chosen_experts(
     token_values, token_scales, expert_ids, route_weights, gate_weight, up_weight, down_weight
 ):
     tok_rows, top_count = expert_ids.shape
@@ -70,7 +295,7 @@
     gate_out = jnp.dot(dequant, gate_weight[0], preferred_element_type=jnp.float32)
     up_out = jnp.dot(dequant, up_weight[0], preferred_element_type=jnp.float32)
     hidden = (jax.nn.silu(gate_out) * up_out).astype(jnp.bfloat16)
-    partner = partner_2(hidden, "tensor", 0)
+    partner = swap(hidden, (0, 0), 1)
     own_part = hidden.astype(jnp.float32)
     theirs = partner.astype(jnp.float32)
     combined = jnp.where(lax.axis_index("tensor") == 0, own_part + theirs, theirs - own_part)
@@ -101,6 +326,13 @@
     route = route_weights.astype(jnp.float32)
     route = route / jnp.sum(route, axis=1, keepdims=True)
     return jnp.sum(picked * route[:, :, None], axis=1).astype(jnp.bfloat16)
+
+
+def shards(*arrays):
+    experts = lax.axis_size("expert")
+    top = arrays[2].shape[1]
+    dense = 2 * top >= experts and experts % 4 == 0 and experts & (experts - 1) == 0
+    return (every_expert if dense else chosen_experts)(*arrays)
 
 
 def solution(mesh):

time: 256 us -> 153 us (0.60)
  blocking collectives: 79.5 us -> 0 us
  Pallas kernels: 0 us -> 32.5 us
  local copies, waits for them, and re-layouts: 38 us -> 16.3 us
  starting transfers between devices: 7.3 us -> 27.5 us
  other arithmetic: 21.8 us -> 3.28 us
  matrix products: 16.5 us -> 0 us
  between operations: 13.6 us -> 0.41 us
  waiting for transfers between devices: 76.8 us -> 72.1 us
    all_to_all x2 -> x0, blocking collectives: 77.3 us -> none  [the longest x1 66.9 us: shards(): lax.all_to_all(send_values, 'expert', split_axis=0, concat_axis=0, tiled=...]
    ppermute x1 -> x35, waiting for transfers between devices: 2.03 us -> 72.1 us  [swap(): return lax.ppermute(array, ('expert', 'tensor'), pairs)]
    all_to_all x1 -> x0, waiting for transfers between devices: 57.7 us -> none  [shards(): lax.all_to_all(summed.reshape(experts, capacity, -1), 'expert', split_axi...]
    pallas_call x0 -> x9, Pallas kernels: none -> 32.5 us  [the longest x4 15.6 us: hidden_units(): pl.pallas_call(kernel, grid_spec=pltpu.PrefetchScalarGridSpec(num_scalar_...]
    ppermute x1 -> x35, starting transfers between devices: 0.16 us -> 27.5 us  [swap(): return lax.ppermute(array, ('expert', 'tensor'), pairs)]
    mul x5 -> x0, local copies, waits for them, and re-layouts: 19.3 us -> none  [the longest x3 19.1 us: shards(): joined_values.astype(jnp.float32)]
    reduce_scatter x1 -> x0, waiting for transfers between devices: 17 us -> none  [shards(): lax.psum_scatter(partial_value, 'tensor', scatter_dimension=1, tiled=True)]
    dot_general x4 -> x0, matrix products: 16.5 us -> none  [the longest x1 6.24 us: shards(): jnp.dot(dequant, gate_weight[0], preferred_element_type=jnp.float32)]
  transfers between devices with their start and end apart: 4 -> 35, of which waited for: 3 -> 14; matrix products, arithmetic and copies ran while one was open for 9% -> 4% of each run, Pallas kernels for 0% -> 20%
where the time goes in v1:
time: 153 us; the launch traced here: 152 us
  waiting for transfers between devices  72.1 us (47%)
  Pallas kernels  32.5 us (21%)
  starting transfers between devices  27.5 us (18%)
  local copies, waits for them, and re-layouts  16.3 us (11%)
  other arithmetic  3.28 us (2%)
    ppermute x35, waiting for transfers between devices, swap(): return lax.ppermute(array, ('expert', 'tensor'), pairs)  72.1 us
    ppermute x35, starting transfers between devices, swap(): return lax.ppermute(array, ('expert', 'tensor'), pairs)  27.5 us
    pallas_call x4, Pallas kernels, hidden_units(): pl.pallas_call(kernel, grid_spec=pltpu.PrefetchScalarGridSpec(num_scalar_...  15.6 us
    pallas_call x4, Pallas kernels, routed_outputs(): pl.pallas_call(kernel, grid_spec=pltpu.PrefetchScalarGridSpec(num_scalar_...  14.8 us
    unnamed x44, local copies, waits for them, and re-layouts  12.6 us
  transfers between devices with their start and end apart: 35, of which 14 were waited for; matrix products, arithmetic and copies ran while one was open for 4% of the time, Pallas kernels for 20%

profile of v1, /device:TPU:8, one launch (start us, length us, event | category | flops | bytes accessed | tf_op | source)
XLA Modules:
  0.0 152.1 jit_solution(16912511378238484767)
XLA Ops:
  0.0 1.4 copy.10.weights_ref
  1.4 1.4 copy.9.ids_ref
  2.8 1.4 copy.8.scales_ref
  4.1 2.1 %scaled_tokens.1 = bf16[64,2176]{1,0:T(8,128)(2,1)} custom-call(bf16[64,2048]{1,0:T(8,128)(2,1)} %values_ref.1, bf16[64,16]{1,0:T(8,128)(2,1)} %copy.8.scales_ref, s32[64,8]{1,0:T(8,128)} %copy.9.ids_ref, s32[64,8]{1,0:T(8,128)} %copy.10.weights_ref), custom_call_target="tpu_custom_call" | custom-call | tf_op jit(solution)/shard_map/scaled_tokens/pallas_call | solution.py:65
  6.2 1.5 collective-permute-start
  7.7 0.4 collective-permute-start.8
  8.1 2.6 %collective-permute-start.17 = (bf16[64,2176]{1,0:T(8,128)(2,1)}, bf16[64,2176]{1,0:T(8,128)(2,1)S(1)}, u32[]{:S(2)}, u32[]{:S(2)}) collective-permute-start(bf16[64,2176]{1,0:T(8,128)(2,1)} %scaled_tokens.1), channel_id=1, source_target_pairs={{0,16},{1,17},{2,18},{3,19},{4,20},{5,21},{6,22},{7,23},{8,24},{9,... | collective-permute-start | bytes 835592 | tf_op jit(solution)/shard_map/ppermute | solution.py:34
  10.7 0.5 collective-permute-start.26
  11.2 2.8 %dynamic-slice_bitcast_fusion = bf16[384,2048]{1,0:T(8,128)(2,1)} fusion(bf16[1,384,4096]{2,1,0:T(8,128)(2,1)} %param.13, s32[]{:T(128)S(6)} %select_n.36), kind=kLoop, calls=%fused_computation | loop fusion | bytes 3145732 | tf_op jit(solution)/shard_map/dynamic_slice | solution.py:217
  14.0 1.6 %collective-permute-start.2 = (bf16[128,2176]{1,0:T(8,128)(2,1)S(1)}, bf16[128,2176]{1,0:T(8,128)(2,1)S(1)}, u32[]{:S(2)}, u32[]{:S(2)}) collective-permute-start(bf16[128,2176]{1,0:T(8,128)(2,1)S(1)} %pad_maximum_fusion.near_ref), channel_id=1, source_target_pairs={{0,4},{1,3},{2,6},{3,1},{4,0},{5,7},{6,2},{7,5},{8,12},{9,11},{10,... | collective-permute-start | bytes 1671176 | tf_op jit(solution)/shard_map/ppermute | solution.py:34
  15.6 3.6 %collective-permute-done.8 = bf16[64,2176]{1,0:T(8,128)(2,1)S(1)} collective-permute-done((bf16[64,2176]{1,0:T(8,128)(2,1)}, bf16[64,2176]{1,0:T(8,128)(2,1)S(1)}, u32[]{:S(2)}, u32[]{:S(2)}) %collective-permute-start.8) | collective-permute-done | bytes 278560 | tf_op jit(solution)/shard_map/ppermute | solution.py:34
  19.2 10.9 %collective-permute-done.17 = bf16[64,2176]{1,0:T(8,128)(2,1)S(1)} collective-permute-done((bf16[64,2176]{1,0:T(8,128)(2,1)}, bf16[64,2176]{1,0:T(8,128)(2,1)S(1)}, u32[]{:S(2)}, u32[]{:S(2)}) %collective-permute-start.17) | collective-permute-done | bytes 278560 | tf_op jit(solution)/shard_map/ppermute | solution.py:34
  30.1 0.5 collective-permute-start.9
  30.6 0.7 constant_dynamic-update-slice_fusion.3
  31.3 3.9 %collective-permute-done.26 = bf16[64,2176]{1,0:T(8,128)(2,1)S(1)} collective-permute-done((bf16[64,2176]{1,0:T(8,128)(2,1)}, bf16[64,2176]{1,0:T(8,128)(2,1)S(1)}, u32[]{:S(2)}, u32[]{:S(2)}) %collective-permute-start.26) | collective-permute-done | bytes 278560 | tf_op jit(solution)/shard_map/ppermute | solution.py:34
  35.2 1.5 collective-permute-start.18
  36.7 0.6 collective-permute-start.27
  37.4 4.4 %collective-permute-done.18 = bf16[64,2176]{1,0:T(8,128)(2,1)S(1)} collective-permute-done((bf16[64,2176]{1,0:T(8,128)(2,1)S(1)}, bf16[64,2176]{1,0:T(8,128)(2,1)S(1)}, u32[]{:S(2)}, u32[]{:S(2)}) %collective-permute-start.18) | collective-permute-done | bytes 278560 | tf_op jit(solution)/shard_map/ppermute | solution.py:34
  41.8 0.5 collective-permute-start.11
  42.3 0.7 constant_dynamic-update-slice_fusion.2.near_ref
  43.0 3.7 %collective-permute-done.27 = bf16[64,2176]{1,0:T(8,128)(2,1)S(1)} collective-permute-done((bf16[64,2176]{1,0:T(8,128)(2,1)S(1)}, bf16[64,2176]{1,0:T(8,128)(2,1)S(1)}, u32[]{:S(2)}, u32[]{:S(2)}) %collective-permute-start.27) | collective-permute-done | bytes 278560 | tf_op jit(solution)/shard_map/ppermute | solution.py:34
  46.7 0.5 collective-permute-start.3
  47.3 0.8 collective-permute-start.20
  48.1 3.3 %collective-permute-done.11.far_ref = bf16[128,2176]{1,0:T(8,128)(2,1)} collective-permute-done((bf16[128,2176]{1,0:T(8,128)(2,1)S(1)}, bf16[128,2176]{1,0:T(8,128)(2,1)}, u32[]{:S(2)}, u32[]{:S(2)}) %collective-permute-start.11) | collective-permute-done | bytes 557088 | tf_op jit(solution)/shard_map/ppermute | solution.py:34
  51.4 0.5 collective-permute-start.29
  51.9 0.3 collective-permute-start.12
  52.2 1.9 %copy-done.3 = bf16[1,4096,384]{2,1,0:T(8,128)(2,1)S(1)} copy-done((bf16[1,4096,384]{2,1,0:T(8,128)(2,1)S(1)}, bf16[1,4096,384]{2,1,0:T(8,128)(2,1)}, u32[]{:S(2)}) %copy-start.3) | copy-done | bytes 3145752
  54.1 3.3 %hidden_units.4.mine_ref = bf16[256,384]{1,0:T(8,128)(2,1)S(1)} custom-call(s32[1]{0:T(128)} %bitcast.core_ref, bf16[128,2176]{1,0:T(8,128)(2,1)S(1)} %pad_maximum_fusion.near_ref, bf16[128,2176]{1,0:T(8,128)(2,1)S(1)} %collective-permute-done.1.near_pair_ref, bf16[128,2176]{1,0:T(8,128)(2,1)S(1)} %collective-permute-done.2.far_ref, ...), custom_call_target="tpu_custom_call" | custom-call | flops 1610612736 | bytes 8519680 | tf_op jit(solution)/shard_map/hidden_units/pallas_call | solution.py:105
  57.5 0.8 copy-done.16
  58.3 0.3 collective-permute-start.19
  58.6 0.2 collective-permute-start.21
  58.8 4.4 %collective-permute-done.29.far_ref = bf16[128,2176]{1,0:T(8,128)(2,1)S(1)} collective-permute-done((bf16[128,2176]{1,0:T(8,128)(2,1)S(1)}, bf16[128,2176]{1,0:T(8,128)(2,1)S(1)}, u32[]{:S(2)}, u32[]{:S(2)}) %collective-permute-start.29) | collective-permute-done | bytes 557088 | tf_op jit(solution)/shard_map/ppermute | solution.py:34
  63.2 0.8 copy-done.12
  64.0 0.8 multiply_convert_fusion.1
  64.9 0.5 collective-permute-start.28
  65.6 0.9 maximum_maximum_fusion.mix_ref
  66.5 1.0 copy-done.6
  67.5 1.1 copy-done.15
  68.6 3.9 %routed_outputs.4 = (bf16[128,2048]{1,0:T(8,128)(2,1)S(1)}, bf16[128,2048]{1,0:T(8,128)(2,1)S(1)}) custom-call(s32[1]{0:T(128)} %bitcast.core_ref, bf16[256,384]{1,0:T(8,128)(2,1)S(1)} %hidden_units.4.mine_ref, bf16[256,384]{1,0:T(8,128)(2,1)S(1)} %collective-permute-done.4.theirs_ref, bf16[256,256]{1,0:T(8,128)(2,1)S(1)} %maximum_maximum_fusion.mix_ref, ...), custom_call_target="tpu_custom_call" | custom-call | flops 805306368 | bytes 4653056 | tf_op jit(solution)/shard_map/routed_outputs/pallas_call | solution.py:169
  72.5 0.6 collective-permute-start.6
  73.1 1.1 copy-done.10
  74.2 1.1 copy-done.17
  75.3 4.3 %hidden_units.5.mine_ref = bf16[256,384]{1,0:T(8,128)(2,1)S(1)} custom-call(s32[1]{0:T(128)} %bitcast.core_ref, bf16[128,2176]{1,0:T(8,128)(2,1)S(1)} %copy-done.10, bf16[128,2176]{1,0:T(8,128)(2,1)S(1)} %copy-done.17, bf16[128,2176]{1,0:T(8,128)(2,1)} %collective-permute-done.11.far_ref, bf16[128,2176]{1,0:T(8,128)(2,1)} %collective-permute-done.12.far_pair_ref, ...), custom_call_target="tpu_custom_call" | custom-call | flops 1610612736 | bytes 8519680 | tf_op jit(solution)/shard_map/hidden_units/pallas_call | solution.py:105
  79.6 1.1 collective-permute-start.13
  80.7 4.6 %hidden_units.6.mine_ref = bf16[256,384]{1,0:T(8,128)(2,1)S(1)} custom-call(s32[1]{0:T(128)} %bitcast.core_ref, bf16[128,2176]{1,0:T(8,128)(2,1)} %constant_dynamic-update-slice_fusion.2.near_ref, bf16[128,2176]{1,0:T(8,128)(2,1)} %collective-permute-done.19.near_pair_ref, bf16[128,2176]{1,0:T(8,128)(2,1)} %collective-permute-done.20.far_ref, ...), custom_call_target="tpu_custom_call" | custom-call | flops 1610612736 | bytes 8519680 | tf_op jit(solution)/shard_map/hidden_units/pallas_call | solution.py:105
  85.4 3.4 %hidden_units.7.mine_ref = bf16[256,384]{1,0:T(8,128)(2,1)S(1)} custom-call(s32[1]{0:T(128)} %bitcast.core_ref, bf16[128,2176]{1,0:T(8,128)(2,1)S(1)} %copy-done.8, bf16[128,2176]{1,0:T(8,128)(2,1)S(1)} %collective-permute-done.28.near_pair_ref, bf16[128,2176]{1,0:T(8,128)(2,1)S(1)} %copy-done.13, ...), custom_call_target="tpu_custom_call" | custom-call | flops 1610612736 | bytes 8519680 | tf_op jit(solution)/shard_map/hidden_units/pallas_call | solution.py:105
  88.8 0.5 collective-permute-start.31
  89.3 3.6 %routed_outputs.5 = (bf16[128,2048]{1,0:T(8,128)(2,1)S(1)}, bf16[128,2048]{1,0:T(8,128)(2,1)S(1)}) custom-call(s32[1]{0:T(128)} %bitcast.core_ref, bf16[256,384]{1,0:T(8,128)(2,1)S(1)} %hidden_units.5.mine_ref, bf16[256,384]{1,0:T(8,128)(2,1)S(1)} %collective-permute-done.13.theirs_ref, bf16[256,256]{1,0:T(8,128)(2,1)S(1)} %maximum_maximum_fusion.mix_ref, ...), custom_call_target="tpu_custom_call" | custom-call | flops 805306368 | bytes 4653056 | tf_op jit(solution)/shard_map/routed_outputs/pallas_call | solution.py:169
  93.0 0.6 collective-permute-start.14
  93.6 3.6 %routed_outputs.6 = (bf16[128,2048]{1,0:T(8,128)(2,1)S(1)}, bf16[128,2048]{1,0:T(8,128)(2,1)S(1)}) custom-call(s32[1]{0:T(128)} %bitcast.core_ref, bf16[256,384]{1,0:T(8,128)(2,1)S(1)} %hidden_units.6.mine_ref, bf16[256,384]{1,0:T(8,128)(2,1)S(1)} %collective-permute-done.22.theirs_ref, bf16[256,256]{1,0:T(8,128)(2,1)S(1)} %maximum_maximum_fusion.mix_ref, ...), custom_call_target="tpu_custom_call" | custom-call | flops 805306368 | bytes 4653056 | tf_op jit(solution)/shard_map/routed_outputs/pallas_call | solution.py:169
  97.2 1.6 %collective-permute-start.23 = (bf16[128,2048]{1,0:T(8,128)(2,1)S(1)}, bf16[128,2048]{1,0:T(8,128)(2,1)S(1)}, u32[]{:S(2)}, u32[]{:S(2)}) collective-permute-start(bf16[128,2048]{1,0:T(8,128)(2,1)S(1)} %get-tuple-element.18), channel_id=1, source_target_pairs={{0,4},{1,3},{2,6},{3,1},{4,0},{5,7},{6,2},{7,5},{8,12},{9,11},{10,... | collective-permute-start | bytes 1572872 | tf_op jit(solution)/shard_map/ppermute | solution.py:34
  98.8 3.6 %routed_outputs.7 = (bf16[128,2048]{1,0:T(8,128)(2,1)S(1)}, bf16[128,2048]{1,0:T(8,128)(2,1)S(1)}) custom-call(s32[1]{0:T(128)} %bitcast.core_ref, bf16[256,384]{1,0:T(8,128)(2,1)S(1)} %hidden_units.7.mine_ref, bf16[256,384]{1,0:T(8,128)(2,1)S(1)} %collective-permute-done.31.theirs_ref, bf16[256,256]{1,0:T(8,128)(2,1)S(1)} %maximum_maximum_fusion.mix_ref, ...), custom_call_target="tpu_custom_call" | custom-call | flops 805306368 | bytes 4653056 | tf_op jit(solution)/shard_map/routed_outputs/pallas_call | solution.py:169
  102.4 0.6 collective-permute-start.32
  103.2 1.6 %collective-permute-start.7 = (bf16[64,2048]{1,0:T(8,128)(2,1)S(1)}, bf16[64,2048]{1,0:T(8,128)(2,1)S(1)}, u32[]{:S(2)}, u32[]{:S(2)}) collective-permute-start(bf16[64,2048]{1,0:T(8,128)(2,1)S(1)} %slice.69), channel_id=1, source_target_pairs={{0,2},{1,5},{2,0},{3,7},{4,6},{5,1},{6,4},{7,3},{8,10},{9,13},{10,... | collective-permute-start | bytes 786440 | tf_op jit(solution)/shard_map/ppermute | solution.py:34
  104.9 0.6 collective-permute-start.15
  105.5 4.7 %collective-permute-done.23 = bf16[128,2048]{1,0:T(8,128)(2,1)S(1)} collective-permute-done((bf16[128,2048]{1,0:T(8,128)(2,1)S(1)}, bf16[128,2048]{1,0:T(8,128)(2,1)S(1)}, u32[]{:S(2)}, u32[]{:S(2)}) %collective-permute-start.23) | collective-permute-done | bytes 524320 | tf_op jit(solution)/shard_map/ppermute | solution.py:34
  110.5 11.0 %collective-permute-done.32 = bf16[128,2048]{1,0:T(8,128)(2,1)S(1)} collective-permute-done((bf16[128,2048]{1,0:T(8,128)(2,1)S(1)}, bf16[128,2048]{1,0:T(8,128)(2,1)S(1)}, u32[]{:S(2)}, u32[]{:S(2)}) %collective-permute-start.32) | collective-permute-done | bytes 524320 | tf_op jit(solution)/shard_map/ppermute | solution.py:34
  121.8 5.5 %collective-permute-start.16 = (bf16[64,2048]{1,0:T(8,128)(2,1)S(1)}, bf16[64,2048]{1,0:T(8,128)(2,1)S(1)}, u32[]{:S(2)}, u32[]{:S(2)}) collective-permute-start(bf16[64,2048]{1,0:T(8,128)(2,1)S(1)} %fusion.2), channel_id=1, source_target_pairs={{0,8},{1,9},{2,10},{3,11},{4,12},{5,13},{6,14},{7,15},{8,0},{9,1},... | collective-permute-start | bytes 786440 | tf_op jit(solution)/shard_map/ppermute | solution.py:34
  127.4 0.7 collective-permute-done.33
  128.1 1.6 %collective-permute-start.34 = (bf16[64,2048]{1,0:T(8,128)(2,1)S(1)}, bf16[64,2048]{1,0:T(8,128)(2,1)S(1)}, u32[]{:S(2)}, u32[]{:S(2)}) collective-permute-start(bf16[64,2048]{1,0:T(8,128)(2,1)S(1)} %fusion), channel_id=1, source_target_pairs={{0,24},{1,25},{2,26},{3,27},{4,28},{5,29},{6,30},{7,31},{8,16},{9,... | collective-permute-start | bytes 786440 | tf_op jit(solution)/shard_map/ppermute | solution.py:34
  129.8 4.7 %collective-permute-done.16 = bf16[64,2048]{1,0:T(8,128)(2,1)S(1)} collective-permute-done((bf16[64,2048]{1,0:T(8,128)(2,1)S(1)}, bf16[64,2048]{1,0:T(8,128)(2,1)S(1)}, u32[]{:S(2)}, u32[]{:S(2)}) %collective-permute-start.16) | collective-permute-done | bytes 262176 | tf_op jit(solution)/shard_map/ppermute | solution.py:34
  134.5 10.3 %collective-permute-done.25 = bf16[64,2048]{1,0:T(8,128)(2,1)S(1)} collective-permute-done((bf16[64,2048]{1,0:T(8,128)(2,1)S(1)}, bf16[64,2048]{1,0:T(8,128)(2,1)S(1)}, u32[]{:S(2)}, u32[]{:S(2)}) %collective-permute-start.25) | collective-permute-done | bytes 262176 | tf_op jit(solution)/shard_map/ppermute | solution.py:34
  144.8 6.4 %collective-permute-done.34 = bf16[64,2048]{1,0:T(8,128)(2,1)S(1)} collective-permute-done((bf16[64,2048]{1,0:T(8,128)(2,1)S(1)}, bf16[64,2048]{1,0:T(8,128)(2,1)S(1)}, u32[]{:S(2)}, u32[]{:S(2)}) %collective-permute-start.34) | collective-permute-done | bytes 262176 | tf_op jit(solution)/shard_map/ppermute | solution.py:34
  151.2 0.9 fusion.6
  (83 shorter events, 1.6 us)
Async XLA Ops:
  6.2 7.8 %collective-permute-start = (bf16[64,2176]{1,0:T(8,128)(2,1)}, bf16[64,2176]{1,0:T(8,128)(2,1)S(1)}, u32[]{:S(2)}, u32[]{:S(2)}) collective-permute-start(bf16[64,2176]{1,0:T(8,128)(2,1)} %scaled_tokens.1), channel_id=1, source_target_pairs={{0,2},{1,5},{2,0},{3,7},{4,6},{5,1},{6,4},{7,3},{8,10},{9,13},{10,... | collective-permute-start | bytes 835592 | tf_op jit(solution)/shard_map/ppermute | solution.py:34
  7.7 11.5 %collective-permute-start.8 = (bf16[64,2176]{1,0:T(8,128)(2,1)}, bf16[64,2176]{1,0:T(8,128)(2,1)S(1)}, u32[]{:S(2)}, u32[]{:S(2)}) collective-permute-start(bf16[64,2176]{1,0:T(8,128)(2,1)} %scaled_tokens.1), channel_id=1, source_target_pairs={{0,8},{1,9},{2,10},{3,11},{4,12},{5,13},{6,14},{7,15},{8,0},{9,1},... | collective-permute-start | bytes 835592 | tf_op jit(solution)/shard_map/ppermute | solution.py:34
  8.1 22.0 %collective-permute-start.17 = (bf16[64,2176]{1,0:T(8,128)(2,1)}, bf16[64,2176]{1,0:T(8,128)(2,1)S(1)}, u32[]{:S(2)}, u32[]{:S(2)}) collective-permute-start(bf16[64,2176]{1,0:T(8,128)(2,1)} %scaled_tokens.1), channel_id=1, source_target_pairs={{0,16},{1,17},{2,18},{3,19},{4,20},{5,21},{6,22},{7,23},{8,24},{9,... | collective-permute-start | bytes 835592 | tf_op jit(solution)/shard_map/ppermute | solution.py:34
  10.7 24.5 %collective-permute-start.26 = (bf16[64,2176]{1,0:T(8,128)(2,1)}, bf16[64,2176]{1,0:T(8,128)(2,1)S(1)}, u32[]{:S(2)}, u32[]{:S(2)}) collective-permute-start(bf16[64,2176]{1,0:T(8,128)(2,1)} %scaled_tokens.1), channel_id=1, source_target_pairs={{0,24},{1,25},{2,26},{3,27},{4,28},{5,29},{6,30},{7,31},{8,16},{9,... | collective-permute-start | bytes 835592 | tf_op jit(solution)/shard_map/ppermute | solution.py:34
  11.2 2.8 %copy-start.18 = (bf16[64,2176]{1,0:T(8,128)(2,1)S(1)}, bf16[64,2176]{1,0:T(8,128)(2,1)}, u32[]{:S(2)}) copy-start(bf16[64,2176]{1,0:T(8,128)(2,1)} %scaled_tokens.1) | copy-start | bytes 835588
  14.0 50.9 %collective-permute-start.5 = (bf16[384,2048]{1,0:T(8,128)(2,1)}, bf16[384,2048]{1,0:T(8,128)(2,1)}, u32[]{:S(2)}, u32[]{:S(2)}) collective-permute-start(bf16[384,2048]{1,0:T(8,128)(2,1)} %dynamic-slice_bitcast_fusion), channel_id=1, source_target_pairs={{0,1},{1,0},{2,3},{3,2},{4,5},{5,4},{6,7},{7,6},{8,9},{9,8},{10,11... | collective-permute-start | bytes 4718600 | tf_op jit(solution)/shard_map/ppermute | solution.py:34
  14.0 38.2 %copy-start.5 = (bf16[128,2176]{1,0:T(8,128)(2,1)}, bf16[128,2176]{1,0:T(8,128)(2,1)S(1)}, u32[]{:S(2)}) copy-start(bf16[128,2176]{1,0:T(8,128)(2,1)S(1)} %pad_maximum_fusion.near_ref) | copy-start | bytes 1671172
  14.0 38.2 %copy-start.1 = (bf16[1,4096,384]{2,1,0:T(8,128)(2,1)S(1)}, bf16[1,4096,384]{2,1,0:T(8,128)(2,1)}, u32[]{:S(2)}) copy-start(bf16[1,4096,384]{2,1,0:T(8,128)(2,1)} %param.11) | copy-start | bytes 9437188
  14.0 32.7 %collective-permute-start.2 = (bf16[128,2176]{1,0:T(8,128)(2,1)S(1)}, bf16[128,2176]{1,0:T(8,128)(2,1)S(1)}, u32[]{:S(2)}, u32[]{:S(2)}) collective-permute-start(bf16[128,2176]{1,0:T(8,128)(2,1)S(1)} %pad_maximum_fusion.near_ref), channel_id=1, source_target_pairs={{0,4},{1,3},{2,6},{3,1},{4,0},{5,7},{6,2},{7,5},{8,12},{9,11},{10,... | collective-permute-start | bytes 1671176 | tf_op jit(solution)/shard_map/ppermute | solution.py:34
  19.2 28.1 %collective-permute-start.1 = (bf16[128,2176]{1,0:T(8,128)(2,1)S(1)}, bf16[128,2176]{1,0:T(8,128)(2,1)S(1)}, u32[]{:S(2)}, u32[]{:S(2)}) collective-permute-start(bf16[128,2176]{1,0:T(8,128)(2,1)S(1)} %pad_maximum_fusion.near_ref), channel_id=1, source_target_pairs={{0,1},{1,0},{2,3},{3,2},{4,5},{5,4},{6,7},{7,6},{8,9},{9,8},{10,11... | collective-permute-start | bytes 1671176 | tf_op jit(solution)/shard_map/ppermute | solution.py:34
  30.1 6.6 %collective-permute-start.9 = (bf16[64,2176]{1,0:T(8,128)(2,1)S(1)}, bf16[64,2176]{1,0:T(8,128)(2,1)S(1)}, u32[]{:S(2)}, u32[]{:S(2)}) collective-permute-start(bf16[64,2176]{1,0:T(8,128)(2,1)S(1)} %collective-permute-done.8), channel_id=1, source_target_pairs={{0,2},{1,5},{2,0},{3,7},{4,6},{5,1},{6,4},{7,3},{8,10},{9,13},{10,... | collective-permute-start | bytes 835592 | tf_op jit(solution)/shard_map/ppermute | solution.py:34
  35.2 6.5 %collective-permute-start.18 = (bf16[64,2176]{1,0:T(8,128)(2,1)S(1)}, bf16[64,2176]{1,0:T(8,128)(2,1)S(1)}, u32[]{:S(2)}, u32[]{:S(2)}) collective-permute-start(bf16[64,2176]{1,0:T(8,128)(2,1)S(1)} %collective-permute-done.17), channel_id=1, source_target_pairs={{0,2},{1,5},{2,0},{3,7},{4,6},{5,1},{6,4},{7,3},{8,10},{9,13},{10,... | collective-permute-start | bytes 835592 | tf_op jit(solution)/shard_map/ppermute | solution.py:34
  36.7 10.0 %collective-permute-start.27 = (bf16[64,2176]{1,0:T(8,128)(2,1)S(1)}, bf16[64,2176]{1,0:T(8,128)(2,1)S(1)}, u32[]{:S(2)}, u32[]{:S(2)}) collective-permute-start(bf16[64,2176]{1,0:T(8,128)(2,1)S(1)} %collective-permute-done.26), channel_id=1, source_target_pairs={{0,2},{1,5},{2,0},{3,7},{4,6},{5,1},{6,4},{7,3},{8,10},{9,13},{10,... | collective-permute-start | bytes 835592 | tf_op jit(solution)/shard_map/ppermute | solution.py:34
  37.4 20.1 %copy-start.9 = (bf16[128,2176]{1,0:T(8,128)(2,1)}, bf16[128,2176]{1,0:T(8,128)(2,1)S(1)}, u32[]{:S(2)}) copy-start(bf16[128,2176]{1,0:T(8,128)(2,1)S(1)} %constant_dynamic-update-slice_fusion.near_ref) | copy-start | bytes 1671172
  41.8 9.6 %collective-permute-start.11 = (bf16[128,2176]{1,0:T(8,128)(2,1)S(1)}, bf16[128,2176]{1,0:T(8,128)(2,1)}, u32[]{:S(2)}, u32[]{:S(2)}) collective-permute-start(bf16[128,2176]{1,0:T(8,128)(2,1)S(1)} %constant_dynamic-update-slice_fusion.near_ref), channel_id=1, source_target_pairs={{0,4},{1,3},{2,6},{3,1},{4,0},{5,7},{6,2},{7,5},{8,12},{9,11},{10,... | collective-permute-start | bytes 1671176 | tf_op jit(solution)/shard_map/ppermute | solution.py:34
  46.7 10.8 %collective-permute-start.10 = (bf16[128,2176]{1,0:T(8,128)(2,1)S(1)}, bf16[128,2176]{1,0:T(8,128)(2,1)S(1)}, u32[]{:S(2)}, u32[]{:S(2)}) collective-permute-start(bf16[128,2176]{1,0:T(8,128)(2,1)S(1)} %constant_dynamic-update-slice_fusion.near_ref), channel_id=1, source_target_pairs={{0,1},{1,0},{2,3},{3,2},{4,5},{5,4},{6,7},{7,6},{8,9},{9,8},{10,11... | collective-permute-start | bytes 1671176 | tf_op jit(solution)/shard_map/ppermute | solution.py:34
  46.7 10.8 %copy-start.14 = (bf16[128,2176]{1,0:T(8,128)(2,1)}, bf16[128,2176]{1,0:T(8,128)(2,1)S(1)}, u32[]{:S(2)}) copy-start(bf16[128,2176]{1,0:T(8,128)(2,1)S(1)} %collective-permute-done.2.far_ref) | copy-start | bytes 1671172
  46.7 5.2 %collective-permute-start.3 = (bf16[128,2176]{1,0:T(8,128)(2,1)S(1)}, bf16[128,2176]{1,0:T(8,128)(2,1)S(1)}, u32[]{:S(2)}, u32[]{:S(2)}) collective-permute-start(bf16[128,2176]{1,0:T(8,128)(2,1)S(1)} %collective-permute-done.2.far_ref), channel_id=1, source_target_pairs={{0,1},{1,0},{2,3},{3,2},{4,5},{5,4},{6,7},{7,6},{8,9},{9,8},{10,11... | collective-permute-start | bytes 1671176 | tf_op jit(solution)/shard_map/ppermute | solution.py:34
  47.2 10.3 %copy-start.7 = (bf16[128,2176]{1,0:T(8,128)(2,1)}, bf16[128,2176]{1,0:T(8,128)(2,1)S(1)}, u32[]{:S(2)}) copy-start(bf16[128,2176]{1,0:T(8,128)(2,1)S(1)} %constant_dynamic-update-slice_fusion.4.near_ref) | copy-start | bytes 1671172
  47.3 11.3 %collective-permute-start.20 = (bf16[128,2176]{1,0:T(8,128)(2,1)}, bf16[128,2176]{1,0:T(8,128)(2,1)}, u32[]{:S(2)}, u32[]{:S(2)}) collective-permute-start(bf16[128,2176]{1,0:T(8,128)(2,1)} %constant_dynamic-update-slice_fusion.2.near_ref), channel_id=1, source_target_pairs={{0,4},{1,3},{2,6},{3,1},{4,0},{5,7},{6,2},{7,5},{8,12},{9,11},{10,... | collective-permute-start | bytes 1671176 | tf_op jit(solution)/shard_map/ppermute | solution.py:34
  51.4 11.8 %collective-permute-start.29 = (bf16[128,2176]{1,0:T(8,128)(2,1)S(1)}, bf16[128,2176]{1,0:T(8,128)(2,1)S(1)}, u32[]{:S(2)}, u32[]{:S(2)}) collective-permute-start(bf16[128,2176]{1,0:T(8,128)(2,1)S(1)} %constant_dynamic-update-slice_fusion.4.near_ref), channel_id=1, source_target_pairs={{0,4},{1,3},{2,6},{3,1},{4,0},{5,7},{6,2},{7,5},{8,12},{9,11},{10,... | collective-permute-start | bytes 1671176 | tf_op jit(solution)/shard_map/ppermute | solution.py:34
  51.9 20.6 %collective-permute-start.12 = (bf16[128,2176]{1,0:T(8,128)(2,1)}, bf16[128,2176]{1,0:T(8,128)(2,1)}, u32[]{:S(2)}, u32[]{:S(2)}) collective-permute-start(bf16[128,2176]{1,0:T(8,128)(2,1)} %collective-permute-done.11.far_ref), channel_id=1, source_target_pairs={{0,1},{1,0},{2,3},{3,2},{4,5},{5,4},{6,7},{7,6},{8,9},{9,8},{10,11... | collective-permute-start | bytes 1671176 | tf_op jit(solution)/shard_map/ppermute | solution.py:34
  52.2 1.9 %copy-start.3 = (bf16[1,4096,384]{2,1,0:T(8,128)(2,1)S(1)}, bf16[1,4096,384]{2,1,0:T(8,128)(2,1)}, u32[]{:S(2)}) copy-start(bf16[1,4096,384]{2,1,0:T(8,128)(2,1)} %param.12) | copy-start | bytes 9437188
  54.1 12.3 %copy-start = (bf16[1,384,4096]{2,1,0:T(8,128)(2,1)S(1)}, bf16[1,384,4096]{2,1,0:T(8,128)(2,1)}, u32[]{:S(2)}) copy-start(bf16[1,384,4096]{2,1,0:T(8,128)(2,1)} %param.13) | copy-start | bytes 9437188
  57.5 0.8 copy-start.16
  58.3 21.2 %collective-permute-start.19 = (bf16[128,2176]{1,0:T(8,128)(2,1)}, bf16[128,2176]{1,0:T(8,128)(2,1)}, u32[]{:S(2)}, u32[]{:S(2)}) collective-permute-start(bf16[128,2176]{1,0:T(8,128)(2,1)} %constant_dynamic-update-slice_fusion.2.near_ref), channel_id=1, source_target_pairs={{0,1},{1,0},{2,3},{3,2},{4,5},{5,4},{6,7},{7,6},{8,9},{9,8},{10,11... | collective-permute-start | bytes 1671176 | tf_op jit(solution)/shard_map/ppermute | solution.py:34
  58.6 22.1 %collective-permute-start.21 = (bf16[128,2176]{1,0:T(8,128)(2,1)}, bf16[128,2176]{1,0:T(8,128)(2,1)}, u32[]{:S(2)}, u32[]{:S(2)}) collective-permute-start(bf16[128,2176]{1,0:T(8,128)(2,1)} %collective-permute-done.20.far_ref), channel_id=1, source_target_pairs={{0,1},{1,0},{2,3},{3,2},{4,5},{5,4},{6,7},{7,6},{8,9},{9,8},{10,11... | collective-permute-start | bytes 1671176 | tf_op jit(solution)/shard_map/ppermute | solution.py:34
  63.2 0.8 copy-start.12
  64.0 1.4 collective-permute-start.4
  64.9 20.5 %collective-permute-start.28 = (bf16[128,2176]{1,0:T(8,128)(2,1)}, bf16[128,2176]{1,0:T(8,128)(2,1)S(1)}, u32[]{:S(2)}, u32[]{:S(2)}) collective-permute-start(bf16[128,2176]{1,0:T(8,128)(2,1)} %copy-done.7), channel_id=1, source_target_pairs={{0,1},{1,0},{2,3},{3,2},{4,5},{5,4},{6,7},{7,6},{8,9},{9,8},{10,11... | collective-permute-start | bytes 1671176 | tf_op jit(solution)/shard_map/ppermute | solution.py:34
  65.5 19.9 %collective-permute-start.30 = (bf16[128,2176]{1,0:T(8,128)(2,1)}, bf16[128,2176]{1,0:T(8,128)(2,1)S(1)}, u32[]{:S(2)}, u32[]{:S(2)}) collective-permute-start(bf16[128,2176]{1,0:T(8,128)(2,1)} %copy-done.12), channel_id=1, source_target_pairs={{0,1},{1,0},{2,3},{3,2},{4,5},{5,4},{6,7},{7,6},{8,9},{9,8},{10,11... | collective-permute-start | bytes 1671176 | tf_op jit(solution)/shard_map/ppermute | solution.py:34
  66.5 1.1 copy-start.6
  67.5 1.1 copy-start.15
  68.6 4.6 %copy-start.2 = (bf16[1,4096,384]{2,1,0:T(8,128)(2,1)S(1)}, bf16[1,4096,384]{2,1,0:T(8,128)(2,1)}, u32[]{:S(2)}) copy-start(bf16[1,4096,384]{2,1,0:T(8,128)(2,1)} %param.11) | copy-start | bytes 9437188
  68.6 4.6 %copy-start.4 = (bf16[1,4096,384]{2,1,0:T(8,128)(2,1)S(1)}, bf16[1,4096,384]{2,1,0:T(8,128)(2,1)}, u32[]{:S(2)}) copy-start(bf16[1,4096,384]{2,1,0:T(8,128)(2,1)} %param.12) | copy-start | bytes 9437188
  72.5 30.5 %collective-permute-start.6 = (bf16[128,2048]{1,0:T(8,128)(2,1)S(1)}, bf16[128,2048]{1,0:T(8,128)(2,1)S(1)}, u32[]{:S(2)}, u32[]{:S(2)}) collective-permute-start(bf16[128,2048]{1,0:T(8,128)(2,1)S(1)} %get-tuple-element.14), channel_id=1, source_target_pairs={{0,4},{1,3},{2,6},{3,1},{4,0},{5,7},{6,2},{7,5},{8,12},{9,11},{10,... | collective-permute-start | bytes 1572872 | tf_op jit(solution)/shard_map/ppermute | solution.py:34
  73.1 1.1 copy-start.10
  74.2 1.1 copy-start.17
  79.5 5.8 %copy-start.8 = (bf16[128,2176]{1,0:T(8,128)(2,1)S(1)}, bf16[128,2176]{1,0:T(8,128)(2,1)}, u32[]{:S(2)}) copy-start(bf16[128,2176]{1,0:T(8,128)(2,1)} %copy-done.7) | copy-start | bytes 1671172
  79.5 5.8 %copy-start.13 = (bf16[128,2176]{1,0:T(8,128)(2,1)S(1)}, bf16[128,2176]{1,0:T(8,128)(2,1)}, u32[]{:S(2)}) copy-start(bf16[128,2176]{1,0:T(8,128)(2,1)} %copy-done.12) | copy-start | bytes 1671172
  79.6 9.8 %collective-permute-start.13 = (bf16[256,384]{1,0:T(8,128)(2,1)S(1)}, bf16[256,384]{1,0:T(8,128)(2,1)S(1)}, u32[]{:S(2)}, u32[]{:S(2)}) collective-permute-start(bf16[256,384]{1,0:T(8,128)(2,1)S(1)} %hidden_units.5.mine_ref), channel_id=1, source_target_pairs={{0,1},{1,0},{2,3},{3,2},{4,5},{5,4},{6,7},{7,6},{8,9},{9,8},{10,11... | collective-permute-start | bytes 589832 | tf_op jit(solution)/shard_map/ppermute | solution.py:34
  85.2 4.1 %copy-start.11 = (bf16[128,2176]{1,0:T(8,128)(2,1)S(1)}, bf16[128,2176]{1,0:T(8,128)(2,1)}, u32[]{:S(2)}) copy-start(bf16[128,2176]{1,0:T(8,128)(2,1)} %copy-done.9) | copy-start | bytes 1671172
  85.2 8.3 %collective-permute-start.22 = (bf16[256,384]{1,0:T(8,128)(2,1)S(1)}, bf16[256,384]{1,0:T(8,128)(2,1)S(1)}, u32[]{:S(2)}, u32[]{:S(2)}) collective-permute-start(bf16[256,384]{1,0:T(8,128)(2,1)S(1)} %hidden_units.6.mine_ref), channel_id=1, source_target_pairs={{0,1},{1,0},{2,3},{3,2},{4,5},{5,4},{6,7},{7,6},{8,9},{9,8},{10,11... | collective-permute-start | bytes 589832 | tf_op jit(solution)/shard_map/ppermute | solution.py:34
  88.8 10.0 %collective-permute-start.31 = (bf16[256,384]{1,0:T(8,128)(2,1)S(1)}, bf16[256,384]{1,0:T(8,128)(2,1)S(1)}, u32[]{:S(2)}, u32[]{:S(2)}) collective-permute-start(bf16[256,384]{1,0:T(8,128)(2,1)S(1)} %hidden_units.7.mine_ref), channel_id=1, source_target_pairs={{0,1},{1,0},{2,3},{3,2},{4,5},{5,4},{6,7},{7,6},{8,9},{9,8},{10,11... | collective-permute-start | bytes 589832 | tf_op jit(solution)/shard_map/ppermute | solution.py:34
  93.0 11.8 %collective-permute-start.14 = (bf16[128,2048]{1,0:T(8,128)(2,1)S(1)}, bf16[128,2048]{1,0:T(8,128)(2,1)S(1)}, u32[]{:S(2)}, u32[]{:S(2)}) collective-permute-start(bf16[128,2048]{1,0:T(8,128)(2,1)S(1)} %get-tuple-element.16), channel_id=1, source_target_pairs={{0,4},{1,3},{2,6},{3,1},{4,0},{5,7},{6,2},{7,5},{8,12},{9,11},{10,... | collective-permute-start | bytes 1572872 | tf_op jit(solution)/shard_map/ppermute | solution.py:34
  97.2 13.0 %collective-permute-start.23 = (bf16[128,2048]{1,0:T(8,128)(2,1)S(1)}, bf16[128,2048]{1,0:T(8,128)(2,1)S(1)}, u32[]{:S(2)}, u32[]{:S(2)}) collective-permute-start(bf16[128,2048]{1,0:T(8,128)(2,1)S(1)} %get-tuple-element.18), channel_id=1, source_target_pairs={{0,4},{1,3},{2,6},{3,1},{4,0},{5,7},{6,2},{7,5},{8,12},{9,11},{10,... | collective-permute-start | bytes 1572872 | tf_op jit(solution)/shard_map/ppermute | solution.py:34
  102.4 19.0 %collective-permute-start.32 = (bf16[128,2048]{1,0:T(8,128)(2,1)S(1)}, bf16[128,2048]{1,0:T(8,128)(2,1)S(1)}, u32[]{:S(2)}, u32[]{:S(2)}) collective-permute-start(bf16[128,2048]{1,0:T(8,128)(2,1)S(1)} %get-tuple-element.20), channel_id=1, source_target_pairs={{0,4},{1,3},{2,6},{3,1},{4,0},{5,7},{6,2},{7,5},{8,12},{9,11},{10,... | collective-permute-start | bytes 1572872 | tf_op jit(solution)/shard_map/ppermute | solution.py:34
  103.2 26.6 %collective-permute-start.7 = (bf16[64,2048]{1,0:T(8,128)(2,1)S(1)}, bf16[64,2048]{1,0:T(8,128)(2,1)S(1)}, u32[]{:S(2)}, u32[]{:S(2)}) collective-permute-start(bf16[64,2048]{1,0:T(8,128)(2,1)S(1)} %slice.69), channel_id=1, source_target_pairs={{0,2},{1,5},{2,0},{3,7},{4,6},{5,1},{6,4},{7,3},{8,10},{9,13},{10,... | collective-permute-start | bytes 786440 | tf_op jit(solution)/shard_map/ppermute | solution.py:34
  104.9 16.8 %collective-permute-start.15 = (bf16[64,2048]{1,0:T(8,128)(2,1)S(1)}, bf16[64,2048]{1,0:T(8,128)(2,1)S(1)}, u32[]{:S(2)}, u32[]{:S(2)}) collective-permute-start(bf16[64,2048]{1,0:T(8,128)(2,1)S(1)} %slice.68), channel_id=1, source_target_pairs={{0,2},{1,5},{2,0},{3,7},{4,6},{5,1},{6,4},{7,3},{8,10},{9,13},{10,... | collective-permute-start | bytes 786440 | tf_op jit(solution)/shard_map/ppermute | solution.py:34
  110.4 16.9 %collective-permute-start.24 = (bf16[64,2048]{1,0:T(8,128)(2,1)S(1)}, bf16[64,2048]{1,0:T(8,128)(2,1)S(1)}, u32[]{:S(2)}, u32[]{:S(2)}) collective-permute-start(bf16[64,2048]{1,0:T(8,128)(2,1)S(1)} %slice.67), channel_id=1, source_target_pairs={{0,2},{1,5},{2,0},{3,7},{4,6},{5,1},{6,4},{7,3},{8,10},{9,13},{10,... | collective-permute-start | bytes 786440 | tf_op jit(solution)/shard_map/ppermute | solution.py:34
  121.6 6.4 %collective-permute-start.33 = (bf16[64,2048]{1,0:T(8,128)(2,1)S(1)}, bf16[64,2048]{1,0:T(8,128)(2,1)S(1)}, u32[]{:S(2)}, u32[]{:S(2)}) collective-permute-start(bf16[64,2048]{1,0:T(8,128)(2,1)S(1)} %slice.66), channel_id=1, source_target_pairs={{0,2},{1,5},{2,0},{3,7},{4,6},{5,1},{6,4},{7,3},{8,10},{9,13},{10,... | collective-permute-start | bytes 786440 | tf_op jit(solution)/shard_map/ppermute | solution.py:34
  121.8 12.7 %collective-permute-start.16 = (bf16[64,2048]{1,0:T(8,128)(2,1)S(1)}, bf16[64,2048]{1,0:T(8,128)(2,1)S(1)}, u32[]{:S(2)}, u32[]{:S(2)}) collective-permute-start(bf16[64,2048]{1,0:T(8,128)(2,1)S(1)} %fusion.2), channel_id=1, source_target_pairs={{0,8},{1,9},{2,10},{3,11},{4,12},{5,13},{6,14},{7,15},{8,0},{9,1},... | collective-permute-start | bytes 786440 | tf_op jit(solution)/shard_map/ppermute | solution.py:34
  127.3 17.5 %collective-permute-start.25 = (bf16[64,2048]{1,0:T(8,128)(2,1)S(1)}, bf16[64,2048]{1,0:T(8,128)(2,1)S(1)}, u32[]{:S(2)}, u32[]{:S(2)}) collective-permute-start(bf16[64,2048]{1,0:T(8,128)(2,1)S(1)} %fusion.1), channel_id=1, source_target_pairs={{0,16},{1,17},{2,18},{3,19},{4,20},{5,21},{6,22},{7,23},{8,24},{9,... | collective-permute-start | bytes 786440 | tf_op jit(solution)/shard_map/ppermute | solution.py:34
  128.1 23.1 %collective-permute-start.34 = (bf16[64,2048]{1,0:T(8,128)(2,1)S(1)}, bf16[64,2048]{1,0:T(8,128)(2,1)S(1)}, u32[]{:S(2)}, u32[]{:S(2)}) collective-permute-start(bf16[64,2048]{1,0:T(8,128)(2,1)S(1)} %fusion), channel_id=1, source_target_pairs={{0,24},{1,25},{2,26},{3,27},{4,28},{5,29},{6,30},{7,31},{8,16},{9,... | collective-permute-start | bytes 786440 | tf_op jit(solution)/shard_map/ppermute | solution.py:34

commit v2 on v0

--- a/solution.py
+++ b/solution.py
@@ -1,15 +1,16 @@
+import functools
 import math
 
 import jax
 import jax.numpy as jnp
 from jax import lax
+from jax.experimental import pallas as pl
+from jax.experimental.pallas import tpu as pltpu
 from jax.sharding import PartitionSpec as P
 
 WALSH = 128
-
-
-def partner_2(array, axis, bit):
-    return lax.ppermute(array, axis, [(i, i ^ 1 << bit) for i in range(lax.axis_size(axis))])
+LANES = 128
+VMEM_BYTES = 8 << 20
 
 
 def walsh_signs(length):
@@ -26,7 +27,379 @@
     return (1 - 2 * (parity % 2)).astype(jnp.float32)
 
 
-def shards(
+def swap(array, masks, core=0):
+    experts = lax.axis_size("expert")
+    pairs = [
+        (e * 2 + t, (e ^ masks[t]) * 2 + (t ^ core)) for e in range(experts) for t in range(2)
+    ]
+    return lax.ppermute(array, ("expert", "tensor"), pairs)
+
+
+def cost():
+    return pl.CostEstimate(flops=10**9, bytes_accessed=10**6, transcendentals=0)
+
+
+def scaled_tokens(values, scales, ids, route_weights, experts):
+    rows, features = values.shape
+    blocks, top = scales.shape[1], ids.shape[1]
+    width = features // blocks
+
+    def kernel(values_ref, scales_ref, ids_ref, weights_ref, out_ref):
+        spread = (
+            lax.broadcasted_iota(jnp.int32, (blocks, features), 1) // width
+            == lax.broadcasted_iota(jnp.int32, (blocks, features), 0)
+        )
+        factor = lax.dot_general(
+            scales_ref[...],
+            jnp.where(spread, 1.0, 0.0).astype(jnp.bfloat16),
+            (((0,), (0,)), ((), ())),
+            preferred_element_type=jnp.float32,
+        )
+        out_ref[:, :features] = (values_ref[...].astype(jnp.float32) * factor).astype(jnp.bfloat16)
+        weights = weights_ref[...].astype(jnp.float32)
+        route = weights / jnp.sum(weights, axis=0, keepdims=True)
+        lane = lax.broadcasted_iota(jnp.int32, (LANES, rows), 0)
+        expert = lax.rem(lane, experts)
+        table = jnp.zeros((LANES, rows), jnp.float32)
+        for k in range(top):
+            table = table + jnp.where(ids_ref[k : k + 1, :] == expert, route[k : k + 1, :], 0.0)
+        high = table.astype(jnp.bfloat16).astype(jnp.float32)
+        tail = jnp.where(lane < experts, high, jnp.where(lane < 2 * experts, table - high, 0.0))
+        same = lax.broadcasted_iota(jnp.int32, (rows, rows), 0) == lax.broadcasted_iota(
+            jnp.int32, (rows, rows), 1
+        )
+        out_ref[:, features:] = lax.dot_general(
+            jnp.where(same, 1.0, 0.0).astype(jnp.bfloat16),
+            tail.astype(jnp.bfloat16),
+            (((1,), (1,)), ((), ())),
+            preferred_element_type=jnp.float32,
+        ).astype(jnp.bfloat16)
+
+    return pl.pallas_call(
+        kernel,
+        out_shape=jax.ShapeDtypeStruct((rows, features + LANES), jnp.bfloat16),
+        cost_estimate=cost(),
+        name="scaled_tokens",
+    )(values, scales.T, ids.T, route_weights.T)
+
+
+def pick_rows(near, next_near, lanes, capacity, after):
+    rows, wide = near.shape
+    count = 2 * capacity
+
+    def kernel(near_ref, next_ref, lanes_ref, after_ref, mine_ref, theirs_ref, choice_ref):
+        del after_ref
+        both = jnp.concatenate([near_ref[...], next_ref[...]], axis=0)
+        tails = jnp.concatenate([near_ref[:, wide - LANES :], next_ref[:, wide - LANES :]], axis=0)
+        chosen = jnp.where(tails.astype(jnp.float32) > 0.0, 1.0, 0.0).astype(jnp.bfloat16)
+        named = lax.dot_general(
+            lanes_ref[...], chosen, (((1,), (1,)), ((), ())), preferred_element_type=jnp.float32
+        )
+        one = lax.broadcasted_iota(jnp.int32, (2 * rows, 2 * rows), 0)
+        two = lax.broadcasted_iota(jnp.int32, (2 * rows, 2 * rows), 1)
+        before = jnp.where((one < two) & (one // rows == two // rows), 1.0, 0.0)
+        rank = jnp.dot(
+            named.astype(jnp.bfloat16),
+            before.astype(jnp.bfloat16),
+            preferred_element_type=jnp.float32,
+        )
+        place = jnp.where(named > 0.5, rank, -1.0).astype(jnp.int32)
+        slot = lax.broadcasted_iota(jnp.int32, (2 * count, 2 * rows), 0)
+        token = lax.broadcasted_iota(jnp.int32, (2 * count, 2 * rows), 1)
+        wanted = jnp.where(slot < count, place[0:1, :], place[1:2, :])
+        block = lax.rem(slot, count) // capacity
+        hit = (wanted == lax.rem(slot, capacity)) & (token // rows == block)
+        choice = jnp.where(hit, 1.0, 0.0).astype(jnp.bfloat16)
+        choice_ref[...] = choice
+        picked = jnp.dot(choice, both, preferred_element_type=jnp.float32).astype(jnp.bfloat16)
+        mine_ref[...] = picked[:count]
+        theirs_ref[...] = picked[count:]
+
+    vmem = pl.BlockSpec(memory_space=pltpu.VMEM)
+    return pl.pallas_call(
+        kernel,
+        in_specs=[vmem, vmem, vmem, pl.BlockSpec(memory_space=pl.ANY)],
+        out_shape=[
+            jax.ShapeDtypeStruct((count, wide), jnp.bfloat16),
+            jax.ShapeDtypeStruct((count, wide), jnp.bfloat16),
+            jax.ShapeDtypeStruct((2 * count, 2 * rows), jnp.bfloat16),
+        ],
+        compiler_params=pltpu.CompilerParams(vmem_limit_bytes=VMEM_BYTES),
+        cost_estimate=cost(),
+        name="pick_rows",
+    )(near, next_near, lanes, after)
+
+
+def in_this_order(product, block):
+    return jnp.concatenate(
+        [
+            product[:block],
+            product[2 * block : 3 * block],
+            product[block : 2 * block],
+            product[3 * block :],
+        ],
+        axis=0,
+    )
+
+
+def hidden_units(core, near, near_pair, far, far_pair, gate, up, after):
+    count = near.shape[0]
+    rows = 2 * count
+    features, units = gate.shape
+    half = features // 2
+    step = LANES
+
+    def kernel(core_ref, near_ref, near_pair_ref, far_ref, far_pair_ref, gate_ref, up_ref,
+               after_ref, out_ref, own_rows, other_rows):
+        del after_ref
+        own_rows[:count] = near_ref[:, :half]
+        own_rows[count:] = far_ref[:, :half]
+        other_rows[:count] = near_pair_ref[:, :half]
+        other_rows[count:] = far_pair_ref[:, :half]
+        own = pl.multiple_of(core_ref[0] * half, half)
+        other = pl.multiple_of((1 - core_ref[0]) * half, half)
+        for at in range(0, units, step):
+            cols = slice(at, at + step)
+            w_own = jnp.concatenate(
+                [gate_ref[pl.ds(own, half), cols], up_ref[pl.ds(own, half), cols]], axis=1
+            )
+            w_other = jnp.concatenate(
+                [gate_ref[pl.ds(other, half), cols], up_ref[pl.ds(other, half), cols]], axis=1
+            )
+            both = jnp.dot(
+                own_rows[...], w_own, preferred_element_type=jnp.float32
+            ) + in_this_order(
+                jnp.dot(other_rows[...], w_other, preferred_element_type=jnp.float32), count // 2
+            )
+            gate_out, up_out = both[:, :step], both[:, step:]
+            out_ref[:, cols] = (gate_out / (1.0 + jnp.exp(-gate_out)) * up_out).astype(jnp.bfloat16)
+
+    vmem = pl.BlockSpec(memory_space=pltpu.VMEM)
+    return pl.pallas_call(
+        kernel,
+        in_specs=[pl.BlockSpec(memory_space=pltpu.SMEM)]
+        + [vmem] * 6
+        + [pl.BlockSpec(memory_space=pl.ANY)],
+        scratch_shapes=[pltpu.VMEM((rows, half), jnp.bfloat16)] * 2,
+        out_shape=jax.ShapeDtypeStruct((rows, units), jnp.bfloat16),
+        compiler_params=pltpu.CompilerParams(vmem_limit_bytes=VMEM_BYTES),
+        cost_estimate=cost(),
+        name="hidden_units",
+    )(core, near, near_pair, far, far_pair, gate, up, after)
+
+
+def routed_outputs(core, mine, theirs, mix, down, down_pair, near, far, lanes, after):
+    rows, units = mine.shape
+    features = down.shape[1] // 2
+    groups = units // WALSH
+    count = rows // 2
+    step = min(512, features)
+
+    def kernel(core_ref, mine_ref, theirs_ref, mix_ref, down_ref, pair_ref, near_ref, far_ref,
+               lanes_ref, after_ref, near_out, far_out, turned):
+        del after_ref
+        for g in range(groups):
+            cols = slice(g * WALSH, (g + 1) * WALSH)
+            both = jnp.dot(
+                mine_ref[:, cols], mix_ref[:WALSH], preferred_element_type=jnp.float32
+            ) + in_this_order(
+                jnp.dot(theirs_ref[:, cols], mix_ref[WALSH:], preferred_element_type=jnp.float32),
+                count // 2,
+            )
+            both = both.astype(jnp.bfloat16)
+            turned[:, cols] = both[:, :WALSH]
+            turned[:, units + g * WALSH : units + (g + 1) * WALSH] = both[:, WALSH:]
+        tails = jnp.concatenate([near_ref[:, features:], far_ref[:, features:]], axis=0)
+        route = jnp.sum(tails.astype(jnp.float32) * lanes_ref[...], axis=1, keepdims=True)
+        for at in range(0, features, step):
+            cols = pl.ds(pl.multiple_of(core_ref[0] * features + at, step), step)
+            out = jnp.dot(
+                turned[:, :units], down_ref[:, cols], preferred_element_type=jnp.float32
+            ) + jnp.dot(turned[:, units:], pair_ref[:, cols], preferred_element_type=jnp.float32)
+            scaled = (out * route).astype(jnp.bfloat16)
+            near_out[:, at : at + step] = scaled[:count]
+            far_out[:, at : at + step] = scaled[count:]
+
+    vmem = pl.BlockSpec(memory_space=pltpu.VMEM)
+    return pl.pallas_call(
+        kernel,
+        in_specs=[pl.BlockSpec(memory_space=pltpu.SMEM)]
+        + [vmem] * 8
+        + [pl.BlockSpec(memory_space=pl.ANY)],
+        scratch_shapes=[pltpu.VMEM((rows, 2 * units), jnp.bfloat16)],
+        out_shape=[
+            jax.ShapeDtypeStruct((count, features), jnp.bfloat16),
+            jax.ShapeDtypeStruct((count, features), jnp.bfloat16),
+        ],
+        compiler_params=pltpu.CompilerParams(vmem_limit_bytes=VMEM_BYTES),
+        cost_estimate=cost(),
+        name="routed_outputs",
+    )(core, mine, theirs, mix, down, down_pair, near, far, lanes, after)
+
+
+def spread_rows(choice, mine, back, after):
+    count, features = mine.shape
+    rows = choice.shape[1] // 2
+
+    def kernel(choice_ref, mine_ref, back_ref, after_ref, keep_ref, send_ref):
+        del after_ref
+        both = lax.dot_general(
+            choice_ref[...],
+            jnp.concatenate([mine_ref[...], back_ref[...]], axis=0),
+            (((0,), (0,)), ((), ())),
+            preferred_element_type=jnp.float32,
+        )
+        keep_ref[...] = both[:rows]
+        send_ref[...] = both[rows:].astype(jnp.bfloat16)
+
+    vmem = pl.BlockSpec(memory_space=pltpu.VMEM)
+    return pl.pallas_call(
+        kernel,
+        in_specs=[vmem, vmem, vmem, pl.BlockSpec(memory_space=pl.ANY)],
+        out_shape=[
+            jax.ShapeDtypeStruct((rows, features), jnp.float32),
+            jax.ShapeDtypeStruct((rows, features), jnp.bfloat16),
+        ],
+        compiler_params=pltpu.CompilerParams(vmem_limit_bytes=VMEM_BYTES),
+        cost_estimate=cost(),
+        name="spread_rows",
+    )(choice, mine, back, after)
+
+
+def add_rows(parts, kind, after):
+    def kernel(*refs):
+        total = refs[0][...].astype(jnp.float32)
+        for ref in refs[1 : len(parts)]:
+            total = total + ref[...].astype(jnp.float32)
+        refs[-1][...] = total.astype(kind)
+
+    vmem = pl.BlockSpec(memory_space=pltpu.VMEM)
+    return pl.pallas_call(
+        kernel,
+        in_specs=[vmem] * len(parts) + [pl.BlockSpec(memory_space=pl.ANY)],
+        out_shape=jax.ShapeDtypeStruct(parts[0].shape, kind),
+        compiler_params=pltpu.CompilerParams(vmem_limit_bytes=VMEM_BYTES),
+        cost_estimate=cost(),
+        name="add_rows",
+    )(*parts, after)
+
+
+def every_expert(
+    token_values, token_scales, expert_ids, route_weights, gate_weight, up_weight, down_weight
+):
+    experts = lax.axis_size("expert")
+    core_index = lax.axis_index("tensor")
+    core = core_index.astype(jnp.int32).reshape(1)
+    expert = lax.axis_index("expert")
+    rows, features = token_values.shape
+    top = expert_ids.shape[1]
+    capacity = min(rows, 5 * rows * top // (4 * experts))
+    gate, up, down = gate_weight[0], up_weight[0], down_weight[0]
+    first, second = (1, 2), (2, 1)
+    line = experts // 4
+
+    block = scaled_tokens(token_values, token_scales, expert_ids, route_weights, experts)
+    blocks = [block]
+    for index in range(1, line):
+        if index % 2 == 1 and index > 1:
+            blocks.append(swap(blocks[index - 1], (4, 4)))
+        else:
+            blocks.append(swap(block, (4 * index, 4 * index)))
+
+    down_pair = swap(down, (0, 0), 1)
+
+    signs = walsh_signs(WALSH) / math.sqrt(2 * WALSH)
+    sign = jnp.where(core_index == 0, 1.0, -1.0)
+    mix = jnp.concatenate(
+        [
+            jnp.concatenate([signs * sign, signs], axis=1),
+            jnp.concatenate([signs, -signs * sign], axis=1),
+        ],
+        axis=0,
+    ).astype(jnp.bfloat16)
+    lane = jnp.arange(LANES, dtype=jnp.int32)[None, :]
+    lanes = ((lane % experts == expert) & (lane < 2 * experts)).astype(jnp.float32)
+    beyond = expert ^ jnp.where(core_index == 0, second[0], second[1])
+    named = jnp.concatenate([lane == expert, lane == beyond] + [lane < 0] * 6, axis=0).astype(
+        jnp.bfloat16
+    )
+
+    state = [dict() for _ in range(line)]
+    last = blocks[-2]
+    total = None
+
+    def pick(k):
+        nonlocal last
+        it = state[k]
+        it["mine"], away, it["choice"] = pick_rows(
+            blocks[k], swap(blocks[k], first), named, capacity, last
+        )
+        it["mine_pair"] = swap(it["mine"], (0, 0), 1)
+        it["far"] = swap(away, second)
+        it["far_pair"] = swap(it["far"], (0, 0), 1)
+        last = it["choice"]
+
+    def expand_units(k):
+        nonlocal last
+        it = state[k]
+        it["hidden"] = hidden_units(
+            core, it["mine"], it["mine_pair"], it["far"], it["far_pair"], gate, up, last
+        )
+        it["hidden_pair"] = swap(it["hidden"], (0, 0), 1)
+        last = it["hidden"]
+
+    def contract_units(k):
+        nonlocal last
+        it = state[k]
+        it["out"], away = routed_outputs(
+            core, it["hidden"], it["hidden_pair"], mix, down, down_pair, it["mine"], it["far"],
+            lanes, last,
+        )
+        it["back"] = swap(away, second)
+        last = it["out"]
+
+    def spread(k):
+        nonlocal last
+        it = state[k]
+        it["keep"], away = spread_rows(it["choice"], it["out"], it["back"], last)
+        it["next"] = swap(away, first)
+        last = it["keep"]
+
+    def settle(k):
+        nonlocal last, total
+        it = state[k]
+        if k == 0:
+            total = last = add_rows([it["keep"], it["next"]], jnp.float32, last)
+            return
+        parts = [it["keep"], it["next"]]
+        if k % 2 == 1 and k > 1:
+            parts.append(state[k - 1]["sent"])
+        last = add_rows(parts, jnp.bfloat16, last)
+        mask = 4 if k % 2 == 0 else 4 * k
+        it["sent"] = swap(last, (mask, mask))
+
+    def absorb(k):
+        nonlocal last, total
+        if k % 2 == 1:
+            kind = jnp.bfloat16 if k == line - 1 else jnp.float32
+            total = last = add_rows([total, state[k]["sent"]], kind, last)
+
+    near_round = lambda k: (0, 1, 1, 2)[min(k, 3)] + max(0, k - 3)
+    stages = (
+        (settle, lambda k: 6 + near_round(k)),
+        (absorb, lambda k: 7 + near_round(k)),
+        (spread, lambda k: 5 + near_round(k)),
+        (contract_units, lambda k: 4 + near_round(k)),
+        (expand_units, lambda k: 3 + near_round(k)),
+        (pick, lambda k: 1 + near_round(k) - (k > 2) / 2),
+    )
+    due = [(when(k), name, k) for k in range(line) for name, (_, when) in enumerate(stages)]
+    for _, name, k in sorted(due):
+        stages[name][0](k)
+    return total
+
+
+def chosen_experts(
     token_values, token_scales, expert_ids, route_weights, gate_weight, up_weight, down_weight
 ):
     tok_rows, top_count = expert_ids.shape
@@ -70,7 +443,7 @@
     gate_out = jnp.dot(dequant, gate_weight[0], preferred_element_type=jnp.float32)
     up_out = jnp.dot(dequant, up_weight[0], preferred_element_type=jnp.float32)
     hidden = (jax.nn.silu(gate_out) * up_out).astype(jnp.bfloat16)
-    partner = partner_2(hidden, "tensor", 0)
+    partner = swap(hidden, (0, 0), 1)
     own_part = hidden.astype(jnp.float32)
     theirs = partner.astype(jnp.float32)
     combined = jnp.where(lax.axis_index("tensor") == 0, own_part + theirs, theirs - own_part)
@@ -101,6 +474,13 @@
     route = route_weights.astype(jnp.float32)
     route = route / jnp.sum(route, axis=1, keepdims=True)
     return jnp.sum(picked * route[:, :, None], axis=1).astype(jnp.bfloat16)
+
+
+def shards(*arrays):
+    experts = lax.axis_size("expert")
+    top = arrays[2].shape[1]
+    dense = 2 * top >= experts and experts % 4 == 0 and experts & (experts - 1) == 0
+    return (every_expert if dense else chosen_experts)(*arrays)
 
 
 def solution(mesh):

time: 256 us -> 102 us (0.40)
  blocking collectives: 79.5 us -> 0 us
  local copies, waits for them, and re-layouts: 38 us -> 2.69 us
  waiting for transfers between devices: 76.8 us -> 45 us
  starting transfers between devices: 7.3 us -> 31.4 us
  Pallas kernels: 0 us -> 21.8 us
  other arithmetic: 21.8 us -> 0.25 us
  matrix products: 16.5 us -> 0 us
  between operations: 13.6 us -> 0.3 us
    all_to_all x2 -> x0, blocking collectives: 77.3 us -> none  [the longest x1 66.9 us: shards(): lax.all_to_all(send_values, 'expert', split_axis=0, concat_axis=0, tiled=...]
    all_to_all x1 -> x0, waiting for transfers between devices: 57.7 us -> none  [shards(): lax.all_to_all(summed.reshape(experts, capacity, -1), 'expert', split_axi...]
    ppermute x1 -> x35, waiting for transfers between devices: 2.03 us -> 45 us  [swap(): return lax.ppermute(array, ('expert', 'tensor'), pairs)]
    ppermute x1 -> x35, starting transfers between devices: 0.16 us -> 31.4 us  [swap(): return lax.ppermute(array, ('expert', 'tensor'), pairs)]
    pallas_call x0 -> x23, Pallas kernels: none -> 21.8 us  [the longest x4 6.16 us: pick_rows(): pl.pallas_call(kernel, in_specs=[vmem, vmem, vmem, pl.BlockSpec(memory_sp...]
    mul x5 -> x0, local copies, waits for them, and re-layouts: 19.3 us -> none  [the longest x3 19.1 us: shards(): joined_values.astype(jnp.float32)]
    reduce_scatter x1 -> x0, waiting for transfers between devices: 17 us -> none  [shards(): lax.psum_scatter(partial_value, 'tensor', scatter_dimension=1, tiled=True)]
    dot_general x4 -> x0, matrix products: 16.5 us -> none  [the longest x1 6.24 us: shards(): jnp.dot(dequant, gate_weight[0], preferred_element_type=jnp.float32)]
  transfers between devices with their start and end apart: 4 -> 35, of which waited for: 3 -> 14; matrix products, arithmetic and copies ran while one was open for 9% -> 0% of each run, Pallas kernels for 0% -> 21%
where the time goes in v2:
time: 102 us; the launch traced here: 101 us
  waiting for transfers between devices  45 us (44%)
  starting transfers between devices  31.4 us (31%)
  Pallas kernels  21.8 us (21%)
  local copies, waits for them, and re-layouts  2.69 us (3%)
    ppermute x35, waiting for transfers between devices, swap(): return lax.ppermute(array, ('expert', 'tensor'), pairs)  45 us
    ppermute x35, starting transfers between devices, swap(): return lax.ppermute(array, ('expert', 'tensor'), pairs)  31.4 us
    pallas_call x4, Pallas kernels, pick_rows(): pl.pallas_call(kernel, in_specs=[vmem, vmem, vmem, pl.BlockSpec(memory_sp...  6.16 us
    pallas_call x4, Pallas kernels, hidden_units(): pl.pallas_call(kernel, in_specs=[pl.BlockSpec(memory_space=pltpu.SMEM)] +...  6.14 us
    pallas_call x4, Pallas kernels, routed_outputs(): pl.pallas_call(kernel, in_specs=[pl.BlockSpec(memory_space=pltpu.SMEM)] +...  5.26 us
    unnamed x12, local copies, waits for them, and re-layouts  2.65 us
  transfers between devices with their start and end apart: 35, of which 14 were waited for; matrix products, arithmetic and copies ran while one was open for 0% of the time, Pallas kernels for 21%

profile of v2, /device:TPU:8, one launch (start us, length us, event | category | flops | bytes accessed | tf_op | source)
XLA Modules:
  0.0 101.4 jit_solution(1417132359673296737)
XLA Ops:
  0.0 1.9 %scaled_tokens.1.near_ref = bf16[64,2176]{1,0:T(8,128)(2,1)} custom-call(bf16[64,2048]{1,0:T(8,128)(2,1)} %values_ref.1, bf16[16,64]{1,0:T(8,128)(2,1)} %bitcast.20, s32[8,64]{1,0:T(8,128)} %bitcast.21, s32[8,64]{1,0:T(8,128)} %bitcast.22), custom_call_target="tpu_custom_call" | custom-call | flops 1000000000 | bytes 1000000 | tf_op jit(solution)/shard_map/scaled_tokens/pallas_call | solution.py:78
  1.9 2.6 %collective-permute-start.1 = (bf16[64,2176]{1,0:T(8,128)(2,1)}, bf16[64,2176]{1,0:T(8,128)(2,1)}, u32[]{:S(2)}, u32[]{:S(2)}) collective-permute-start(bf16[64,2176]{1,0:T(8,128)(2,1)} %scaled_tokens.1.near_ref), channel_id=1, source_target_pairs={{0,16},{1,17},{2,18},{3,19},{4,20},{5,21},{6,22},{7,23},{8,24},{9,... | collective-permute-start | bytes 835592 | tf_op jit(solution)/shard_map/ppermute | solution.py:35
  4.5 1.5 %collective-permute-start = (bf16[64,2176]{1,0:T(8,128)(2,1)}, bf16[64,2176]{1,0:T(8,128)(2,1)S(1)}, u32[]{:S(2)}, u32[]{:S(2)}) collective-permute-start(bf16[64,2176]{1,0:T(8,128)(2,1)} %scaled_tokens.1.near_ref), channel_id=1, source_target_pairs={{0,2},{1,5},{2,0},{3,7},{4,6},{5,1},{6,4},{7,3},{8,10},{9,13},{10,... | collective-permute-start | bytes 835592 | tf_op jit(solution)/shard_map/ppermute | solution.py:35
  6.0 0.4 collective-permute-start.8
  6.5 10.8 %collective-permute-done.1.after_ref.near_ref = bf16[64,2176]{1,0:T(8,128)(2,1)} collective-permute-done((bf16[64,2176]{1,0:T(8,128)(2,1)}, bf16[64,2176]{1,0:T(8,128)(2,1)}, u32[]{:S(2)}, u32[]{:S(2)}) %collective-permute-start.1) | collective-permute-done | bytes 278560 | tf_op jit(solution)/shard_map/ppermute | solution.py:35
  17.3 0.7 copy-done.4
  18.1 1.0 copy-done.3
  19.0 1.0 copy-done.5
  20.0 1.3 %pick_rows.4 = (bf16[80,2176]{1,0:T(8,128)(2,1)S(1)}, bf16[80,2176]{1,0:T(8,128)(2,1)}, bf16[160,128]{1,0:T(8,128)(2,1)S(1)}) custom-call(bf16[64,2176]{1,0:T(8,128)(2,1)S(1)} %copy-done.3, bf16[64,2176]{1,0:T(8,128)(2,1)S(1)} %copy-done.5, bf16[8,128]{1,0:T(8,128)(2,1)S(1)} %convert_element_type.16.lanes_ref, ...), custom_call_target="tpu_custom_call" | custom-call | flops 1000000000 | bytes 1000000 | tf_op jit(solution)/shard_map/pick_rows/pallas_call | solution.py:119
  21.3 1.5 %collective-permute-start.3 = (bf16[80,2176]{1,0:T(8,128)(2,1)}, bf16[80,2176]{1,0:T(8,128)(2,1)}, u32[]{:S(2)}, u32[]{:S(2)}) collective-permute-start(bf16[80,2176]{1,0:T(8,128)(2,1)} %get-tuple-element.35), channel_id=1, source_target_pairs={{0,4},{1,3},{2,6},{3,1},{4,0},{5,7},{6,2},{7,5},{8,12},{9,11},{10,... | collective-permute-start | bytes 1044488 | tf_op jit(solution)/shard_map/ppermute | solution.py:35
  22.8 1.5 %collective-permute-start.5 = (bf16[64,2176]{1,0:T(8,128)(2,1)}, bf16[64,2176]{1,0:T(8,128)(2,1)}, u32[]{:S(2)}, u32[]{:S(2)}) collective-permute-start(bf16[64,2176]{1,0:T(8,128)(2,1)} %collective-permute-done.1.after_ref.near_ref), channel_id=1, source_target_pairs={{0,8},{1,9},{2,10},{3,11},{4,12},{5,13},{6,14},{7,15},{8,0},{9,1},... | collective-permute-start | bytes 835592 | tf_op jit(solution)/shard_map/ppermute | solution.py:35
  24.2 1.5 %collective-permute-start.9 = (bf16[64,2176]{1,0:T(8,128)(2,1)}, bf16[64,2176]{1,0:T(8,128)(2,1)}, u32[]{:S(2)}, u32[]{:S(2)}) collective-permute-start(bf16[64,2176]{1,0:T(8,128)(2,1)} %collective-permute-done.8.near_ref), channel_id=1, source_target_pairs={{0,2},{1,5},{2,0},{3,7},{4,6},{5,1},{6,4},{7,3},{8,10},{9,13},{10,... | collective-permute-start | bytes 835592 | tf_op jit(solution)/shard_map/ppermute | solution.py:35
  25.7 0.5 collective-permute-start.7
  26.3 4.8 %collective-permute-done.9.next_ref = bf16[64,2176]{1,0:T(8,128)(2,1)} collective-permute-done((bf16[64,2176]{1,0:T(8,128)(2,1)}, bf16[64,2176]{1,0:T(8,128)(2,1)}, u32[]{:S(2)}, u32[]{:S(2)}) %collective-permute-start.9) | collective-permute-done | bytes 278560 | tf_op jit(solution)/shard_map/ppermute | solution.py:35
  31.1 0.8 collective-permute-start.2
  31.9 1.1 %collective-permute-start.6 = (bf16[64,2176]{1,0:T(8,128)(2,1)}, bf16[64,2176]{1,0:T(8,128)(2,1)S(1)}, u32[]{:S(2)}, u32[]{:S(2)}) collective-permute-start(bf16[64,2176]{1,0:T(8,128)(2,1)} %collective-permute-done.5.near_ref), channel_id=1, source_target_pairs={{0,2},{1,5},{2,0},{3,7},{4,6},{5,1},{6,4},{7,3},{8,10},{9,13},{10,... | collective-permute-start | bytes 835592 | tf_op jit(solution)/shard_map/ppermute | solution.py:35
  33.0 0.1 collective-permute-start.4
  33.1 1.6 %pick_rows.5 = (bf16[80,2176]{1,0:T(8,128)(2,1)S(1)}, bf16[80,2176]{1,0:T(8,128)(2,1)S(1)}, bf16[160,128]{1,0:T(8,128)(2,1)S(1)}) custom-call(bf16[64,2176]{1,0:T(8,128)(2,1)} %collective-permute-done.8.near_ref, bf16[64,2176]{1,0:T(8,128)(2,1)} %collective-permute-done.9.next_ref, bf16[8,128]{1,0:T(8,128)(2,1)S(1)} %convert_element_type.16.lanes_ref, ...), custom_call_target="tpu_custom_call" | custom-call | flops 1000000000 | bytes 1000000 | tf_op jit(solution)/shard_map/pick_rows/pallas_call | solution.py:119
  34.8 1.3 %collective-permute-start.17 = (bf16[80,2176]{1,0:T(8,128)(2,1)S(1)}, bf16[80,2176]{1,0:T(8,128)(2,1)S(1)}, u32[]{:S(2)}, u32[]{:S(2)}) collective-permute-start(bf16[80,2176]{1,0:T(8,128)(2,1)S(1)} %get-tuple-element.44), channel_id=1, source_target_pairs={{0,4},{1,3},{2,6},{3,1},{4,0},{5,7},{6,2},{7,5},{8,12},{9,11},{10,... | collective-permute-start | bytes 1044488 | tf_op jit(solution)/shard_map/ppermute | solution.py:35
  36.1 1.7 %pick_rows.6 = (bf16[80,2176]{1,0:T(8,128)(2,1)S(1)}, bf16[80,2176]{1,0:T(8,128)(2,1)S(1)}, bf16[160,128]{1,0:T(8,128)(2,1)S(1)}) custom-call(bf16[64,2176]{1,0:T(8,128)(2,1)} %collective-permute-done.1.after_ref.near_ref, bf16[64,2176]{1,0:T(8,128)(2,1)S(1)} %collective-permute-done.7.next_ref, bf16[8,128]{1,0:T(8,128)(2,1)S(1)} %convert_element_type.16.lanes_ref, ...), custom_call_target="tpu_custom_call" | custom-call | flops 1000000000 | bytes 1000000 | tf_op jit(solution)/shard_map/pick_rows/pallas_call | solution.py:119
  37.8 1.6 %collective-permute-done.6.next_ref = bf16[64,2176]{1,0:T(8,128)(2,1)S(1)} collective-permute-done((bf16[64,2176]{1,0:T(8,128)(2,1)}, bf16[64,2176]{1,0:T(8,128)(2,1)S(1)}, u32[]{:S(2)}, u32[]{:S(2)}) %collective-permute-start.6) | collective-permute-done | bytes 278560 | tf_op jit(solution)/shard_map/ppermute | solution.py:35
  39.4 1.6 %collective-permute-start.14 = (bf16[80,2176]{1,0:T(8,128)(2,1)S(1)}, bf16[80,2176]{1,0:T(8,128)(2,1)S(1)}, u32[]{:S(2)}, u32[]{:S(2)}) collective-permute-start(bf16[80,2176]{1,0:T(8,128)(2,1)S(1)} %get-tuple-element.42), channel_id=1, source_target_pairs={{0,4},{1,3},{2,6},{3,1},{4,0},{5,7},{6,2},{7,5},{8,12},{9,11},{10,... | collective-permute-start | bytes 1044488 | tf_op jit(solution)/shard_map/ppermute | solution.py:35
  41.0 1.5 %pick_rows.7 = (bf16[80,2176]{1,0:T(8,128)(2,1)S(1)}, bf16[80,2176]{1,0:T(8,128)(2,1)S(1)}, bf16[160,128]{1,0:T(8,128)(2,1)S(1)}) custom-call(bf16[64,2176]{1,0:T(8,128)(2,1)} %collective-permute-done.5.near_ref, bf16[64,2176]{1,0:T(8,128)(2,1)S(1)} %collective-permute-done.6.next_ref, bf16[8,128]{1,0:T(8,128)(2,1)S(1)} %convert_element_type.16.lanes_ref, ...), custom_call_target="tpu_custom_call" | custom-call | flops 1000000000 | bytes 1000000 | tf_op jit(solution)/shard_map/pick_rows/pallas_call | solution.py:119
  42.7 2.4 %hidden_units.4.mine_ref.after_ref = bf16[160,384]{1,0:T(8,128)(2,1)S(1)} custom-call(s32[1]{0:T(128)} %bitcast.3.core_ref, bf16[80,2176]{1,0:T(8,128)(2,1)S(1)} %get-tuple-element.34.near_ref, bf16[80,2176]{1,0:T(8,128)(2,1)S(1)} %collective-permute-done.2.near_pair_ref, bf16[80,2176]{1,0:T(8,128)(2,1)} %collective-permute-done.3.far_ref, ...), custom_call_target="tpu_custom_call" | custom-call | flops 1000000000 | bytes 1000000 | tf_op jit(solution)/shard_map/hidden_units/pallas_call | solution.py:178
  45.1 0.5 collective-permute-start.10
  45.6 0.2 multiply_convert_fusion.1
  45.8 0.5 collective-permute-start.21
  46.3 0.4 collective-permute-done.14.far_ref
  46.8 0.6 collective-permute-start.13
  47.4 2.0 %routed_outputs.4 = (bf16[80,2048]{1,0:T(8,128)(2,1)S(1)}, bf16[80,2048]{1,0:T(8,128)(2,1)S(1)}) custom-call(s32[1]{0:T(128)} %bitcast.3.core_ref, bf16[160,384]{1,0:T(8,128)(2,1)S(1)} %hidden_units.4.mine_ref.after_ref, bf16[160,384]{1,0:T(8,128)(2,1)S(1)} %collective-permute-done.10.theirs_ref, bf16[256,256]{1,0:T(8,128)(2,1)S(1)} %maximum_maximum_fusion.mix_ref, ...), custom_call_target="tpu_custom_call" | custom-call | flops 1000000000 | bytes 1000000 | tf_op jit(solution)/shard_map/routed_outputs/pallas_call | solution.py:224
  49.5 1.7 %collective-permute-start.12 = (bf16[80,2048]{1,0:T(8,128)(2,1)S(1)}, bf16[80,2048]{1,0:T(8,128)(2,1)S(1)}, u32[]{:S(2)}, u32[]{:S(2)}) collective-permute-start(bf16[80,2048]{1,0:T(8,128)(2,1)S(1)} %get-tuple-element.40), channel_id=1, source_target_pairs={{0,4},{1,3},{2,6},{3,1},{4,0},{5,7},{6,2},{7,5},{8,12},{9,11},{10,... | collective-permute-start | bytes 983048 | tf_op jit(solution)/shard_map/ppermute | solution.py:35
  51.2 2.0 %collective-permute-done.21.far_ref = bf16[80,2176]{1,0:T(8,128)(2,1)S(1)} collective-permute-done((bf16[80,2176]{1,0:T(8,128)(2,1)S(1)}, bf16[80,2176]{1,0:T(8,128)(2,1)S(1)}, u32[]{:S(2)}, u32[]{:S(2)}) %collective-permute-start.21) | collective-permute-done | bytes 348192 | tf_op jit(solution)/shard_map/ppermute | solution.py:35
  53.2 0.5 collective-permute-start.22
  53.7 1.3 %hidden_units.5.after_ref.mine_ref = bf16[160,384]{1,0:T(8,128)(2,1)S(1)} custom-call(s32[1]{0:T(128)} %bitcast.3.core_ref, bf16[80,2176]{1,0:T(8,128)(2,1)S(1)} %get-tuple-element.43.near_ref, bf16[80,2176]{1,0:T(8,128)(2,1)S(1)} %collective-permute-done.16.near_pair_ref, bf16[80,2176]{1,0:T(8,128)(2,1)S(1)} %collective-permute-done.17.far_ref, ...), custom_call_target="tpu_custom_call" | custom-call | flops 1000000000 | bytes 1000000 | tf_op jit(solution)/shard_map/hidden_units/pallas_call | solution.py:178
  55.1 1.3 %hidden_units.6.after_ref.mine_ref = bf16[160,384]{1,0:T(8,128)(2,1)S(1)} custom-call(s32[1]{0:T(128)} %bitcast.3.core_ref, bf16[80,2176]{1,0:T(8,128)(2,1)S(1)} %get-tuple-element.41.near_ref, bf16[80,2176]{1,0:T(8,128)(2,1)S(1)} %collective-permute-done.13.near_pair_ref, bf16[80,2176]{1,0:T(8,128)(2,1)S(1)} %collective-permute-done.14.far_ref, ...), custom_call_target="tpu_custom_call" | custom-call | flops 1000000000 | bytes 1000000 | tf_op jit(solution)/shard_map/hidden_units/pallas_call | solution.py:178
  56.4 0.5 collective-permute-start.23
  56.9 0.3 spread_rows.4
  57.2 1.1 %collective-permute-start.19 = (bf16[64,2048]{1,0:T(8,128)(2,1)S(1)}, bf16[64,2048]{1,0:T(8,128)(2,1)S(1)}, u32[]{:S(2)}, u32[]{:S(2)}) collective-permute-start(bf16[64,2048]{1,0:T(8,128)(2,1)S(1)} %get-tuple-element.46), channel_id=1, source_target_pairs={{0,2},{1,5},{2,0},{3,7},{4,6},{5,1},{6,4},{7,3},{8,10},{9,13},{10,... | collective-permute-start | bytes 786440 | tf_op jit(solution)/shard_map/ppermute | solution.py:35
  58.3 1.1 %routed_outputs.5 = (bf16[80,2048]{1,0:T(8,128)(2,1)S(1)}, bf16[80,2048]{1,0:T(8,128)(2,1)S(1)}) custom-call(s32[1]{0:T(128)} %bitcast.3.core_ref, bf16[160,384]{1,0:T(8,128)(2,1)S(1)} %hidden_units.5.after_ref.mine_ref, bf16[160,384]{1,0:T(8,128)(2,1)S(1)} %collective-permute-done.24.theirs_ref, bf16[256,256]{1,0:T(8,128)(2,1)S(1)} %maximum_maximum_fusion.mix_ref, ...), custom_call_target="tpu_custom_call" | custom-call | flops 1000000000 | bytes 1000000 | tf_op jit(solution)/shard_map/routed_outputs/pallas_call | solution.py:224
  59.4 1.2 %collective-permute-start.25 = (bf16[80,2048]{1,0:T(8,128)(2,1)S(1)}, bf16[80,2048]{1,0:T(8,128)(2,1)S(1)}, u32[]{:S(2)}, u32[]{:S(2)}) collective-permute-start(bf16[80,2048]{1,0:T(8,128)(2,1)S(1)} %get-tuple-element.51), channel_id=1, source_target_pairs={{0,4},{1,3},{2,6},{3,1},{4,0},{5,7},{6,2},{7,5},{8,12},{9,11},{10,... | collective-permute-start | bytes 983048 | tf_op jit(solution)/shard_map/ppermute | solution.py:35
  60.6 1.1 %routed_outputs.6 = (bf16[80,2048]{1,0:T(8,128)(2,1)S(1)}, bf16[80,2048]{1,0:T(8,128)(2,1)S(1)}) custom-call(s32[1]{0:T(128)} %bitcast.3.core_ref, bf16[160,384]{1,0:T(8,128)(2,1)S(1)} %hidden_units.6.after_ref.mine_ref, bf16[160,384]{1,0:T(8,128)(2,1)S(1)} %collective-permute-done.23.theirs_ref, bf16[256,256]{1,0:T(8,128)(2,1)S(1)} %maximum_maximum_fusion.mix_ref, ...), custom_call_target="tpu_custom_call" | custom-call | flops 1000000000 | bytes 1000000 | tf_op jit(solution)/shard_map/routed_outputs/pallas_call | solution.py:224
  61.7 0.9 collective-permute-start.28
  62.6 1.3 %hidden_units.7.refs_2_.mine_ref = bf16[160,384]{1,0:T(8,128)(2,1)S(1)} custom-call(s32[1]{0:T(128)} %bitcast.3.core_ref, bf16[80,2176]{1,0:T(8,128)(2,1)S(1)} %get-tuple-element.47.near_ref, bf16[80,2176]{1,0:T(8,128)(2,1)S(1)} %collective-permute-done.20.near_pair_ref, bf16[80,2176]{1,0:T(8,128)(2,1)S(1)} %collective-permute-done.21.far_ref, ...), custom_call_target="tpu_custom_call" | custom-call | flops 1000000000 | bytes 1000000 | tf_op jit(solution)/shard_map/hidden_units/pallas_call | solution.py:178
  64.0 1.7 %collective-permute-done.19.refs_1_ = bf16[64,2048]{1,0:T(8,128)(2,1)S(1)} collective-permute-done((bf16[64,2048]{1,0:T(8,128)(2,1)S(1)}, bf16[64,2048]{1,0:T(8,128)(2,1)S(1)}, u32[]{:S(2)}, u32[]{:S(2)}) %collective-permute-start.19) | collective-permute-done | bytes 262176 | tf_op jit(solution)/shard_map/ppermute | solution.py:35
  65.8 0.8 collective-permute-done.25.back_ref
  66.5 0.3 spread_rows.5
  66.9 1.1 %collective-permute-start.26 = (bf16[64,2048]{1,0:T(8,128)(2,1)S(1)}, bf16[64,2048]{1,0:T(8,128)(2,1)S(1)}, u32[]{:S(2)}, u32[]{:S(2)}) collective-permute-start(bf16[64,2048]{1,0:T(8,128)(2,1)S(1)} %get-tuple-element.53), channel_id=1, source_target_pairs={{0,2},{1,5},{2,0},{3,7},{4,6},{5,1},{6,4},{7,3},{8,10},{9,13},{10,... | collective-permute-start | bytes 786440 | tf_op jit(solution)/shard_map/ppermute | solution.py:35
  68.0 2.1 %collective-permute-done.28.back_ref = bf16[80,2048]{1,0:T(8,128)(2,1)S(1)} collective-permute-done((bf16[80,2048]{1,0:T(8,128)(2,1)S(1)}, bf16[80,2048]{1,0:T(8,128)(2,1)S(1)}, u32[]{:S(2)}, u32[]{:S(2)}) %collective-permute-start.28) | collective-permute-done | bytes 327712 | tf_op jit(solution)/shard_map/ppermute | solution.py:35
  70.0 0.3 spread_rows.6
  70.4 1.1 %collective-permute-start.31 = (bf16[64,2048]{1,0:T(8,128)(2,1)S(1)}, bf16[64,2048]{1,0:T(8,128)(2,1)S(1)}, u32[]{:S(2)}, u32[]{:S(2)}) collective-permute-start(bf16[64,2048]{1,0:T(8,128)(2,1)S(1)} %get-tuple-element.58), channel_id=1, source_target_pairs={{0,2},{1,5},{2,0},{3,7},{4,6},{5,1},{6,4},{7,3},{8,10},{9,13},{10,... | collective-permute-start | bytes 786440 | tf_op jit(solution)/shard_map/ppermute | solution.py:35
  71.5 1.1 %routed_outputs.7 = (bf16[80,2048]{1,0:T(8,128)(2,1)S(1)}, bf16[80,2048]{1,0:T(8,128)(2,1)S(1)}) custom-call(s32[1]{0:T(128)} %bitcast.3.core_ref, bf16[160,384]{1,0:T(8,128)(2,1)S(1)} %hidden_units.7.refs_2_.mine_ref, bf16[160,384]{1,0:T(8,128)(2,1)S(1)} %collective-permute-done.27.theirs_ref, bf16[256,256]{1,0:T(8,128)(2,1)S(1)} %maximum_maximum_fusion.mix_ref, ...), custom_call_target="tpu_custom_call" | custom-call | flops 1000000000 | bytes 1000000 | tf_op jit(solution)/shard_map/routed_outputs/pallas_call | solution.py:224
  72.6 1.4 %collective-permute-start.30 = (bf16[80,2048]{1,0:T(8,128)(2,1)S(1)}, bf16[80,2048]{1,0:T(8,128)(2,1)S(1)}, u32[]{:S(2)}, u32[]{:S(2)}) collective-permute-start(bf16[80,2048]{1,0:T(8,128)(2,1)S(1)} %get-tuple-element.57), channel_id=1, source_target_pairs={{0,4},{1,3},{2,6},{3,1},{4,0},{5,7},{6,2},{7,5},{8,12},{9,11},{10,... | collective-permute-start | bytes 983048 | tf_op jit(solution)/shard_map/ppermute | solution.py:35
  74.0 3.2 %collective-permute-done.31.refs_1_ = bf16[64,2048]{1,0:T(8,128)(2,1)S(1)} collective-permute-done((bf16[64,2048]{1,0:T(8,128)(2,1)S(1)}, bf16[64,2048]{1,0:T(8,128)(2,1)S(1)}, u32[]{:S(2)}, u32[]{:S(2)}) %collective-permute-start.31) | collective-permute-done | bytes 262176 | tf_op jit(solution)/shard_map/ppermute | solution.py:35
  77.3 1.1 %collective-permute-start.33 = (bf16[64,2048]{1,0:T(8,128)(2,1)S(1)}, bf16[64,2048]{1,0:T(8,128)(2,1)S(1)}, u32[]{:S(2)}, u32[]{:S(2)}) collective-permute-start(bf16[64,2048]{1,0:T(8,128)(2,1)S(1)} %add_rows.8.after_ref), channel_id=1, source_target_pairs={{0,8},{1,9},{2,10},{3,11},{4,12},{5,13},{6,14},{7,15},{8,0},{9,1},... | collective-permute-start | bytes 786440 | tf_op jit(solution)/shard_map/ppermute | solution.py:35
  78.4 1.8 %collective-permute-done.30.back_ref = bf16[80,2048]{1,0:T(8,128)(2,1)S(1)} collective-permute-done((bf16[80,2048]{1,0:T(8,128)(2,1)S(1)}, bf16[80,2048]{1,0:T(8,128)(2,1)S(1)}, u32[]{:S(2)}, u32[]{:S(2)}) %collective-permute-start.30) | collective-permute-done | bytes 327712 | tf_op jit(solution)/shard_map/ppermute | solution.py:35
  80.3 0.3 spread_rows.7
  80.6 1.0 collective-permute-start.32
  81.6 1.2 %collective-permute-start.29 = (bf16[64,2048]{1,0:T(8,128)(2,1)S(1)}, bf16[64,2048]{1,0:T(8,128)(2,1)S(1)}, u32[]{:S(2)}, u32[]{:S(2)}) collective-permute-start(bf16[64,2048]{1,0:T(8,128)(2,1)S(1)} %add_rows.7.refs_2_), channel_id=1, source_target_pairs={{0,8},{1,9},{2,10},{3,11},{4,12},{5,13},{6,14},{7,15},{8,0},{9,1},... | collective-permute-start | bytes 786440 | tf_op jit(solution)/shard_map/ppermute | solution.py:35
  82.8 3.7 %collective-permute-done.33.refs_2_ = bf16[64,2048]{1,0:T(8,128)(2,1)S(1)} collective-permute-done((bf16[64,2048]{1,0:T(8,128)(2,1)S(1)}, bf16[64,2048]{1,0:T(8,128)(2,1)S(1)}, u32[]{:S(2)}, u32[]{:S(2)}) %collective-permute-start.33) | collective-permute-done | bytes 262176 | tf_op jit(solution)/shard_map/ppermute | solution.py:35
  86.5 0.5 collective-permute-done.32.refs_1_
  87.1 2.2 %collective-permute-start.34 = (bf16[64,2048]{1,0:T(8,128)(2,1)S(1)}, bf16[64,2048]{1,0:T(8,128)(2,1)S(1)}, u32[]{:S(2)}, u32[]{:S(2)}) collective-permute-start(bf16[64,2048]{1,0:T(8,128)(2,1)S(1)} %add_rows.9.refs_2_), channel_id=1, source_target_pairs={{0,24},{1,25},{2,26},{3,27},{4,28},{5,29},{6,30},{7,31},{8,16},{9,... | collective-permute-start | bytes 786440 | tf_op jit(solution)/shard_map/ppermute | solution.py:35
  89.3 2.7 %collective-permute-done.29.refs_1_ = bf16[64,2048]{1,0:T(8,128)(2,1)S(1)} collective-permute-done((bf16[64,2048]{1,0:T(8,128)(2,1)S(1)}, bf16[64,2048]{1,0:T(8,128)(2,1)S(1)}, u32[]{:S(2)}, u32[]{:S(2)}) %collective-permute-start.29) | collective-permute-done | bytes 262176 | tf_op jit(solution)/shard_map/ppermute | solution.py:35
  92.1 8.6 %collective-permute-done.34.refs_1_ = bf16[64,2048]{1,0:T(8,128)(2,1)S(1)} collective-permute-done((bf16[64,2048]{1,0:T(8,128)(2,1)S(1)}, bf16[64,2048]{1,0:T(8,128)(2,1)S(1)}, u32[]{:S(2)}, u32[]{:S(2)}) %collective-permute-start.34) | collective-permute-done | bytes 262176 | tf_op jit(solution)/shard_map/ppermute | solution.py:35
  100.7 0.7 add_rows.11
  (52 shorter events, 0.8 us)
Async XLA Ops:
  0.0 47.3 %collective-permute-start.11 = (bf16[384,4096]{1,0:T(8,128)(2,1)}, bf16[384,4096]{1,0:T(8,128)(2,1)S(1)}, u32[]{:S(2)}, u32[]{:S(2)}) collective-permute-start(bf16[384,4096]{1,0:T(8,128)(2,1)} %bitcast.7), channel_id=1, source_target_pairs={{0,1},{1,0},{2,3},{3,2},{4,5},{5,4},{6,7},{7,6},{8,9},{9,8},{10,11... | collective-permute-start | bytes 9437192 | tf_op jit(solution)/shard_map/ppermute | solution.py:35
  1.9 15.4 %collective-permute-start.1 = (bf16[64,2176]{1,0:T(8,128)(2,1)}, bf16[64,2176]{1,0:T(8,128)(2,1)}, u32[]{:S(2)}, u32[]{:S(2)}) collective-permute-start(bf16[64,2176]{1,0:T(8,128)(2,1)} %scaled_tokens.1.near_ref), channel_id=1, source_target_pairs={{0,16},{1,17},{2,18},{3,19},{4,20},{5,21},{6,22},{7,23},{8,24},{9,... | collective-permute-start | bytes 835592 | tf_op jit(solution)/shard_map/ppermute | solution.py:35
  4.5 12.8 %collective-permute-start = (bf16[64,2176]{1,0:T(8,128)(2,1)}, bf16[64,2176]{1,0:T(8,128)(2,1)S(1)}, u32[]{:S(2)}, u32[]{:S(2)}) collective-permute-start(bf16[64,2176]{1,0:T(8,128)(2,1)} %scaled_tokens.1.near_ref), channel_id=1, source_target_pairs={{0,2},{1,5},{2,0},{3,7},{4,6},{5,1},{6,4},{7,3},{8,10},{9,13},{10,... | collective-permute-start | bytes 835592 | tf_op jit(solution)/shard_map/ppermute | solution.py:35
  6.0 18.2 %collective-permute-start.8 = (bf16[64,2176]{1,0:T(8,128)(2,1)}, bf16[64,2176]{1,0:T(8,128)(2,1)}, u32[]{:S(2)}, u32[]{:S(2)}) collective-permute-start(bf16[64,2176]{1,0:T(8,128)(2,1)} %scaled_tokens.1.near_ref), channel_id=1, source_target_pairs={{0,8},{1,9},{2,10},{3,11},{4,12},{5,13},{6,14},{7,15},{8,0},{9,1},... | collective-permute-start | bytes 835592 | tf_op jit(solution)/shard_map/ppermute | solution.py:35
  17.3 0.7 copy-start.4
  18.1 1.0 copy-start.3
  19.0 1.0 copy-start.5
  21.3 11.7 %collective-permute-start.3 = (bf16[80,2176]{1,0:T(8,128)(2,1)}, bf16[80,2176]{1,0:T(8,128)(2,1)}, u32[]{:S(2)}, u32[]{:S(2)}) collective-permute-start(bf16[80,2176]{1,0:T(8,128)(2,1)} %get-tuple-element.35), channel_id=1, source_target_pairs={{0,4},{1,3},{2,6},{3,1},{4,0},{5,7},{6,2},{7,5},{8,12},{9,11},{10,... | collective-permute-start | bytes 1044488 | tf_op jit(solution)/shard_map/ppermute | solution.py:35
  22.8 9.1 %collective-permute-start.5 = (bf16[64,2176]{1,0:T(8,128)(2,1)}, bf16[64,2176]{1,0:T(8,128)(2,1)}, u32[]{:S(2)}, u32[]{:S(2)}) collective-permute-start(bf16[64,2176]{1,0:T(8,128)(2,1)} %collective-permute-done.1.after_ref.near_ref), channel_id=1, source_target_pairs={{0,8},{1,9},{2,10},{3,11},{4,12},{5,13},{6,14},{7,15},{8,0},{9,1},... | collective-permute-start | bytes 835592 | tf_op jit(solution)/shard_map/ppermute | solution.py:35
  24.2 6.9 %collective-permute-start.9 = (bf16[64,2176]{1,0:T(8,128)(2,1)}, bf16[64,2176]{1,0:T(8,128)(2,1)}, u32[]{:S(2)}, u32[]{:S(2)}) collective-permute-start(bf16[64,2176]{1,0:T(8,128)(2,1)} %collective-permute-done.8.near_ref), channel_id=1, source_target_pairs={{0,2},{1,5},{2,0},{3,7},{4,6},{5,1},{6,4},{7,3},{8,10},{9,13},{10,... | collective-permute-start | bytes 835592 | tf_op jit(solution)/shard_map/ppermute | solution.py:35
  25.7 9.0 %collective-permute-start.7 = (bf16[64,2176]{1,0:T(8,128)(2,1)}, bf16[64,2176]{1,0:T(8,128)(2,1)S(1)}, u32[]{:S(2)}, u32[]{:S(2)}) collective-permute-start(bf16[64,2176]{1,0:T(8,128)(2,1)} %collective-permute-done.1.after_ref.near_ref), channel_id=1, source_target_pairs={{0,2},{1,5},{2,0},{3,7},{4,6},{5,1},{6,4},{7,3},{8,10},{9,13},{10,... | collective-permute-start | bytes 835592 | tf_op jit(solution)/shard_map/ppermute | solution.py:35
  31.1 11.5 %collective-permute-start.2 = (bf16[80,2176]{1,0:T(8,128)(2,1)S(1)}, bf16[80,2176]{1,0:T(8,128)(2,1)S(1)}, u32[]{:S(2)}, u32[]{:S(2)}) collective-permute-start(bf16[80,2176]{1,0:T(8,128)(2,1)S(1)} %get-tuple-element.34.near_ref), channel_id=1, source_target_pairs={{0,1},{1,0},{2,3},{3,2},{4,5},{5,4},{6,7},{7,6},{8,9},{9,8},{10,11... | collective-permute-start | bytes 1044488 | tf_op jit(solution)/shard_map/ppermute | solution.py:35
  31.9 7.5 %collective-permute-start.6 = (bf16[64,2176]{1,0:T(8,128)(2,1)}, bf16[64,2176]{1,0:T(8,128)(2,1)S(1)}, u32[]{:S(2)}, u32[]{:S(2)}) collective-permute-start(bf16[64,2176]{1,0:T(8,128)(2,1)} %collective-permute-done.5.near_ref), channel_id=1, source_target_pairs={{0,2},{1,5},{2,0},{3,7},{4,6},{5,1},{6,4},{7,3},{8,10},{9,13},{10,... | collective-permute-start | bytes 835592 | tf_op jit(solution)/shard_map/ppermute | solution.py:35
  33.0 9.7 %collective-permute-start.4 = (bf16[80,2176]{1,0:T(8,128)(2,1)}, bf16[80,2176]{1,0:T(8,128)(2,1)S(1)}, u32[]{:S(2)}, u32[]{:S(2)}) collective-permute-start(bf16[80,2176]{1,0:T(8,128)(2,1)} %collective-permute-done.3.far_ref), channel_id=1, source_target_pairs={{0,1},{1,0},{2,3},{3,2},{4,5},{5,4},{6,7},{7,6},{8,9},{9,8},{10,11... | collective-permute-start | bytes 1044488 | tf_op jit(solution)/shard_map/ppermute | solution.py:35
  34.8 11.1 %collective-permute-start.17 = (bf16[80,2176]{1,0:T(8,128)(2,1)S(1)}, bf16[80,2176]{1,0:T(8,128)(2,1)S(1)}, u32[]{:S(2)}, u32[]{:S(2)}) collective-permute-start(bf16[80,2176]{1,0:T(8,128)(2,1)S(1)} %get-tuple-element.44), channel_id=1, source_target_pairs={{0,4},{1,3},{2,6},{3,1},{4,0},{5,7},{6,2},{7,5},{8,12},{9,11},{10,... | collective-permute-start | bytes 1044488 | tf_op jit(solution)/shard_map/ppermute | solution.py:35
  36.1 6.6 %copy-start.1 = (bf16[1,4096,384]{2,1,0:T(8,128)(2,1)S(1)}, bf16[1,4096,384]{2,1,0:T(8,128)(2,1)}, u32[]{:S(2)}) copy-start(bf16[1,4096,384]{2,1,0:T(8,128)(2,1)} %param.11) | copy-start | bytes 9437188
  36.1 6.6 %copy-start.2 = (bf16[1,4096,384]{2,1,0:T(8,128)(2,1)S(1)}, bf16[1,4096,384]{2,1,0:T(8,128)(2,1)}, u32[]{:S(2)}) copy-start(bf16[1,4096,384]{2,1,0:T(8,128)(2,1)} %param.12) | copy-start | bytes 9437188
  39.4 7.3 %collective-permute-start.14 = (bf16[80,2176]{1,0:T(8,128)(2,1)S(1)}, bf16[80,2176]{1,0:T(8,128)(2,1)S(1)}, u32[]{:S(2)}, u32[]{:S(2)}) collective-permute-start(bf16[80,2176]{1,0:T(8,128)(2,1)S(1)} %get-tuple-element.42), channel_id=1, source_target_pairs={{0,4},{1,3},{2,6},{3,1},{4,0},{5,7},{6,2},{7,5},{8,12},{9,11},{10,... | collective-permute-start | bytes 1044488 | tf_op jit(solution)/shard_map/ppermute | solution.py:35
  42.6 6.9 %collective-permute-start.16 = (bf16[80,2176]{1,0:T(8,128)(2,1)S(1)}, bf16[80,2176]{1,0:T(8,128)(2,1)S(1)}, u32[]{:S(2)}, u32[]{:S(2)}) collective-permute-start(bf16[80,2176]{1,0:T(8,128)(2,1)S(1)} %get-tuple-element.43.near_ref), channel_id=1, source_target_pairs={{0,1},{1,0},{2,3},{3,2},{4,5},{5,4},{6,7},{7,6},{8,9},{9,8},{10,11... | collective-permute-start | bytes 1044488 | tf_op jit(solution)/shard_map/ppermute | solution.py:35
  42.7 4.7 %copy-start = (bf16[1,384,4096]{2,1,0:T(8,128)(2,1)S(1)}, bf16[1,384,4096]{2,1,0:T(8,128)(2,1)}, u32[]{:S(2)}) copy-start(bf16[1,384,4096]{2,1,0:T(8,128)(2,1)} %param.13) | copy-start | bytes 9437188
  45.1 1.7 %collective-permute-start.10 = (bf16[160,384]{1,0:T(8,128)(2,1)S(1)}, bf16[160,384]{1,0:T(8,128)(2,1)S(1)}, u32[]{:S(2)}, u32[]{:S(2)}) collective-permute-start(bf16[160,384]{1,0:T(8,128)(2,1)S(1)} %hidden_units.4.mine_ref.after_ref), channel_id=1, source_target_pairs={{0,1},{1,0},{2,3},{3,2},{4,5},{5,4},{6,7},{7,6},{8,9},{9,8},{10,11... | collective-permute-start | bytes 368648 | tf_op jit(solution)/shard_map/ppermute | solution.py:35
  45.8 7.4 %collective-permute-start.21 = (bf16[80,2176]{1,0:T(8,128)(2,1)S(1)}, bf16[80,2176]{1,0:T(8,128)(2,1)S(1)}, u32[]{:S(2)}, u32[]{:S(2)}) collective-permute-start(bf16[80,2176]{1,0:T(8,128)(2,1)S(1)} %get-tuple-element.48), channel_id=1, source_target_pairs={{0,4},{1,3},{2,6},{3,1},{4,0},{5,7},{6,2},{7,5},{8,12},{9,11},{10,... | collective-permute-start | bytes 1044488 | tf_op jit(solution)/shard_map/ppermute | solution.py:35
  46.7 6.5 %collective-permute-start.18 = (bf16[80,2176]{1,0:T(8,128)(2,1)S(1)}, bf16[80,2176]{1,0:T(8,128)(2,1)S(1)}, u32[]{:S(2)}, u32[]{:S(2)}) collective-permute-start(bf16[80,2176]{1,0:T(8,128)(2,1)S(1)} %collective-permute-done.17.far_ref), channel_id=1, source_target_pairs={{0,1},{1,0},{2,3},{3,2},{4,5},{5,4},{6,7},{7,6},{8,9},{9,8},{10,11... | collective-permute-start | bytes 1044488 | tf_op jit(solution)/shard_map/ppermute | solution.py:35
  46.8 8.3 %collective-permute-start.13 = (bf16[80,2176]{1,0:T(8,128)(2,1)S(1)}, bf16[80,2176]{1,0:T(8,128)(2,1)S(1)}, u32[]{:S(2)}, u32[]{:S(2)}) collective-permute-start(bf16[80,2176]{1,0:T(8,128)(2,1)S(1)} %get-tuple-element.41.near_ref), channel_id=1, source_target_pairs={{0,1},{1,0},{2,3},{3,2},{4,5},{5,4},{6,7},{7,6},{8,9},{9,8},{10,11... | collective-permute-start | bytes 1044488 | tf_op jit(solution)/shard_map/ppermute | solution.py:35
  47.3 7.8 %collective-permute-start.15 = (bf16[80,2176]{1,0:T(8,128)(2,1)S(1)}, bf16[80,2176]{1,0:T(8,128)(2,1)S(1)}, u32[]{:S(2)}, u32[]{:S(2)}) collective-permute-start(bf16[80,2176]{1,0:T(8,128)(2,1)S(1)} %collective-permute-done.14.far_ref), channel_id=1, source_target_pairs={{0,1},{1,0},{2,3},{3,2},{4,5},{5,4},{6,7},{7,6},{8,9},{9,8},{10,11... | collective-permute-start | bytes 1044488 | tf_op jit(solution)/shard_map/ppermute | solution.py:35
  49.5 7.4 %collective-permute-start.12 = (bf16[80,2048]{1,0:T(8,128)(2,1)S(1)}, bf16[80,2048]{1,0:T(8,128)(2,1)S(1)}, u32[]{:S(2)}, u32[]{:S(2)}) collective-permute-start(bf16[80,2048]{1,0:T(8,128)(2,1)S(1)} %get-tuple-element.40), channel_id=1, source_target_pairs={{0,4},{1,3},{2,6},{3,1},{4,0},{5,7},{6,2},{7,5},{8,12},{9,11},{10,... | collective-permute-start | bytes 983048 | tf_op jit(solution)/shard_map/ppermute | solution.py:35
  53.2 9.4 %collective-permute-start.20 = (bf16[80,2176]{1,0:T(8,128)(2,1)S(1)}, bf16[80,2176]{1,0:T(8,128)(2,1)S(1)}, u32[]{:S(2)}, u32[]{:S(2)}) collective-permute-start(bf16[80,2176]{1,0:T(8,128)(2,1)S(1)} %get-tuple-element.47.near_ref), channel_id=1, source_target_pairs={{0,1},{1,0},{2,3},{3,2},{4,5},{5,4},{6,7},{7,6},{8,9},{9,8},{10,11... | collective-permute-start | bytes 1044488 | tf_op jit(solution)/shard_map/ppermute | solution.py:35
  53.2 9.4 %collective-permute-start.22 = (bf16[80,2176]{1,0:T(8,128)(2,1)S(1)}, bf16[80,2176]{1,0:T(8,128)(2,1)S(1)}, u32[]{:S(2)}, u32[]{:S(2)}) collective-permute-start(bf16[80,2176]{1,0:T(8,128)(2,1)S(1)} %collective-permute-done.21.far_ref), channel_id=1, source_target_pairs={{0,1},{1,0},{2,3},{3,2},{4,5},{5,4},{6,7},{7,6},{8,9},{9,8},{10,11... | collective-permute-start | bytes 1044488 | tf_op jit(solution)/shard_map/ppermute | solution.py:35
  55.0 3.3 %collective-permute-start.24 = (bf16[160,384]{1,0:T(8,128)(2,1)S(1)}, bf16[160,384]{1,0:T(8,128)(2,1)S(1)}, u32[]{:S(2)}, u32[]{:S(2)}) collective-permute-start(bf16[160,384]{1,0:T(8,128)(2,1)S(1)} %hidden_units.5.after_ref.mine_ref), channel_id=1, source_target_pairs={{0,1},{1,0},{2,3},{3,2},{4,5},{5,4},{6,7},{7,6},{8,9},{9,8},{10,11... | collective-permute-start | bytes 368648 | tf_op jit(solution)/shard_map/ppermute | solution.py:35
  56.4 4.3 %collective-permute-start.23 = (bf16[160,384]{1,0:T(8,128)(2,1)S(1)}, bf16[160,384]{1,0:T(8,128)(2,1)S(1)}, u32[]{:S(2)}, u32[]{:S(2)}) collective-permute-start(bf16[160,384]{1,0:T(8,128)(2,1)S(1)} %hidden_units.6.after_ref.mine_ref), channel_id=1, source_target_pairs={{0,1},{1,0},{2,3},{3,2},{4,5},{5,4},{6,7},{7,6},{8,9},{9,8},{10,11... | collective-permute-start | bytes 368648 | tf_op jit(solution)/shard_map/ppermute | solution.py:35
  57.2 8.5 %collective-permute-start.19 = (bf16[64,2048]{1,0:T(8,128)(2,1)S(1)}, bf16[64,2048]{1,0:T(8,128)(2,1)S(1)}, u32[]{:S(2)}, u32[]{:S(2)}) collective-permute-start(bf16[64,2048]{1,0:T(8,128)(2,1)S(1)} %get-tuple-element.46), channel_id=1, source_target_pairs={{0,2},{1,5},{2,0},{3,7},{4,6},{5,1},{6,4},{7,3},{8,10},{9,13},{10,... | collective-permute-start | bytes 786440 | tf_op jit(solution)/shard_map/ppermute | solution.py:35
  59.4 7.1 %collective-permute-start.25 = (bf16[80,2048]{1,0:T(8,128)(2,1)S(1)}, bf16[80,2048]{1,0:T(8,128)(2,1)S(1)}, u32[]{:S(2)}, u32[]{:S(2)}) collective-permute-start(bf16[80,2048]{1,0:T(8,128)(2,1)S(1)} %get-tuple-element.51), channel_id=1, source_target_pairs={{0,4},{1,3},{2,6},{3,1},{4,0},{5,7},{6,2},{7,5},{8,12},{9,11},{10,... | collective-permute-start | bytes 983048 | tf_op jit(solution)/shard_map/ppermute | solution.py:35
  61.7 8.3 %collective-permute-start.28 = (bf16[80,2048]{1,0:T(8,128)(2,1)S(1)}, bf16[80,2048]{1,0:T(8,128)(2,1)S(1)}, u32[]{:S(2)}, u32[]{:S(2)}) collective-permute-start(bf16[80,2048]{1,0:T(8,128)(2,1)S(1)} %get-tuple-element.54), channel_id=1, source_target_pairs={{0,4},{1,3},{2,6},{3,1},{4,0},{5,7},{6,2},{7,5},{8,12},{9,11},{10,... | collective-permute-start | bytes 983048 | tf_op jit(solution)/shard_map/ppermute | solution.py:35
  63.9 7.6 %collective-permute-start.27 = (bf16[160,384]{1,0:T(8,128)(2,1)S(1)}, bf16[160,384]{1,0:T(8,128)(2,1)S(1)}, u32[]{:S(2)}, u32[]{:S(2)}) collective-permute-start(bf16[160,384]{1,0:T(8,128)(2,1)S(1)} %hidden_units.7.refs_2_.mine_ref), channel_id=1, source_target_pairs={{0,1},{1,0},{2,3},{3,2},{4,5},{5,4},{6,7},{7,6},{8,9},{9,8},{10,11... | collective-permute-start | bytes 368648 | tf_op jit(solution)/shard_map/ppermute | solution.py:35
  66.9 7.1 %collective-permute-start.26 = (bf16[64,2048]{1,0:T(8,128)(2,1)S(1)}, bf16[64,2048]{1,0:T(8,128)(2,1)S(1)}, u32[]{:S(2)}, u32[]{:S(2)}) collective-permute-start(bf16[64,2048]{1,0:T(8,128)(2,1)S(1)} %get-tuple-element.53), channel_id=1, source_target_pairs={{0,2},{1,5},{2,0},{3,7},{4,6},{5,1},{6,4},{7,3},{8,10},{9,13},{10,... | collective-permute-start | bytes 786440 | tf_op jit(solution)/shard_map/ppermute | solution.py:35
  70.4 6.9 %collective-permute-start.31 = (bf16[64,2048]{1,0:T(8,128)(2,1)S(1)}, bf16[64,2048]{1,0:T(8,128)(2,1)S(1)}, u32[]{:S(2)}, u32[]{:S(2)}) collective-permute-start(bf16[64,2048]{1,0:T(8,128)(2,1)S(1)} %get-tuple-element.58), channel_id=1, source_target_pairs={{0,2},{1,5},{2,0},{3,7},{4,6},{5,1},{6,4},{7,3},{8,10},{9,13},{10,... | collective-permute-start | bytes 786440 | tf_op jit(solution)/shard_map/ppermute | solution.py:35
  72.6 7.7 %collective-permute-start.30 = (bf16[80,2048]{1,0:T(8,128)(2,1)S(1)}, bf16[80,2048]{1,0:T(8,128)(2,1)S(1)}, u32[]{:S(2)}, u32[]{:S(2)}) collective-permute-start(bf16[80,2048]{1,0:T(8,128)(2,1)S(1)} %get-tuple-element.57), channel_id=1, source_target_pairs={{0,4},{1,3},{2,6},{3,1},{4,0},{5,7},{6,2},{7,5},{8,12},{9,11},{10,... | collective-permute-start | bytes 983048 | tf_op jit(solution)/shard_map/ppermute | solution.py:35
  77.3 9.2 %collective-permute-start.33 = (bf16[64,2048]{1,0:T(8,128)(2,1)S(1)}, bf16[64,2048]{1,0:T(8,128)(2,1)S(1)}, u32[]{:S(2)}, u32[]{:S(2)}) collective-permute-start(bf16[64,2048]{1,0:T(8,128)(2,1)S(1)} %add_rows.8.after_ref), channel_id=1, source_target_pairs={{0,8},{1,9},{2,10},{3,11},{4,12},{5,13},{6,14},{7,15},{8,0},{9,1},... | collective-permute-start | bytes 786440 | tf_op jit(solution)/shard_map/ppermute | solution.py:35
  80.6 6.4 %collective-permute-start.32 = (bf16[64,2048]{1,0:T(8,128)(2,1)S(1)}, bf16[64,2048]{1,0:T(8,128)(2,1)S(1)}, u32[]{:S(2)}, u32[]{:S(2)}) collective-permute-start(bf16[64,2048]{1,0:T(8,128)(2,1)S(1)} %get-tuple-element.60), channel_id=1, source_target_pairs={{0,2},{1,5},{2,0},{3,7},{4,6},{5,1},{6,4},{7,3},{8,10},{9,13},{10,... | collective-permute-start | bytes 786440 | tf_op jit(solution)/shard_map/ppermute | solution.py:35
  81.6 10.4 %collective-permute-start.29 = (bf16[64,2048]{1,0:T(8,128)(2,1)S(1)}, bf16[64,2048]{1,0:T(8,128)(2,1)S(1)}, u32[]{:S(2)}, u32[]{:S(2)}) collective-permute-start(bf16[64,2048]{1,0:T(8,128)(2,1)S(1)} %add_rows.7.refs_2_), channel_id=1, source_target_pairs={{0,8},{1,9},{2,10},{3,11},{4,12},{5,13},{6,14},{7,15},{8,0},{9,1},... | collective-permute-start | bytes 786440 | tf_op jit(solution)/shard_map/ppermute | solution.py:35
  87.1 13.6 %collective-permute-start.34 = (bf16[64,2048]{1,0:T(8,128)(2,1)S(1)}, bf16[64,2048]{1,0:T(8,128)(2,1)S(1)}, u32[]{:S(2)}, u32[]{:S(2)}) collective-permute-start(bf16[64,2048]{1,0:T(8,128)(2,1)S(1)} %add_rows.9.refs_2_), channel_id=1, source_target_pairs={{0,24},{1,25},{2,26},{3,27},{4,28},{5,29},{6,30},{7,31},{8,16},{9,... | collective-permute-start | bytes 786440 | tf_op jit(solution)/shard_map/ppermute | solution.py:35

commit v3 on v2

--- a/solution.py
+++ b/solution.py
@@ -10,6 +10,15 @@
 
 WALSH = 128
 LANES = 128
+ORDER = (
+    (0, 1, 2, 3),
+    (4, 6, 7, 8),
+    (5, 10, 9, 11),
+    (12, 14, 13, 15),
+    (19, 17, 16, 18),
+    (19.1, 20, 16.1, 21),
+)
+HEAVY, LIGHT = 2 * 10**9, 10**7
 VMEM_BYTES = 8 << 20
 
 
@@ -35,8 +44,8 @@
     return lax.ppermute(array, ("expert", "tensor"), pairs)
 
 
-def cost():
-    return pl.CostEstimate(flops=10**9, bytes_accessed=10**6, transcendentals=0)
+def cost(flops=HEAVY):
+    return pl.CostEstimate(flops=flops, bytes_accessed=10**6, transcendentals=0)
 
 
 def scaled_tokens(values, scales, ids, route_weights, experts):
@@ -279,7 +288,7 @@
         in_specs=[vmem] * len(parts) + [pl.BlockSpec(memory_space=pl.ANY)],
         out_shape=jax.ShapeDtypeStruct(parts[0].shape, kind),
         compiler_params=pltpu.CompilerParams(vmem_limit_bytes=VMEM_BYTES),
-        cost_estimate=cost(),
+        cost_estimate=cost(LIGHT),
         name="add_rows",
     )(*parts, after)
 
@@ -325,7 +334,7 @@
     )
 
     state = [dict() for _ in range(line)]
-    last = blocks[-2]
+    last = named
     total = None
 
     def pick(k):
@@ -384,18 +393,14 @@
             kind = jnp.bfloat16 if k == line - 1 else jnp.float32
             total = last = add_rows([total, state[k]["sent"]], kind, last)
 
-    near_round = lambda k: (0, 1, 1, 2)[min(k, 3)] + max(0, k - 3)
-    stages = (
-        (settle, lambda k: 6 + near_round(k)),
-        (absorb, lambda k: 7 + near_round(k)),
-        (spread, lambda k: 5 + near_round(k)),
-        (contract_units, lambda k: 4 + near_round(k)),
-        (expand_units, lambda k: 3 + near_round(k)),
-        (pick, lambda k: 1 + near_round(k) - (k > 2) / 2),
-    )
-    due = [(when(k), name, k) for k in range(line) for name, (_, when) in enumerate(stages)]
+    steps = (pick, expand_units, contract_units, spread, settle, absorb)
+    due = [
+        (times[min(k, 3)] + 10 * max(0, k - 3), name, k)
+        for name, times in enumerate(ORDER)
+        for k in range(line)
+    ]
     for _, name, k in sorted(due):
-        stages[name][0](k)
+        steps[name](k)
     return total
 
 

time: 102 us -> 97.7 us (0.958)
  waiting for transfers between devices: 45 us -> 49.9 us
  starting transfers between devices: 31.4 us -> 27.2 us
  Pallas kernels: 21.8 us -> 17.9 us
  local copies, waits for them, and re-layouts: 2.69 us -> 1.01 us
    ppermute x35, waiting for transfers between devices: 45 us -> 49.9 us  [swap(): return lax.ppermute(array, ('expert', 'tensor'), pairs)]
    ppermute x35, starting transfers between devices: 31.4 us -> 27.2 us  [swap(): return lax.ppermute(array, ('expert', 'tensor'), pairs)]
    pallas_call x4, Pallas kernels: 6.16 us -> 4.25 us  [pick_rows(): pl.pallas_call(kernel, in_specs=[vmem, vmem, vmem, pl.BlockSpec(memory_sp...]
    unnamed x12 -> x8, local copies, waits for them, and re-layouts: 2.65 us -> 0.97 us
  transfers between devices with their start and end apart: 35 -> 35, of which waited for: 14 -> 17; matrix products, arithmetic and copies ran while one was open for 0% -> 0% of each run, Pallas kernels for 21% -> 18%
where the time goes in v3:
time: 97.7 us; the launch traced here: 96.6 us
  waiting for transfers between devices  49.9 us (51%)
  starting transfers between devices  27.2 us (28%)
  Pallas kernels  17.9 us (18%)
  local copies, waits for them, and re-layouts  1.01 us (1%)
    ppermute x35, waiting for transfers between devices, swap(): return lax.ppermute(array, ('expert', 'tensor'), pairs)  49.9 us
    ppermute x35, starting transfers between devices, swap(): return lax.ppermute(array, ('expert', 'tensor'), pairs)  27.2 us
    pallas_call x4, Pallas kernels, hidden_units(): pl.pallas_call(kernel, in_specs=[pl.BlockSpec(memory_space=pltpu.SMEM)] +...  5.15 us
    pallas_call x4, Pallas kernels, routed_outputs(): pl.pallas_call(kernel, in_specs=[pl.BlockSpec(memory_space=pltpu.SMEM)] +...  4.3 us
    pallas_call x4, Pallas kernels, pick_rows(): pl.pallas_call(kernel, in_specs=[vmem, vmem, vmem, pl.BlockSpec(memory_sp...  4.25 us
  transfers between devices with their start and end apart: 35, of which 17 were waited for; matrix products, arithmetic and copies ran while one was open for 0% of the time, Pallas kernels for 18%

profile of v3, /device:TPU:8, one launch (start us, length us, event | category | flops | bytes accessed | tf_op | source)
XLA Modules:
  0.0 96.6 jit_solution(14342737997662476061)
XLA Ops:
  0.0 1.9 %scaled_tokens.1.near_ref = bf16[64,2176]{1,0:T(8,128)(2,1)} custom-call(bf16[64,2048]{1,0:T(8,128)(2,1)} %values_ref.1, bf16[16,64]{1,0:T(8,128)(2,1)} %bitcast.20, s32[8,64]{1,0:T(8,128)} %bitcast.21, s32[8,64]{1,0:T(8,128)} %bitcast.22), custom_call_target="tpu_custom_call" | custom-call | flops 2000000000 | bytes 1000000 | tf_op jit(solution)/shard_map/scaled_tokens/pallas_call | solution.py:87
  1.9 1.5 %collective-permute-start = (bf16[64,2176]{1,0:T(8,128)(2,1)}, bf16[64,2176]{1,0:T(8,128)(2,1)}, u32[]{:S(2)}, u32[]{:S(2)}) collective-permute-start(bf16[64,2176]{1,0:T(8,128)(2,1)} %scaled_tokens.1.near_ref), channel_id=1, source_target_pairs={{0,2},{1,5},{2,0},{3,7},{4,6},{5,1},{6,4},{7,3},{8,10},{9,13},{10,... | collective-permute-start | bytes 835592 | tf_op jit(solution)/shard_map/ppermute | solution.py:44
  3.4 0.4 collective-permute-start.8
  3.9 2.6 %collective-permute-start.4 = (bf16[64,2176]{1,0:T(8,128)(2,1)}, bf16[64,2176]{1,0:T(8,128)(2,1)S(1)}, u32[]{:S(2)}, u32[]{:S(2)}) collective-permute-start(bf16[64,2176]{1,0:T(8,128)(2,1)} %scaled_tokens.1.near_ref), channel_id=1, source_target_pairs={{0,16},{1,17},{2,18},{3,19},{4,20},{5,21},{6,22},{7,23},{8,24},{9,... | collective-permute-start | bytes 835592 | tf_op jit(solution)/shard_map/ppermute | solution.py:44
  6.6 9.8 %collective-permute-done.8.near_ref = bf16[64,2176]{1,0:T(8,128)(2,1)} collective-permute-done((bf16[64,2176]{1,0:T(8,128)(2,1)}, bf16[64,2176]{1,0:T(8,128)(2,1)}, u32[]{:S(2)}, u32[]{:S(2)}) %collective-permute-start.8) | collective-permute-done | bytes 278560 | tf_op jit(solution)/shard_map/ppermute | solution.py:44
  16.4 3.2 %collective-permute-done.4.near_ref = bf16[64,2176]{1,0:T(8,128)(2,1)S(1)} collective-permute-done((bf16[64,2176]{1,0:T(8,128)(2,1)}, bf16[64,2176]{1,0:T(8,128)(2,1)S(1)}, u32[]{:S(2)}, u32[]{:S(2)}) %collective-permute-start.4) | collective-permute-done | bytes 278560 | tf_op jit(solution)/shard_map/ppermute | solution.py:44
  19.5 1.6 %collective-permute-start.5 = (bf16[64,2176]{1,0:T(8,128)(2,1)S(1)}, bf16[64,2176]{1,0:T(8,128)(2,1)S(1)}, u32[]{:S(2)}, u32[]{:S(2)}) collective-permute-start(bf16[64,2176]{1,0:T(8,128)(2,1)S(1)} %collective-permute-done.4.near_ref), channel_id=1, source_target_pairs={{0,8},{1,9},{2,10},{3,11},{4,12},{5,13},{6,14},{7,15},{8,0},{9,1},... | collective-permute-start | bytes 835592 | tf_op jit(solution)/shard_map/ppermute | solution.py:44
  21.1 1.0 copy-done.3
  22.1 1.5 %pick_rows.4 = (bf16[80,2176]{1,0:T(8,128)(2,1)S(1)}, bf16[80,2176]{1,0:T(8,128)(2,1)S(1)}, bf16[160,128]{1,0:T(8,128)(2,1)S(1)}) custom-call(bf16[64,2176]{1,0:T(8,128)(2,1)S(1)} %copy-done.3, bf16[64,2176]{1,0:T(8,128)(2,1)} %collective-permute-done.next_ref, bf16[8,128]{1,0:T(8,128)(2,1)S(1)} %convert_element_type.16.lanes_ref.after_ref, ...), custom_call_target="tpu_custom_call" | custom-call | flops 2000000000 | bytes 1000000 | tf_op jit(solution)/shard_map/pick_rows/pallas_call | solution.py:128
  23.6 0.6 collective-permute-start.2
  24.2 1.5 %collective-permute-start.7 = (bf16[64,2176]{1,0:T(8,128)(2,1)S(1)}, bf16[64,2176]{1,0:T(8,128)(2,1)S(1)}, u32[]{:S(2)}, u32[]{:S(2)}) collective-permute-start(bf16[64,2176]{1,0:T(8,128)(2,1)S(1)} %collective-permute-done.4.near_ref), channel_id=1, source_target_pairs={{0,2},{1,5},{2,0},{3,7},{4,6},{5,1},{6,4},{7,3},{8,10},{9,13},{10,... | collective-permute-start | bytes 835592 | tf_op jit(solution)/shard_map/ppermute | solution.py:44
  25.7 0.2 multiply_convert_fusion.1
  26.0 1.5 %collective-permute-done.5.near_ref = bf16[64,2176]{1,0:T(8,128)(2,1)S(1)} collective-permute-done((bf16[64,2176]{1,0:T(8,128)(2,1)S(1)}, bf16[64,2176]{1,0:T(8,128)(2,1)S(1)}, u32[]{:S(2)}, u32[]{:S(2)}) %collective-permute-start.5) | collective-permute-done | bytes 278560 | tf_op jit(solution)/shard_map/ppermute | solution.py:44
  27.5 2.0 %collective-permute-start.6 = (bf16[64,2176]{1,0:T(8,128)(2,1)S(1)}, bf16[64,2176]{1,0:T(8,128)(2,1)S(1)}, u32[]{:S(2)}, u32[]{:S(2)}) collective-permute-start(bf16[64,2176]{1,0:T(8,128)(2,1)S(1)} %collective-permute-done.5.near_ref), channel_id=1, source_target_pairs={{0,2},{1,5},{2,0},{3,7},{4,6},{5,1},{6,4},{7,3},{8,10},{9,13},{10,... | collective-permute-start | bytes 835592 | tf_op jit(solution)/shard_map/ppermute | solution.py:44
  29.5 1.5 %pick_rows.5 = (bf16[80,2176]{1,0:T(8,128)(2,1)S(1)}, bf16[80,2176]{1,0:T(8,128)(2,1)S(1)}, bf16[160,128]{1,0:T(8,128)(2,1)S(1)}) custom-call(bf16[64,2176]{1,0:T(8,128)(2,1)} %collective-permute-done.8.near_ref, bf16[64,2176]{1,0:T(8,128)(2,1)S(1)} %collective-permute-done.9.next_ref, bf16[8,128]{1,0:T(8,128)(2,1)S(1)} %convert_element_type.16.lanes_ref.after_ref, ...), custom_call_target="tpu_custom_call" | custom-call | flops 2000000000 | bytes 1000000 | tf_op jit(solution)/shard_map/pick_rows/pallas_call | solution.py:128
  31.1 1.5 %collective-permute-done.7.next_ref = bf16[64,2176]{1,0:T(8,128)(2,1)S(1)} collective-permute-done((bf16[64,2176]{1,0:T(8,128)(2,1)S(1)}, bf16[64,2176]{1,0:T(8,128)(2,1)S(1)}, u32[]{:S(2)}, u32[]{:S(2)}) %collective-permute-start.7) | collective-permute-done | bytes 278560 | tf_op jit(solution)/shard_map/ppermute | solution.py:44
  32.6 2.1 %collective-permute-done.2.far_ref = bf16[80,2176]{1,0:T(8,128)(2,1)S(1)} collective-permute-done((bf16[80,2176]{1,0:T(8,128)(2,1)S(1)}, bf16[80,2176]{1,0:T(8,128)(2,1)S(1)}, u32[]{:S(2)}, u32[]{:S(2)}) %collective-permute-start.2) | collective-permute-done | bytes 348192 | tf_op jit(solution)/shard_map/ppermute | solution.py:44
  34.7 0.6 pick_rows.6
  35.3 0.5 collective-permute-done.6.next_ref
  35.8 0.1 collective-permute-start.17
  35.9 0.6 pick_rows.7
  36.5 2.0 %collective-permute-start.19 = (bf16[80,2176]{1,0:T(8,128)(2,1)S(1)}, bf16[80,2176]{1,0:T(8,128)(2,1)S(1)}, u32[]{:S(2)}, u32[]{:S(2)}) collective-permute-start(bf16[80,2176]{1,0:T(8,128)(2,1)S(1)} %get-tuple-element.45.near_ref), channel_id=1, source_target_pairs={{0,1},{1,0},{2,3},{3,2},{4,5},{5,4},{6,7},{7,6},{8,9},{9,8},{10,11... | collective-permute-start | bytes 1044488 | tf_op jit(solution)/shard_map/ppermute | solution.py:44
  38.5 2.2 %collective-permute-done.20.far_ref = bf16[80,2176]{1,0:T(8,128)(2,1)S(1)} collective-permute-done((bf16[80,2176]{1,0:T(8,128)(2,1)S(1)}, bf16[80,2176]{1,0:T(8,128)(2,1)S(1)}, u32[]{:S(2)}, u32[]{:S(2)}) %collective-permute-start.20) | collective-permute-done | bytes 348192 | tf_op jit(solution)/shard_map/ppermute | solution.py:44
  40.7 0.3 collective-permute-start.14
  41.1 1.3 %hidden_units.4.mine_ref.after_ref = bf16[160,384]{1,0:T(8,128)(2,1)S(1)} custom-call(s32[1]{0:T(128)} %bitcast.3.core_ref, bf16[80,2176]{1,0:T(8,128)(2,1)S(1)} %get-tuple-element.34.near_ref, bf16[80,2176]{1,0:T(8,128)(2,1)S(1)} %collective-permute-done.1.near_pair_ref, bf16[80,2176]{1,0:T(8,128)(2,1)S(1)} %collective-permute-done.2.far_ref, ...), custom_call_target="tpu_custom_call" | custom-call | flops 2000000000 | bytes 1000000 | tf_op jit(solution)/shard_map/hidden_units/pallas_call | solution.py:187
  42.4 2.1 %collective-permute-done.17.far_ref = bf16[80,2176]{1,0:T(8,128)(2,1)S(1)} collective-permute-done((bf16[80,2176]{1,0:T(8,128)(2,1)S(1)}, bf16[80,2176]{1,0:T(8,128)(2,1)S(1)}, u32[]{:S(2)}, u32[]{:S(2)}) %collective-permute-start.17) | collective-permute-done | bytes 348192 | tf_op jit(solution)/shard_map/ppermute | solution.py:44
  44.5 1.3 %collective-permute-done.10.theirs_ref = bf16[160,384]{1,0:T(8,128)(2,1)S(1)} collective-permute-done((bf16[160,384]{1,0:T(8,128)(2,1)S(1)}, bf16[160,384]{1,0:T(8,128)(2,1)S(1)}, u32[]{:S(2)}, u32[]{:S(2)}) %collective-permute-start.10) | collective-permute-done | bytes 122912 | tf_op jit(solution)/shard_map/ppermute | solution.py:44
  45.8 0.1 collective-permute-start.16
  45.9 0.4 collective-permute-start.18
  46.3 1.1 %routed_outputs.4 = (bf16[80,2048]{1,0:T(8,128)(2,1)S(1)}, bf16[80,2048]{1,0:T(8,128)(2,1)S(1)}) custom-call(s32[1]{0:T(128)} %bitcast.3.core_ref, bf16[160,384]{1,0:T(8,128)(2,1)S(1)} %hidden_units.4.mine_ref.after_ref, bf16[160,384]{1,0:T(8,128)(2,1)S(1)} %collective-permute-done.10.theirs_ref, bf16[256,256]{1,0:T(8,128)(2,1)S(1)} %maximum_maximum_fusion.mix_ref, ...), custom_call_target="tpu_custom_call" | custom-call | flops 2000000000 | bytes 1000000 | tf_op jit(solution)/shard_map/routed_outputs/pallas_call | solution.py:233
  47.4 0.2 collective-permute-start.13
  47.6 0.6 collective-permute-done.14.far_ref
  48.2 1.3 %hidden_units.5.after_ref.mine_ref = bf16[160,384]{1,0:T(8,128)(2,1)S(1)} custom-call(s32[1]{0:T(128)} %bitcast.3.core_ref, bf16[80,2176]{1,0:T(8,128)(2,1)S(1)} %get-tuple-element.45.near_ref, bf16[80,2176]{1,0:T(8,128)(2,1)S(1)} %collective-permute-done.19.near_pair_ref, bf16[80,2176]{1,0:T(8,128)(2,1)S(1)} %collective-permute-done.20.far_ref, ...), custom_call_target="tpu_custom_call" | custom-call | flops 2000000000 | bytes 1000000 | tf_op jit(solution)/shard_map/hidden_units/pallas_call | solution.py:187
  49.5 0.6 collective-permute-start.23
  50.0 1.3 %hidden_units.6.after_ref.mine_ref = bf16[160,384]{1,0:T(8,128)(2,1)S(1)} custom-call(s32[1]{0:T(128)} %bitcast.3.core_ref, bf16[80,2176]{1,0:T(8,128)(2,1)S(1)} %get-tuple-element.43.near_ref, bf16[80,2176]{1,0:T(8,128)(2,1)S(1)} %collective-permute-done.16.near_pair_ref, bf16[80,2176]{1,0:T(8,128)(2,1)S(1)} %collective-permute-done.17.far_ref, ...), custom_call_target="tpu_custom_call" | custom-call | flops 2000000000 | bytes 1000000 | tf_op jit(solution)/shard_map/hidden_units/pallas_call | solution.py:187
  51.4 0.1 collective-permute-start.24
  51.5 1.3 %hidden_units.7.after_ref.mine_ref = bf16[160,384]{1,0:T(8,128)(2,1)S(1)} custom-call(s32[1]{0:T(128)} %bitcast.3.core_ref, bf16[80,2176]{1,0:T(8,128)(2,1)S(1)} %get-tuple-element.41.near_ref, bf16[80,2176]{1,0:T(8,128)(2,1)S(1)} %collective-permute-done.13.near_pair_ref, bf16[80,2176]{1,0:T(8,128)(2,1)S(1)} %collective-permute-done.14.far_ref, ...), custom_call_target="tpu_custom_call" | custom-call | flops 2000000000 | bytes 1000000 | tf_op jit(solution)/shard_map/hidden_units/pallas_call | solution.py:187
  52.8 0.5 collective-permute-start.22
  53.3 0.3 collective-permute-start.12
  53.6 1.1 %routed_outputs.5 = (bf16[80,2048]{1,0:T(8,128)(2,1)S(1)}, bf16[80,2048]{1,0:T(8,128)(2,1)S(1)}) custom-call(s32[1]{0:T(128)} %bitcast.3.core_ref, bf16[160,384]{1,0:T(8,128)(2,1)S(1)} %hidden_units.6.after_ref.mine_ref, bf16[160,384]{1,0:T(8,128)(2,1)S(1)} %collective-permute-done.24.theirs_ref, bf16[256,256]{1,0:T(8,128)(2,1)S(1)} %maximum_maximum_fusion.mix_ref, ...), custom_call_target="tpu_custom_call" | custom-call | flops 2000000000 | bytes 1000000 | tf_op jit(solution)/shard_map/routed_outputs/pallas_call | solution.py:233
  54.7 1.8 %collective-permute-start.28 = (bf16[80,2048]{1,0:T(8,128)(2,1)S(1)}, bf16[80,2048]{1,0:T(8,128)(2,1)S(1)}, u32[]{:S(2)}, u32[]{:S(2)}) collective-permute-start(bf16[80,2048]{1,0:T(8,128)(2,1)S(1)} %get-tuple-element.54), channel_id=1, source_target_pairs={{0,4},{1,3},{2,6},{3,1},{4,0},{5,7},{6,2},{7,5},{8,12},{9,11},{10,... | collective-permute-start | bytes 983048 | tf_op jit(solution)/shard_map/ppermute | solution.py:44
  56.5 1.1 %routed_outputs.6 = (bf16[80,2048]{1,0:T(8,128)(2,1)S(1)}, bf16[80,2048]{1,0:T(8,128)(2,1)S(1)}) custom-call(s32[1]{0:T(128)} %bitcast.3.core_ref, bf16[160,384]{1,0:T(8,128)(2,1)S(1)} %hidden_units.5.after_ref.mine_ref, bf16[160,384]{1,0:T(8,128)(2,1)S(1)} %collective-permute-done.23.theirs_ref, bf16[256,256]{1,0:T(8,128)(2,1)S(1)} %maximum_maximum_fusion.mix_ref, ...), custom_call_target="tpu_custom_call" | custom-call | flops 2000000000 | bytes 1000000 | tf_op jit(solution)/shard_map/routed_outputs/pallas_call | solution.py:233
  57.6 0.4 collective-permute-start.27
  58.0 1.1 %routed_outputs.7 = (bf16[80,2048]{1,0:T(8,128)(2,1)S(1)}, bf16[80,2048]{1,0:T(8,128)(2,1)S(1)}) custom-call(s32[1]{0:T(128)} %bitcast.3.core_ref, bf16[160,384]{1,0:T(8,128)(2,1)S(1)} %hidden_units.7.after_ref.mine_ref, bf16[160,384]{1,0:T(8,128)(2,1)S(1)} %collective-permute-done.22.theirs_ref, bf16[256,256]{1,0:T(8,128)(2,1)S(1)} %maximum_maximum_fusion.mix_ref, ...), custom_call_target="tpu_custom_call" | custom-call | flops 2000000000 | bytes 1000000 | tf_op jit(solution)/shard_map/routed_outputs/pallas_call | solution.py:233
  59.0 1.8 %collective-permute-start.26 = (bf16[80,2048]{1,0:T(8,128)(2,1)S(1)}, bf16[80,2048]{1,0:T(8,128)(2,1)S(1)}, u32[]{:S(2)}, u32[]{:S(2)}) collective-permute-start(bf16[80,2048]{1,0:T(8,128)(2,1)S(1)} %get-tuple-element.52), channel_id=1, source_target_pairs={{0,4},{1,3},{2,6},{3,1},{4,0},{5,7},{6,2},{7,5},{8,12},{9,11},{10,... | collective-permute-start | bytes 983048 | tf_op jit(solution)/shard_map/ppermute | solution.py:44
  60.8 0.3 spread_rows.4
  61.1 2.7 %collective-permute-done.28.back_ref = bf16[80,2048]{1,0:T(8,128)(2,1)S(1)} collective-permute-done((bf16[80,2048]{1,0:T(8,128)(2,1)S(1)}, bf16[80,2048]{1,0:T(8,128)(2,1)S(1)}, u32[]{:S(2)}, u32[]{:S(2)}) %collective-permute-start.28) | collective-permute-done | bytes 327712 | tf_op jit(solution)/shard_map/ppermute | solution.py:44
  63.9 0.3 spread_rows.5
  64.2 1.2 %collective-permute-start.30 = (bf16[64,2048]{1,0:T(8,128)(2,1)S(1)}, bf16[64,2048]{1,0:T(8,128)(2,1)S(1)}, u32[]{:S(2)}, u32[]{:S(2)}) collective-permute-start(bf16[64,2048]{1,0:T(8,128)(2,1)S(1)} %get-tuple-element.59), channel_id=1, source_target_pairs={{0,2},{1,5},{2,0},{3,7},{4,6},{5,1},{6,4},{7,3},{8,10},{9,13},{10,... | collective-permute-start | bytes 786440 | tf_op jit(solution)/shard_map/ppermute | solution.py:44
  65.4 3.2 %collective-permute-done.27.back_ref = bf16[80,2048]{1,0:T(8,128)(2,1)S(1)} collective-permute-done((bf16[80,2048]{1,0:T(8,128)(2,1)S(1)}, bf16[80,2048]{1,0:T(8,128)(2,1)S(1)}, u32[]{:S(2)}, u32[]{:S(2)}) %collective-permute-start.27) | collective-permute-done | bytes 327712 | tf_op jit(solution)/shard_map/ppermute | solution.py:44
  68.6 0.3 spread_rows.6
  68.9 1.2 %collective-permute-start.32 = (bf16[64,2048]{1,0:T(8,128)(2,1)S(1)}, bf16[64,2048]{1,0:T(8,128)(2,1)S(1)}, u32[]{:S(2)}, u32[]{:S(2)}) collective-permute-start(bf16[64,2048]{1,0:T(8,128)(2,1)S(1)} %get-tuple-element.60), channel_id=1, source_target_pairs={{0,2},{1,5},{2,0},{3,7},{4,6},{5,1},{6,4},{7,3},{8,10},{9,13},{10,... | collective-permute-start | bytes 786440 | tf_op jit(solution)/shard_map/ppermute | solution.py:44
  70.1 5.5 %collective-permute-done.26.back_ref = bf16[80,2048]{1,0:T(8,128)(2,1)S(1)} collective-permute-done((bf16[80,2048]{1,0:T(8,128)(2,1)S(1)}, bf16[80,2048]{1,0:T(8,128)(2,1)S(1)}, u32[]{:S(2)}, u32[]{:S(2)}) %collective-permute-start.26) | collective-permute-done | bytes 327712 | tf_op jit(solution)/shard_map/ppermute | solution.py:44
  75.6 0.3 spread_rows.7
  76.0 1.2 %collective-permute-start.29 = (bf16[64,2048]{1,0:T(8,128)(2,1)S(1)}, bf16[64,2048]{1,0:T(8,128)(2,1)S(1)}, u32[]{:S(2)}, u32[]{:S(2)}) collective-permute-start(bf16[64,2048]{1,0:T(8,128)(2,1)S(1)} %get-tuple-element.58), channel_id=1, source_target_pairs={{0,2},{1,5},{2,0},{3,7},{4,6},{5,1},{6,4},{7,3},{8,10},{9,13},{10,... | collective-permute-start | bytes 786440 | tf_op jit(solution)/shard_map/ppermute | solution.py:44
  77.2 0.9 collective-permute-start.31
  78.1 0.4 collective-permute-start.25
  78.6 1.8 %collective-permute-start.33 = (bf16[64,2048]{1,0:T(8,128)(2,1)S(1)}, bf16[64,2048]{1,0:T(8,128)(2,1)S(1)}, u32[]{:S(2)}, u32[]{:S(2)}) collective-permute-start(bf16[64,2048]{1,0:T(8,128)(2,1)S(1)} %add_rows.7.refs_3_), channel_id=1, source_target_pairs={{0,8},{1,9},{2,10},{3,11},{4,12},{5,13},{6,14},{7,15},{8,0},{9,1},... | collective-permute-start | bytes 786440 | tf_op jit(solution)/shard_map/ppermute | solution.py:44
  80.3 2.1 %collective-permute-done.29.refs_1_ = bf16[64,2048]{1,0:T(8,128)(2,1)S(1)} collective-permute-done((bf16[64,2048]{1,0:T(8,128)(2,1)S(1)}, bf16[64,2048]{1,0:T(8,128)(2,1)S(1)}, u32[]{:S(2)}, u32[]{:S(2)}) %collective-permute-start.29) | collective-permute-done | bytes 262176 | tf_op jit(solution)/shard_map/ppermute | solution.py:44
  82.4 4.1 %collective-permute-done.31.refs_2_ = bf16[64,2048]{1,0:T(8,128)(2,1)S(1)} collective-permute-done((bf16[64,2048]{1,0:T(8,128)(2,1)S(1)}, bf16[64,2048]{1,0:T(8,128)(2,1)S(1)}, u32[]{:S(2)}, u32[]{:S(2)}) %collective-permute-start.31) | collective-permute-done | bytes 262176 | tf_op jit(solution)/shard_map/ppermute | solution.py:44
  86.6 1.6 %collective-permute-start.34 = (bf16[64,2048]{1,0:T(8,128)(2,1)S(1)}, bf16[64,2048]{1,0:T(8,128)(2,1)S(1)}, u32[]{:S(2)}, u32[]{:S(2)}) collective-permute-start(bf16[64,2048]{1,0:T(8,128)(2,1)S(1)} %add_rows.8.refs_2_), channel_id=1, source_target_pairs={{0,24},{1,25},{2,26},{3,27},{4,28},{5,29},{6,30},{7,31},{8,16},{9,... | collective-permute-start | bytes 786440 | tf_op jit(solution)/shard_map/ppermute | solution.py:44
  88.3 2.0 %collective-permute-done.33.refs_1_ = bf16[64,2048]{1,0:T(8,128)(2,1)S(1)} collective-permute-done((bf16[64,2048]{1,0:T(8,128)(2,1)S(1)}, bf16[64,2048]{1,0:T(8,128)(2,1)S(1)}, u32[]{:S(2)}, u32[]{:S(2)}) %collective-permute-start.33) | collective-permute-done | bytes 262176 | tf_op jit(solution)/shard_map/ppermute | solution.py:44
  90.3 5.5 %collective-permute-done.34.refs_1_ = bf16[64,2048]{1,0:T(8,128)(2,1)S(1)} collective-permute-done((bf16[64,2048]{1,0:T(8,128)(2,1)S(1)}, bf16[64,2048]{1,0:T(8,128)(2,1)S(1)}, u32[]{:S(2)}, u32[]{:S(2)}) %collective-permute-start.34) | collective-permute-done | bytes 262176 | tf_op jit(solution)/shard_map/ppermute | solution.py:44
  95.8 0.7 add_rows.11
  (48 shorter events, 0.5 us)
Async XLA Ops:
  0.0 45.9 %collective-permute-start.11 = (bf16[384,4096]{1,0:T(8,128)(2,1)}, bf16[384,4096]{1,0:T(8,128)(2,1)S(1)}, u32[]{:S(2)}, u32[]{:S(2)}) collective-permute-start(bf16[384,4096]{1,0:T(8,128)(2,1)} %bitcast.7), channel_id=1, source_target_pairs={{0,1},{1,0},{2,3},{3,2},{4,5},{5,4},{6,7},{7,6},{8,9},{9,8},{10,11... | collective-permute-start | bytes 9437192 | tf_op jit(solution)/shard_map/ppermute | solution.py:44
  1.9 19.2 %collective-permute-start = (bf16[64,2176]{1,0:T(8,128)(2,1)}, bf16[64,2176]{1,0:T(8,128)(2,1)}, u32[]{:S(2)}, u32[]{:S(2)}) collective-permute-start(bf16[64,2176]{1,0:T(8,128)(2,1)} %scaled_tokens.1.near_ref), channel_id=1, source_target_pairs={{0,2},{1,5},{2,0},{3,7},{4,6},{5,1},{6,4},{7,3},{8,10},{9,13},{10,... | collective-permute-start | bytes 835592 | tf_op jit(solution)/shard_map/ppermute | solution.py:44
  3.4 12.9 %collective-permute-start.8 = (bf16[64,2176]{1,0:T(8,128)(2,1)}, bf16[64,2176]{1,0:T(8,128)(2,1)}, u32[]{:S(2)}, u32[]{:S(2)}) collective-permute-start(bf16[64,2176]{1,0:T(8,128)(2,1)} %scaled_tokens.1.near_ref), channel_id=1, source_target_pairs={{0,8},{1,9},{2,10},{3,11},{4,12},{5,13},{6,14},{7,15},{8,0},{9,1},... | collective-permute-start | bytes 835592 | tf_op jit(solution)/shard_map/ppermute | solution.py:44
  3.9 15.7 %collective-permute-start.4 = (bf16[64,2176]{1,0:T(8,128)(2,1)}, bf16[64,2176]{1,0:T(8,128)(2,1)S(1)}, u32[]{:S(2)}, u32[]{:S(2)}) collective-permute-start(bf16[64,2176]{1,0:T(8,128)(2,1)} %scaled_tokens.1.near_ref), channel_id=1, source_target_pairs={{0,16},{1,17},{2,18},{3,19},{4,20},{5,21},{6,22},{7,23},{8,24},{9,... | collective-permute-start | bytes 835592 | tf_op jit(solution)/shard_map/ppermute | solution.py:44
  16.4 9.6 %collective-permute-start.9 = (bf16[64,2176]{1,0:T(8,128)(2,1)}, bf16[64,2176]{1,0:T(8,128)(2,1)S(1)}, u32[]{:S(2)}, u32[]{:S(2)}) collective-permute-start(bf16[64,2176]{1,0:T(8,128)(2,1)} %collective-permute-done.8.near_ref), channel_id=1, source_target_pairs={{0,2},{1,5},{2,0},{3,7},{4,6},{5,1},{6,4},{7,3},{8,10},{9,13},{10,... | collective-permute-start | bytes 835592 | tf_op jit(solution)/shard_map/ppermute | solution.py:44
  19.5 8.0 %collective-permute-start.5 = (bf16[64,2176]{1,0:T(8,128)(2,1)S(1)}, bf16[64,2176]{1,0:T(8,128)(2,1)S(1)}, u32[]{:S(2)}, u32[]{:S(2)}) collective-permute-start(bf16[64,2176]{1,0:T(8,128)(2,1)S(1)} %collective-permute-done.4.near_ref), channel_id=1, source_target_pairs={{0,8},{1,9},{2,10},{3,11},{4,12},{5,13},{6,14},{7,15},{8,0},{9,1},... | collective-permute-start | bytes 835592 | tf_op jit(solution)/shard_map/ppermute | solution.py:44
  21.1 1.0 copy-start.3
  23.6 11.0 %collective-permute-start.2 = (bf16[80,2176]{1,0:T(8,128)(2,1)S(1)}, bf16[80,2176]{1,0:T(8,128)(2,1)S(1)}, u32[]{:S(2)}, u32[]{:S(2)}) collective-permute-start(bf16[80,2176]{1,0:T(8,128)(2,1)S(1)} %get-tuple-element.35), channel_id=1, source_target_pairs={{0,4},{1,3},{2,6},{3,1},{4,0},{5,7},{6,2},{7,5},{8,12},{9,11},{10,... | collective-permute-start | bytes 1044488 | tf_op jit(solution)/shard_map/ppermute | solution.py:44
  24.2 8.4 %collective-permute-start.7 = (bf16[64,2176]{1,0:T(8,128)(2,1)S(1)}, bf16[64,2176]{1,0:T(8,128)(2,1)S(1)}, u32[]{:S(2)}, u32[]{:S(2)}) collective-permute-start(bf16[64,2176]{1,0:T(8,128)(2,1)S(1)} %collective-permute-done.4.near_ref), channel_id=1, source_target_pairs={{0,2},{1,5},{2,0},{3,7},{4,6},{5,1},{6,4},{7,3},{8,10},{9,13},{10,... | collective-permute-start | bytes 835592 | tf_op jit(solution)/shard_map/ppermute | solution.py:44
  25.9 10.6 %collective-permute-start.1 = (bf16[80,2176]{1,0:T(8,128)(2,1)S(1)}, bf16[80,2176]{1,0:T(8,128)(2,1)S(1)}, u32[]{:S(2)}, u32[]{:S(2)}) collective-permute-start(bf16[80,2176]{1,0:T(8,128)(2,1)S(1)} %get-tuple-element.34.near_ref), channel_id=1, source_target_pairs={{0,1},{1,0},{2,3},{3,2},{4,5},{5,4},{6,7},{7,6},{8,9},{9,8},{10,11... | collective-permute-start | bytes 1044488 | tf_op jit(solution)/shard_map/ppermute | solution.py:44
  27.5 8.3 %collective-permute-start.6 = (bf16[64,2176]{1,0:T(8,128)(2,1)S(1)}, bf16[64,2176]{1,0:T(8,128)(2,1)S(1)}, u32[]{:S(2)}, u32[]{:S(2)}) collective-permute-start(bf16[64,2176]{1,0:T(8,128)(2,1)S(1)} %collective-permute-done.5.near_ref), channel_id=1, source_target_pairs={{0,2},{1,5},{2,0},{3,7},{4,6},{5,1},{6,4},{7,3},{8,10},{9,13},{10,... | collective-permute-start | bytes 835592 | tf_op jit(solution)/shard_map/ppermute | solution.py:44
  32.6 8.1 %collective-permute-start.20 = (bf16[80,2176]{1,0:T(8,128)(2,1)S(1)}, bf16[80,2176]{1,0:T(8,128)(2,1)S(1)}, u32[]{:S(2)}, u32[]{:S(2)}) collective-permute-start(bf16[80,2176]{1,0:T(8,128)(2,1)S(1)} %get-tuple-element.46), channel_id=1, source_target_pairs={{0,4},{1,3},{2,6},{3,1},{4,0},{5,7},{6,2},{7,5},{8,12},{9,11},{10,... | collective-permute-start | bytes 1044488 | tf_op jit(solution)/shard_map/ppermute | solution.py:44
  34.7 6.4 %collective-permute-start.3 = (bf16[80,2176]{1,0:T(8,128)(2,1)S(1)}, bf16[80,2176]{1,0:T(8,128)(2,1)S(1)}, u32[]{:S(2)}, u32[]{:S(2)}) collective-permute-start(bf16[80,2176]{1,0:T(8,128)(2,1)S(1)} %collective-permute-done.2.far_ref), channel_id=1, source_target_pairs={{0,1},{1,0},{2,3},{3,2},{4,5},{5,4},{6,7},{7,6},{8,9},{9,8},{10,11... | collective-permute-start | bytes 1044488 | tf_op jit(solution)/shard_map/ppermute | solution.py:44
  35.8 8.7 %collective-permute-start.17 = (bf16[80,2176]{1,0:T(8,128)(2,1)S(1)}, bf16[80,2176]{1,0:T(8,128)(2,1)S(1)}, u32[]{:S(2)}, u32[]{:S(2)}) collective-permute-start(bf16[80,2176]{1,0:T(8,128)(2,1)S(1)} %get-tuple-element.44), channel_id=1, source_target_pairs={{0,4},{1,3},{2,6},{3,1},{4,0},{5,7},{6,2},{7,5},{8,12},{9,11},{10,... | collective-permute-start | bytes 1044488 | tf_op jit(solution)/shard_map/ppermute | solution.py:44
  35.9 5.1 %copy-start.1 = (bf16[1,4096,384]{2,1,0:T(8,128)(2,1)S(1)}, bf16[1,4096,384]{2,1,0:T(8,128)(2,1)}, u32[]{:S(2)}) copy-start(bf16[1,4096,384]{2,1,0:T(8,128)(2,1)} %param.11) | copy-start | bytes 9437188
  35.9 5.1 %copy-start.2 = (bf16[1,4096,384]{2,1,0:T(8,128)(2,1)S(1)}, bf16[1,4096,384]{2,1,0:T(8,128)(2,1)}, u32[]{:S(2)}) copy-start(bf16[1,4096,384]{2,1,0:T(8,128)(2,1)} %param.12) | copy-start | bytes 9437188
  36.5 10.8 %collective-permute-start.19 = (bf16[80,2176]{1,0:T(8,128)(2,1)S(1)}, bf16[80,2176]{1,0:T(8,128)(2,1)S(1)}, u32[]{:S(2)}, u32[]{:S(2)}) collective-permute-start(bf16[80,2176]{1,0:T(8,128)(2,1)S(1)} %get-tuple-element.45.near_ref), channel_id=1, source_target_pairs={{0,1},{1,0},{2,3},{3,2},{4,5},{5,4},{6,7},{7,6},{8,9},{9,8},{10,11... | collective-permute-start | bytes 1044488 | tf_op jit(solution)/shard_map/ppermute | solution.py:44
  40.7 7.5 %collective-permute-start.14 = (bf16[80,2176]{1,0:T(8,128)(2,1)S(1)}, bf16[80,2176]{1,0:T(8,128)(2,1)S(1)}, u32[]{:S(2)}, u32[]{:S(2)}) collective-permute-start(bf16[80,2176]{1,0:T(8,128)(2,1)S(1)} %get-tuple-element.42), channel_id=1, source_target_pairs={{0,4},{1,3},{2,6},{3,1},{4,0},{5,7},{6,2},{7,5},{8,12},{9,11},{10,... | collective-permute-start | bytes 1044488 | tf_op jit(solution)/shard_map/ppermute | solution.py:44
  41.0 7.1 %collective-permute-start.21 = (bf16[80,2176]{1,0:T(8,128)(2,1)S(1)}, bf16[80,2176]{1,0:T(8,128)(2,1)S(1)}, u32[]{:S(2)}, u32[]{:S(2)}) collective-permute-start(bf16[80,2176]{1,0:T(8,128)(2,1)S(1)} %collective-permute-done.20.far_ref), channel_id=1, source_target_pairs={{0,1},{1,0},{2,3},{3,2},{4,5},{5,4},{6,7},{7,6},{8,9},{9,8},{10,11... | collective-permute-start | bytes 1044488 | tf_op jit(solution)/shard_map/ppermute | solution.py:44
  41.1 5.2 %copy-start = (bf16[1,384,4096]{2,1,0:T(8,128)(2,1)S(1)}, bf16[1,384,4096]{2,1,0:T(8,128)(2,1)}, u32[]{:S(2)}) copy-start(bf16[1,384,4096]{2,1,0:T(8,128)(2,1)} %param.13) | copy-start | bytes 9437188
  44.4 1.3 %collective-permute-start.10 = (bf16[160,384]{1,0:T(8,128)(2,1)S(1)}, bf16[160,384]{1,0:T(8,128)(2,1)S(1)}, u32[]{:S(2)}, u32[]{:S(2)}) collective-permute-start(bf16[160,384]{1,0:T(8,128)(2,1)S(1)} %hidden_units.4.mine_ref.after_ref), channel_id=1, source_target_pairs={{0,1},{1,0},{2,3},{3,2},{4,5},{5,4},{6,7},{7,6},{8,9},{9,8},{10,11... | collective-permute-start | bytes 368648 | tf_op jit(solution)/shard_map/ppermute | solution.py:44
  45.8 4.3 %collective-permute-start.16 = (bf16[80,2176]{1,0:T(8,128)(2,1)S(1)}, bf16[80,2176]{1,0:T(8,128)(2,1)S(1)}, u32[]{:S(2)}, u32[]{:S(2)}) collective-permute-start(bf16[80,2176]{1,0:T(8,128)(2,1)S(1)} %get-tuple-element.43.near_ref), channel_id=1, source_target_pairs={{0,1},{1,0},{2,3},{3,2},{4,5},{5,4},{6,7},{7,6},{8,9},{9,8},{10,11... | collective-permute-start | bytes 1044488 | tf_op jit(solution)/shard_map/ppermute | solution.py:44
  45.9 4.1 %collective-permute-start.18 = (bf16[80,2176]{1,0:T(8,128)(2,1)S(1)}, bf16[80,2176]{1,0:T(8,128)(2,1)S(1)}, u32[]{:S(2)}, u32[]{:S(2)}) collective-permute-start(bf16[80,2176]{1,0:T(8,128)(2,1)S(1)} %collective-permute-done.17.far_ref), channel_id=1, source_target_pairs={{0,1},{1,0},{2,3},{3,2},{4,5},{5,4},{6,7},{7,6},{8,9},{9,8},{10,11... | collective-permute-start | bytes 1044488 | tf_op jit(solution)/shard_map/ppermute | solution.py:44
  47.4 4.1 %collective-permute-start.13 = (bf16[80,2176]{1,0:T(8,128)(2,1)S(1)}, bf16[80,2176]{1,0:T(8,128)(2,1)S(1)}, u32[]{:S(2)}, u32[]{:S(2)}) collective-permute-start(bf16[80,2176]{1,0:T(8,128)(2,1)S(1)} %get-tuple-element.41.near_ref), channel_id=1, source_target_pairs={{0,1},{1,0},{2,3},{3,2},{4,5},{5,4},{6,7},{7,6},{8,9},{9,8},{10,11... | collective-permute-start | bytes 1044488 | tf_op jit(solution)/shard_map/ppermute | solution.py:44
  48.2 3.3 %collective-permute-start.15 = (bf16[80,2176]{1,0:T(8,128)(2,1)S(1)}, bf16[80,2176]{1,0:T(8,128)(2,1)S(1)}, u32[]{:S(2)}, u32[]{:S(2)}) collective-permute-start(bf16[80,2176]{1,0:T(8,128)(2,1)S(1)} %collective-permute-done.14.far_ref), channel_id=1, source_target_pairs={{0,1},{1,0},{2,3},{3,2},{4,5},{5,4},{6,7},{7,6},{8,9},{9,8},{10,11... | collective-permute-start | bytes 1044488 | tf_op jit(solution)/shard_map/ppermute | solution.py:44
  49.5 7.0 %collective-permute-start.23 = (bf16[160,384]{1,0:T(8,128)(2,1)S(1)}, bf16[160,384]{1,0:T(8,128)(2,1)S(1)}, u32[]{:S(2)}, u32[]{:S(2)}) collective-permute-start(bf16[160,384]{1,0:T(8,128)(2,1)S(1)} %hidden_units.5.after_ref.mine_ref), channel_id=1, source_target_pairs={{0,1},{1,0},{2,3},{3,2},{4,5},{5,4},{6,7},{7,6},{8,9},{9,8},{10,11... | collective-permute-start | bytes 368648 | tf_op jit(solution)/shard_map/ppermute | solution.py:44
  51.4 2.3 %collective-permute-start.24 = (bf16[160,384]{1,0:T(8,128)(2,1)S(1)}, bf16[160,384]{1,0:T(8,128)(2,1)S(1)}, u32[]{:S(2)}, u32[]{:S(2)}) collective-permute-start(bf16[160,384]{1,0:T(8,128)(2,1)S(1)} %hidden_units.6.after_ref.mine_ref), channel_id=1, source_target_pairs={{0,1},{1,0},{2,3},{3,2},{4,5},{5,4},{6,7},{7,6},{8,9},{9,8},{10,11... | collective-permute-start | bytes 368648 | tf_op jit(solution)/shard_map/ppermute | solution.py:44
  52.8 5.2 %collective-permute-start.22 = (bf16[160,384]{1,0:T(8,128)(2,1)S(1)}, bf16[160,384]{1,0:T(8,128)(2,1)S(1)}, u32[]{:S(2)}, u32[]{:S(2)}) collective-permute-start(bf16[160,384]{1,0:T(8,128)(2,1)S(1)} %hidden_units.7.after_ref.mine_ref), channel_id=1, source_target_pairs={{0,1},{1,0},{2,3},{3,2},{4,5},{5,4},{6,7},{7,6},{8,9},{9,8},{10,11... | collective-permute-start | bytes 368648 | tf_op jit(solution)/shard_map/ppermute | solution.py:44
  53.3 7.5 %collective-permute-start.12 = (bf16[80,2048]{1,0:T(8,128)(2,1)S(1)}, bf16[80,2048]{1,0:T(8,128)(2,1)S(1)}, u32[]{:S(2)}, u32[]{:S(2)}) collective-permute-start(bf16[80,2048]{1,0:T(8,128)(2,1)S(1)} %get-tuple-element.40), channel_id=1, source_target_pairs={{0,4},{1,3},{2,6},{3,1},{4,0},{5,7},{6,2},{7,5},{8,12},{9,11},{10,... | collective-permute-start | bytes 983048 | tf_op jit(solution)/shard_map/ppermute | solution.py:44
  54.7 9.2 %collective-permute-start.28 = (bf16[80,2048]{1,0:T(8,128)(2,1)S(1)}, bf16[80,2048]{1,0:T(8,128)(2,1)S(1)}, u32[]{:S(2)}, u32[]{:S(2)}) collective-permute-start(bf16[80,2048]{1,0:T(8,128)(2,1)S(1)} %get-tuple-element.54), channel_id=1, source_target_pairs={{0,4},{1,3},{2,6},{3,1},{4,0},{5,7},{6,2},{7,5},{8,12},{9,11},{10,... | collective-permute-start | bytes 983048 | tf_op jit(solution)/shard_map/ppermute | solution.py:44
  57.6 11.1 %collective-permute-start.27 = (bf16[80,2048]{1,0:T(8,128)(2,1)S(1)}, bf16[80,2048]{1,0:T(8,128)(2,1)S(1)}, u32[]{:S(2)}, u32[]{:S(2)}) collective-permute-start(bf16[80,2048]{1,0:T(8,128)(2,1)S(1)} %get-tuple-element.53), channel_id=1, source_target_pairs={{0,4},{1,3},{2,6},{3,1},{4,0},{5,7},{6,2},{7,5},{8,12},{9,11},{10,... | collective-permute-start | bytes 983048 | tf_op jit(solution)/shard_map/ppermute | solution.py:44
  59.0 16.6 %collective-permute-start.26 = (bf16[80,2048]{1,0:T(8,128)(2,1)S(1)}, bf16[80,2048]{1,0:T(8,128)(2,1)S(1)}, u32[]{:S(2)}, u32[]{:S(2)}) collective-permute-start(bf16[80,2048]{1,0:T(8,128)(2,1)S(1)} %get-tuple-element.52), channel_id=1, source_target_pairs={{0,4},{1,3},{2,6},{3,1},{4,0},{5,7},{6,2},{7,5},{8,12},{9,11},{10,... | collective-permute-start | bytes 983048 | tf_op jit(solution)/shard_map/ppermute | solution.py:44
  64.2 12.9 %collective-permute-start.30 = (bf16[64,2048]{1,0:T(8,128)(2,1)S(1)}, bf16[64,2048]{1,0:T(8,128)(2,1)S(1)}, u32[]{:S(2)}, u32[]{:S(2)}) collective-permute-start(bf16[64,2048]{1,0:T(8,128)(2,1)S(1)} %get-tuple-element.59), channel_id=1, source_target_pairs={{0,2},{1,5},{2,0},{3,7},{4,6},{5,1},{6,4},{7,3},{8,10},{9,13},{10,... | collective-permute-start | bytes 786440 | tf_op jit(solution)/shard_map/ppermute | solution.py:44
  68.9 9.6 %collective-permute-start.32 = (bf16[64,2048]{1,0:T(8,128)(2,1)S(1)}, bf16[64,2048]{1,0:T(8,128)(2,1)S(1)}, u32[]{:S(2)}, u32[]{:S(2)}) collective-permute-start(bf16[64,2048]{1,0:T(8,128)(2,1)S(1)} %get-tuple-element.60), channel_id=1, source_target_pairs={{0,2},{1,5},{2,0},{3,7},{4,6},{5,1},{6,4},{7,3},{8,10},{9,13},{10,... | collective-permute-start | bytes 786440 | tf_op jit(solution)/shard_map/ppermute | solution.py:44
  76.0 6.4 %collective-permute-start.29 = (bf16[64,2048]{1,0:T(8,128)(2,1)S(1)}, bf16[64,2048]{1,0:T(8,128)(2,1)S(1)}, u32[]{:S(2)}, u32[]{:S(2)}) collective-permute-start(bf16[64,2048]{1,0:T(8,128)(2,1)S(1)} %get-tuple-element.58), channel_id=1, source_target_pairs={{0,2},{1,5},{2,0},{3,7},{4,6},{5,1},{6,4},{7,3},{8,10},{9,13},{10,... | collective-permute-start | bytes 786440 | tf_op jit(solution)/shard_map/ppermute | solution.py:44
  77.2 9.3 %collective-permute-start.31 = (bf16[64,2048]{1,0:T(8,128)(2,1)S(1)}, bf16[64,2048]{1,0:T(8,128)(2,1)S(1)}, u32[]{:S(2)}, u32[]{:S(2)}) collective-permute-start(bf16[64,2048]{1,0:T(8,128)(2,1)S(1)} %add_rows.6.refs_2_), channel_id=1, source_target_pairs={{0,8},{1,9},{2,10},{3,11},{4,12},{5,13},{6,14},{7,15},{8,0},{9,1},... | collective-permute-start | bytes 786440 | tf_op jit(solution)/shard_map/ppermute | solution.py:44
  78.1 10.1 %collective-permute-start.25 = (bf16[64,2048]{1,0:T(8,128)(2,1)S(1)}, bf16[64,2048]{1,0:T(8,128)(2,1)S(1)}, u32[]{:S(2)}, u32[]{:S(2)}) collective-permute-start(bf16[64,2048]{1,0:T(8,128)(2,1)S(1)} %get-tuple-element.51), channel_id=1, source_target_pairs={{0,2},{1,5},{2,0},{3,7},{4,6},{5,1},{6,4},{7,3},{8,10},{9,13},{10,... | collective-permute-start | bytes 786440 | tf_op jit(solution)/shard_map/ppermute | solution.py:44
  78.6 11.7 %collective-permute-start.33 = (bf16[64,2048]{1,0:T(8,128)(2,1)S(1)}, bf16[64,2048]{1,0:T(8,128)(2,1)S(1)}, u32[]{:S(2)}, u32[]{:S(2)}) collective-permute-start(bf16[64,2048]{1,0:T(8,128)(2,1)S(1)} %add_rows.7.refs_3_), channel_id=1, source_target_pairs={{0,8},{1,9},{2,10},{3,11},{4,12},{5,13},{6,14},{7,15},{8,0},{9,1},... | collective-permute-start | bytes 786440 | tf_op jit(solution)/shard_map/ppermute | solution.py:44
  86.6 9.2 %collective-permute-start.34 = (bf16[64,2048]{1,0:T(8,128)(2,1)S(1)}, bf16[64,2048]{1,0:T(8,128)(2,1)S(1)}, u32[]{:S(2)}, u32[]{:S(2)}) collective-permute-start(bf16[64,2048]{1,0:T(8,128)(2,1)S(1)} %add_rows.8.refs_2_), channel_id=1, source_target_pairs={{0,24},{1,25},{2,26},{3,27},{4,28},{5,29},{6,30},{7,31},{8,16},{9,... | collective-permute-start | bytes 786440 | tf_op jit(solution)/shard_map/ppermute | solution.py:44

commit v4 on v3

--- a/solution.py
+++ b/solution.py
@@ -14,9 +14,9 @@
     (0, 1, 2, 3),
     (4, 6, 7, 8),
     (5, 10, 9, 11),
-    (12, 14, 13, 15),
-    (19, 17, 16, 18),
-    (19.1, 20, 16.1, 21),
+    (12, 14, 13, 16),
+    (19, 17, 15, 18),
+    (19.1, 20, 15.1, 21),
 )
 HEAVY, LIGHT = 2 * 10**9, 10**7
 VMEM_BYTES = 8 << 20

time: 97.7 us -> 97.6 us (level)
  transfers between devices with their start and end apart: 35 -> 35, of which waited for: 17 -> 18; matrix products, arithmetic and copies ran while one was open for 0% -> 0% of each run, Pallas kernels for 18% -> 18%
where the time goes in v4:
time: 97.6 us; the launch traced here: 96.5 us
  waiting for transfers between devices  49.9 us (51%)
  starting transfers between devices  27.1 us (28%)
  Pallas kernels  17.9 us (18%)
  local copies, waits for them, and re-layouts  1.01 us (1%)
    ppermute x35, waiting for transfers between devices, swap(): return lax.ppermute(array, ('expert', 'tensor'), pairs)  49.9 us
    ppermute x35, starting transfers between devices, swap(): return lax.ppermute(array, ('expert', 'tensor'), pairs)  27.1 us
    pallas_call x4, Pallas kernels, hidden_units(): pl.pallas_call(kernel, in_specs=[pl.BlockSpec(memory_space=pltpu.SMEM)] +...  5.15 us
    pallas_call x4, Pallas kernels, routed_outputs(): pl.pallas_call(kernel, in_specs=[pl.BlockSpec(memory_space=pltpu.SMEM)] +...  4.3 us
    pallas_call x4, Pallas kernels, pick_rows(): pl.pallas_call(kernel, in_specs=[vmem, vmem, vmem, pl.BlockSpec(memory_sp...  4.25 us
  transfers between devices with their start and end apart: 35, of which 18 were waited for; matrix products, arithmetic and copies ran while one was open for 0% of the time, Pallas kernels for 18%

profile of v4, /device:TPU:8, one launch (start us, length us, event | category | flops | bytes accessed | tf_op | source)
XLA Modules:
  0.0 96.5 jit_solution(6764041580682335393)
XLA Ops:
  0.0 1.9 %scaled_tokens.1.near_ref = bf16[64,2176]{1,0:T(8,128)(2,1)} custom-call(bf16[64,2048]{1,0:T(8,128)(2,1)} %values_ref.1, bf16[16,64]{1,0:T(8,128)(2,1)} %bitcast.20, s32[8,64]{1,0:T(8,128)} %bitcast.21, s32[8,64]{1,0:T(8,128)} %bitcast.22), custom_call_target="tpu_custom_call" | custom-call | flops 2000000000 | bytes 1000000 | tf_op jit(solution)/shard_map/scaled_tokens/pallas_call | solution.py:87
  1.9 1.5 %collective-permute-start = (bf16[64,2176]{1,0:T(8,128)(2,1)}, bf16[64,2176]{1,0:T(8,128)(2,1)}, u32[]{:S(2)}, u32[]{:S(2)}) collective-permute-start(bf16[64,2176]{1,0:T(8,128)(2,1)} %scaled_tokens.1.near_ref), channel_id=1, source_target_pairs={{0,2},{1,5},{2,0},{3,7},{4,6},{5,1},{6,4},{7,3},{8,10},{9,13},{10,... | collective-permute-start | bytes 835592 | tf_op jit(solution)/shard_map/ppermute | solution.py:44
  3.4 0.4 collective-permute-start.8
  3.9 2.6 %collective-permute-start.4 = (bf16[64,2176]{1,0:T(8,128)(2,1)}, bf16[64,2176]{1,0:T(8,128)(2,1)S(1)}, u32[]{:S(2)}, u32[]{:S(2)}) collective-permute-start(bf16[64,2176]{1,0:T(8,128)(2,1)} %scaled_tokens.1.near_ref), channel_id=1, source_target_pairs={{0,16},{1,17},{2,18},{3,19},{4,20},{5,21},{6,22},{7,23},{8,24},{9,... | collective-permute-start | bytes 835592 | tf_op jit(solution)/shard_map/ppermute | solution.py:44
  6.6 9.8 %collective-permute-done.8.near_ref = bf16[64,2176]{1,0:T(8,128)(2,1)} collective-permute-done((bf16[64,2176]{1,0:T(8,128)(2,1)}, bf16[64,2176]{1,0:T(8,128)(2,1)}, u32[]{:S(2)}, u32[]{:S(2)}) %collective-permute-start.8) | collective-permute-done | bytes 278560 | tf_op jit(solution)/shard_map/ppermute | solution.py:44
  16.4 3.2 %collective-permute-done.4.near_ref = bf16[64,2176]{1,0:T(8,128)(2,1)S(1)} collective-permute-done((bf16[64,2176]{1,0:T(8,128)(2,1)}, bf16[64,2176]{1,0:T(8,128)(2,1)S(1)}, u32[]{:S(2)}, u32[]{:S(2)}) %collective-permute-start.4) | collective-permute-done | bytes 278560 | tf_op jit(solution)/shard_map/ppermute | solution.py:44
  19.5 1.6 %collective-permute-start.5 = (bf16[64,2176]{1,0:T(8,128)(2,1)S(1)}, bf16[64,2176]{1,0:T(8,128)(2,1)S(1)}, u32[]{:S(2)}, u32[]{:S(2)}) collective-permute-start(bf16[64,2176]{1,0:T(8,128)(2,1)S(1)} %collective-permute-done.4.near_ref), channel_id=1, source_target_pairs={{0,8},{1,9},{2,10},{3,11},{4,12},{5,13},{6,14},{7,15},{8,0},{9,1},... | collective-permute-start | bytes 835592 | tf_op jit(solution)/shard_map/ppermute | solution.py:44
  21.1 1.0 copy-done.3
  22.1 1.5 %pick_rows.4 = (bf16[80,2176]{1,0:T(8,128)(2,1)S(1)}, bf16[80,2176]{1,0:T(8,128)(2,1)S(1)}, bf16[160,128]{1,0:T(8,128)(2,1)S(1)}) custom-call(bf16[64,2176]{1,0:T(8,128)(2,1)S(1)} %copy-done.3, bf16[64,2176]{1,0:T(8,128)(2,1)} %collective-permute-done.next_ref, bf16[8,128]{1,0:T(8,128)(2,1)S(1)} %convert_element_type.16.lanes_ref.after_ref, ...), custom_call_target="tpu_custom_call" | custom-call | flops 2000000000 | bytes 1000000 | tf_op jit(solution)/shard_map/pick_rows/pallas_call | solution.py:128
  23.6 0.6 collective-permute-start.2
  24.2 1.5 %collective-permute-start.7 = (bf16[64,2176]{1,0:T(8,128)(2,1)S(1)}, bf16[64,2176]{1,0:T(8,128)(2,1)S(1)}, u32[]{:S(2)}, u32[]{:S(2)}) collective-permute-start(bf16[64,2176]{1,0:T(8,128)(2,1)S(1)} %collective-permute-done.4.near_ref), channel_id=1, source_target_pairs={{0,2},{1,5},{2,0},{3,7},{4,6},{5,1},{6,4},{7,3},{8,10},{9,13},{10,... | collective-permute-start | bytes 835592 | tf_op jit(solution)/shard_map/ppermute | solution.py:44
  25.7 0.2 multiply_convert_fusion.1
  26.0 1.5 %collective-permute-done.5.near_ref = bf16[64,2176]{1,0:T(8,128)(2,1)S(1)} collective-permute-done((bf16[64,2176]{1,0:T(8,128)(2,1)S(1)}, bf16[64,2176]{1,0:T(8,128)(2,1)S(1)}, u32[]{:S(2)}, u32[]{:S(2)}) %collective-permute-start.5) | collective-permute-done | bytes 278560 | tf_op jit(solution)/shard_map/ppermute | solution.py:44
  27.5 2.0 %collective-permute-start.6 = (bf16[64,2176]{1,0:T(8,128)(2,1)S(1)}, bf16[64,2176]{1,0:T(8,128)(2,1)S(1)}, u32[]{:S(2)}, u32[]{:S(2)}) collective-permute-start(bf16[64,2176]{1,0:T(8,128)(2,1)S(1)} %collective-permute-done.5.near_ref), channel_id=1, source_target_pairs={{0,2},{1,5},{2,0},{3,7},{4,6},{5,1},{6,4},{7,3},{8,10},{9,13},{10,... | collective-permute-start | bytes 835592 | tf_op jit(solution)/shard_map/ppermute | solution.py:44
  29.5 1.5 %pick_rows.5 = (bf16[80,2176]{1,0:T(8,128)(2,1)S(1)}, bf16[80,2176]{1,0:T(8,128)(2,1)S(1)}, bf16[160,128]{1,0:T(8,128)(2,1)S(1)}) custom-call(bf16[64,2176]{1,0:T(8,128)(2,1)} %collective-permute-done.8.near_ref, bf16[64,2176]{1,0:T(8,128)(2,1)S(1)} %collective-permute-done.9.next_ref, bf16[8,128]{1,0:T(8,128)(2,1)S(1)} %convert_element_type.16.lanes_ref.after_ref, ...), custom_call_target="tpu_custom_call" | custom-call | flops 2000000000 | bytes 1000000 | tf_op jit(solution)/shard_map/pick_rows/pallas_call | solution.py:128
  31.1 1.5 %collective-permute-done.7.next_ref = bf16[64,2176]{1,0:T(8,128)(2,1)S(1)} collective-permute-done((bf16[64,2176]{1,0:T(8,128)(2,1)S(1)}, bf16[64,2176]{1,0:T(8,128)(2,1)S(1)}, u32[]{:S(2)}, u32[]{:S(2)}) %collective-permute-start.7) | collective-permute-done | bytes 278560 | tf_op jit(solution)/shard_map/ppermute | solution.py:44
  32.6 2.1 %collective-permute-done.2.far_ref = bf16[80,2176]{1,0:T(8,128)(2,1)S(1)} collective-permute-done((bf16[80,2176]{1,0:T(8,128)(2,1)S(1)}, bf16[80,2176]{1,0:T(8,128)(2,1)S(1)}, u32[]{:S(2)}, u32[]{:S(2)}) %collective-permute-start.2) | collective-permute-done | bytes 348192 | tf_op jit(solution)/shard_map/ppermute | solution.py:44
  34.7 0.6 pick_rows.6
  35.3 0.5 collective-permute-done.6.next_ref
  35.8 0.1 collective-permute-start.17
  35.9 0.6 pick_rows.7
  36.5 2.0 %collective-permute-start.19 = (bf16[80,2176]{1,0:T(8,128)(2,1)S(1)}, bf16[80,2176]{1,0:T(8,128)(2,1)S(1)}, u32[]{:S(2)}, u32[]{:S(2)}) collective-permute-start(bf16[80,2176]{1,0:T(8,128)(2,1)S(1)} %get-tuple-element.45.near_ref), channel_id=1, source_target_pairs={{0,1},{1,0},{2,3},{3,2},{4,5},{5,4},{6,7},{7,6},{8,9},{9,8},{10,11... | collective-permute-start | bytes 1044488 | tf_op jit(solution)/shard_map/ppermute | solution.py:44
  38.5 2.2 %collective-permute-done.20.far_ref = bf16[80,2176]{1,0:T(8,128)(2,1)S(1)} collective-permute-done((bf16[80,2176]{1,0:T(8,128)(2,1)S(1)}, bf16[80,2176]{1,0:T(8,128)(2,1)S(1)}, u32[]{:S(2)}, u32[]{:S(2)}) %collective-permute-start.20) | collective-permute-done | bytes 348192 | tf_op jit(solution)/shard_map/ppermute | solution.py:44
  40.7 0.3 collective-permute-start.14
  41.1 1.3 %hidden_units.4.mine_ref.after_ref = bf16[160,384]{1,0:T(8,128)(2,1)S(1)} custom-call(s32[1]{0:T(128)} %bitcast.3.core_ref, bf16[80,2176]{1,0:T(8,128)(2,1)S(1)} %get-tuple-element.34.near_ref, bf16[80,2176]{1,0:T(8,128)(2,1)S(1)} %collective-permute-done.1.near_pair_ref, bf16[80,2176]{1,0:T(8,128)(2,1)S(1)} %collective-permute-done.2.far_ref, ...), custom_call_target="tpu_custom_call" | custom-call | flops 2000000000 | bytes 1000000 | tf_op jit(solution)/shard_map/hidden_units/pallas_call | solution.py:187
  42.4 2.1 %collective-permute-done.17.far_ref = bf16[80,2176]{1,0:T(8,128)(2,1)S(1)} collective-permute-done((bf16[80,2176]{1,0:T(8,128)(2,1)S(1)}, bf16[80,2176]{1,0:T(8,128)(2,1)S(1)}, u32[]{:S(2)}, u32[]{:S(2)}) %collective-permute-start.17) | collective-permute-done | bytes 348192 | tf_op jit(solution)/shard_map/ppermute | solution.py:44
  44.5 1.3 %collective-permute-done.10.theirs_ref = bf16[160,384]{1,0:T(8,128)(2,1)S(1)} collective-permute-done((bf16[160,384]{1,0:T(8,128)(2,1)S(1)}, bf16[160,384]{1,0:T(8,128)(2,1)S(1)}, u32[]{:S(2)}, u32[]{:S(2)}) %collective-permute-start.10) | collective-permute-done | bytes 122912 | tf_op jit(solution)/shard_map/ppermute | solution.py:44
  45.8 0.1 collective-permute-start.16
  45.9 0.4 collective-permute-start.18
  46.3 1.1 %routed_outputs.4 = (bf16[80,2048]{1,0:T(8,128)(2,1)S(1)}, bf16[80,2048]{1,0:T(8,128)(2,1)S(1)}) custom-call(s32[1]{0:T(128)} %bitcast.3.core_ref, bf16[160,384]{1,0:T(8,128)(2,1)S(1)} %hidden_units.4.mine_ref.after_ref, bf16[160,384]{1,0:T(8,128)(2,1)S(1)} %collective-permute-done.10.theirs_ref, bf16[256,256]{1,0:T(8,128)(2,1)S(1)} %maximum_maximum_fusion.mix_ref, ...), custom_call_target="tpu_custom_call" | custom-call | flops 2000000000 | bytes 1000000 | tf_op jit(solution)/shard_map/routed_outputs/pallas_call | solution.py:233
  47.4 0.2 collective-permute-start.13
  47.6 0.6 collective-permute-done.14.far_ref
  48.2 1.3 %hidden_units.5.after_ref.mine_ref = bf16[160,384]{1,0:T(8,128)(2,1)S(1)} custom-call(s32[1]{0:T(128)} %bitcast.3.core_ref, bf16[80,2176]{1,0:T(8,128)(2,1)S(1)} %get-tuple-element.45.near_ref, bf16[80,2176]{1,0:T(8,128)(2,1)S(1)} %collective-permute-done.19.near_pair_ref, bf16[80,2176]{1,0:T(8,128)(2,1)S(1)} %collective-permute-done.20.far_ref, ...), custom_call_target="tpu_custom_call" | custom-call | flops 2000000000 | bytes 1000000 | tf_op jit(solution)/shard_map/hidden_units/pallas_call | solution.py:187
  49.5 0.6 collective-permute-start.23
  50.0 1.3 %hidden_units.6.after_ref.mine_ref = bf16[160,384]{1,0:T(8,128)(2,1)S(1)} custom-call(s32[1]{0:T(128)} %bitcast.3.core_ref, bf16[80,2176]{1,0:T(8,128)(2,1)S(1)} %get-tuple-element.43.near_ref, bf16[80,2176]{1,0:T(8,128)(2,1)S(1)} %collective-permute-done.16.near_pair_ref, bf16[80,2176]{1,0:T(8,128)(2,1)S(1)} %collective-permute-done.17.far_ref, ...), custom_call_target="tpu_custom_call" | custom-call | flops 2000000000 | bytes 1000000 | tf_op jit(solution)/shard_map/hidden_units/pallas_call | solution.py:187
  51.5 1.3 %hidden_units.7.after_ref.mine_ref = bf16[160,384]{1,0:T(8,128)(2,1)S(1)} custom-call(s32[1]{0:T(128)} %bitcast.3.core_ref, bf16[80,2176]{1,0:T(8,128)(2,1)S(1)} %get-tuple-element.41.near_ref, bf16[80,2176]{1,0:T(8,128)(2,1)S(1)} %collective-permute-done.13.near_pair_ref, bf16[80,2176]{1,0:T(8,128)(2,1)S(1)} %collective-permute-done.14.far_ref, ...), custom_call_target="tpu_custom_call" | custom-call | flops 2000000000 | bytes 1000000 | tf_op jit(solution)/shard_map/hidden_units/pallas_call | solution.py:187
  52.8 0.5 collective-permute-start.22
  53.3 0.3 collective-permute-start.12
  53.6 1.1 %routed_outputs.5 = (bf16[80,2048]{1,0:T(8,128)(2,1)S(1)}, bf16[80,2048]{1,0:T(8,128)(2,1)S(1)}) custom-call(s32[1]{0:T(128)} %bitcast.3.core_ref, bf16[160,384]{1,0:T(8,128)(2,1)S(1)} %hidden_units.6.after_ref.mine_ref, bf16[160,384]{1,0:T(8,128)(2,1)S(1)} %collective-permute-done.24.theirs_ref, bf16[256,256]{1,0:T(8,128)(2,1)S(1)} %maximum_maximum_fusion.mix_ref, ...), custom_call_target="tpu_custom_call" | custom-call | flops 2000000000 | bytes 1000000 | tf_op jit(solution)/shard_map/routed_outputs/pallas_call | solution.py:233
  54.7 1.8 %collective-permute-start.27 = (bf16[80,2048]{1,0:T(8,128)(2,1)S(1)}, bf16[80,2048]{1,0:T(8,128)(2,1)S(1)}, u32[]{:S(2)}, u32[]{:S(2)}) collective-permute-start(bf16[80,2048]{1,0:T(8,128)(2,1)S(1)} %get-tuple-element.53), channel_id=1, source_target_pairs={{0,4},{1,3},{2,6},{3,1},{4,0},{5,7},{6,2},{7,5},{8,12},{9,11},{10,... | collective-permute-start | bytes 983048 | tf_op jit(solution)/shard_map/ppermute | solution.py:44
  56.5 1.1 %routed_outputs.6 = (bf16[80,2048]{1,0:T(8,128)(2,1)S(1)}, bf16[80,2048]{1,0:T(8,128)(2,1)S(1)}) custom-call(s32[1]{0:T(128)} %bitcast.3.core_ref, bf16[160,384]{1,0:T(8,128)(2,1)S(1)} %hidden_units.5.after_ref.mine_ref, bf16[160,384]{1,0:T(8,128)(2,1)S(1)} %collective-permute-done.23.theirs_ref, bf16[256,256]{1,0:T(8,128)(2,1)S(1)} %maximum_maximum_fusion.mix_ref, ...), custom_call_target="tpu_custom_call" | custom-call | flops 2000000000 | bytes 1000000 | tf_op jit(solution)/shard_map/routed_outputs/pallas_call | solution.py:233
  57.6 0.4 collective-permute-start.29
  58.0 1.1 %routed_outputs.7 = (bf16[80,2048]{1,0:T(8,128)(2,1)S(1)}, bf16[80,2048]{1,0:T(8,128)(2,1)S(1)}) custom-call(s32[1]{0:T(128)} %bitcast.3.core_ref, bf16[160,384]{1,0:T(8,128)(2,1)S(1)} %hidden_units.7.after_ref.mine_ref, bf16[160,384]{1,0:T(8,128)(2,1)S(1)} %collective-permute-done.22.theirs_ref, bf16[256,256]{1,0:T(8,128)(2,1)S(1)} %maximum_maximum_fusion.mix_ref, ...), custom_call_target="tpu_custom_call" | custom-call | flops 2000000000 | bytes 1000000 | tf_op jit(solution)/shard_map/routed_outputs/pallas_call | solution.py:233
  59.1 1.8 %collective-permute-start.26 = (bf16[80,2048]{1,0:T(8,128)(2,1)S(1)}, bf16[80,2048]{1,0:T(8,128)(2,1)S(1)}, u32[]{:S(2)}, u32[]{:S(2)}) collective-permute-start(bf16[80,2048]{1,0:T(8,128)(2,1)S(1)} %get-tuple-element.52), channel_id=1, source_target_pairs={{0,4},{1,3},{2,6},{3,1},{4,0},{5,7},{6,2},{7,5},{8,12},{9,11},{10,... | collective-permute-start | bytes 983048 | tf_op jit(solution)/shard_map/ppermute | solution.py:44
  60.8 0.3 spread_rows.4
  61.1 2.7 %collective-permute-done.27.back_ref = bf16[80,2048]{1,0:T(8,128)(2,1)S(1)} collective-permute-done((bf16[80,2048]{1,0:T(8,128)(2,1)S(1)}, bf16[80,2048]{1,0:T(8,128)(2,1)S(1)}, u32[]{:S(2)}, u32[]{:S(2)}) %collective-permute-start.27) | collective-permute-done | bytes 327712 | tf_op jit(solution)/shard_map/ppermute | solution.py:44
  63.9 0.3 spread_rows.5
  64.2 1.2 %collective-permute-start.28 = (bf16[64,2048]{1,0:T(8,128)(2,1)S(1)}, bf16[64,2048]{1,0:T(8,128)(2,1)S(1)}, u32[]{:S(2)}, u32[]{:S(2)}) collective-permute-start(bf16[64,2048]{1,0:T(8,128)(2,1)S(1)} %get-tuple-element.55), channel_id=1, source_target_pairs={{0,2},{1,5},{2,0},{3,7},{4,6},{5,1},{6,4},{7,3},{8,10},{9,13},{10,... | collective-permute-start | bytes 786440 | tf_op jit(solution)/shard_map/ppermute | solution.py:44
  65.4 3.2 %collective-permute-done.29.back_ref = bf16[80,2048]{1,0:T(8,128)(2,1)S(1)} collective-permute-done((bf16[80,2048]{1,0:T(8,128)(2,1)S(1)}, bf16[80,2048]{1,0:T(8,128)(2,1)S(1)}, u32[]{:S(2)}, u32[]{:S(2)}) %collective-permute-start.29) | collective-permute-done | bytes 327712 | tf_op jit(solution)/shard_map/ppermute | solution.py:44
  68.6 0.3 spread_rows.6
  69.0 1.2 %collective-permute-start.32 = (bf16[64,2048]{1,0:T(8,128)(2,1)S(1)}, bf16[64,2048]{1,0:T(8,128)(2,1)S(1)}, u32[]{:S(2)}, u32[]{:S(2)}) collective-permute-start(bf16[64,2048]{1,0:T(8,128)(2,1)S(1)} %get-tuple-element.60), channel_id=1, source_target_pairs={{0,2},{1,5},{2,0},{3,7},{4,6},{5,1},{6,4},{7,3},{8,10},{9,13},{10,... | collective-permute-start | bytes 786440 | tf_op jit(solution)/shard_map/ppermute | solution.py:44
  70.1 2.7 %collective-permute-done.28.refs_1_ = bf16[64,2048]{1,0:T(8,128)(2,1)S(1)} collective-permute-done((bf16[64,2048]{1,0:T(8,128)(2,1)S(1)}, bf16[64,2048]{1,0:T(8,128)(2,1)S(1)}, u32[]{:S(2)}, u32[]{:S(2)}) %collective-permute-start.28) | collective-permute-done | bytes 262176 | tf_op jit(solution)/shard_map/ppermute | solution.py:44
  72.9 2.8 %collective-permute-done.26.back_ref = bf16[80,2048]{1,0:T(8,128)(2,1)S(1)} collective-permute-done((bf16[80,2048]{1,0:T(8,128)(2,1)S(1)}, bf16[80,2048]{1,0:T(8,128)(2,1)S(1)}, u32[]{:S(2)}, u32[]{:S(2)}) %collective-permute-start.26) | collective-permute-done | bytes 327712 | tf_op jit(solution)/shard_map/ppermute | solution.py:44
  75.7 0.3 spread_rows.7
  76.0 1.2 %collective-permute-start.30 = (bf16[64,2048]{1,0:T(8,128)(2,1)S(1)}, bf16[64,2048]{1,0:T(8,128)(2,1)S(1)}, u32[]{:S(2)}, u32[]{:S(2)}) collective-permute-start(bf16[64,2048]{1,0:T(8,128)(2,1)S(1)} %get-tuple-element.59), channel_id=1, source_target_pairs={{0,2},{1,5},{2,0},{3,7},{4,6},{5,1},{6,4},{7,3},{8,10},{9,13},{10,... | collective-permute-start | bytes 786440 | tf_op jit(solution)/shard_map/ppermute | solution.py:44
  77.2 0.9 collective-permute-start.31
  78.0 0.4 collective-permute-start.25
  78.5 1.7 %collective-permute-start.33 = (bf16[64,2048]{1,0:T(8,128)(2,1)S(1)}, bf16[64,2048]{1,0:T(8,128)(2,1)S(1)}, u32[]{:S(2)}, u32[]{:S(2)}) collective-permute-start(bf16[64,2048]{1,0:T(8,128)(2,1)S(1)} %add_rows.7.refs_3_), channel_id=1, source_target_pairs={{0,8},{1,9},{2,10},{3,11},{4,12},{5,13},{6,14},{7,15},{8,0},{9,1},... | collective-permute-start | bytes 786440 | tf_op jit(solution)/shard_map/ppermute | solution.py:44
  80.2 2.2 %collective-permute-done.30.refs_1_ = bf16[64,2048]{1,0:T(8,128)(2,1)S(1)} collective-permute-done((bf16[64,2048]{1,0:T(8,128)(2,1)S(1)}, bf16[64,2048]{1,0:T(8,128)(2,1)S(1)}, u32[]{:S(2)}, u32[]{:S(2)}) %collective-permute-start.30) | collective-permute-done | bytes 262176 | tf_op jit(solution)/shard_map/ppermute | solution.py:44
  82.4 4.0 %collective-permute-done.31.refs_2_ = bf16[64,2048]{1,0:T(8,128)(2,1)S(1)} collective-permute-done((bf16[64,2048]{1,0:T(8,128)(2,1)S(1)}, bf16[64,2048]{1,0:T(8,128)(2,1)S(1)}, u32[]{:S(2)}, u32[]{:S(2)}) %collective-permute-start.31) | collective-permute-done | bytes 262176 | tf_op jit(solution)/shard_map/ppermute | solution.py:44
  86.5 1.6 %collective-permute-start.34 = (bf16[64,2048]{1,0:T(8,128)(2,1)S(1)}, bf16[64,2048]{1,0:T(8,128)(2,1)S(1)}, u32[]{:S(2)}, u32[]{:S(2)}) collective-permute-start(bf16[64,2048]{1,0:T(8,128)(2,1)S(1)} %add_rows.8.refs_2_), channel_id=1, source_target_pairs={{0,24},{1,25},{2,26},{3,27},{4,28},{5,29},{6,30},{7,31},{8,16},{9,... | collective-permute-start | bytes 786440 | tf_op jit(solution)/shard_map/ppermute | solution.py:44
  88.2 2.1 %collective-permute-done.33.refs_1_ = bf16[64,2048]{1,0:T(8,128)(2,1)S(1)} collective-permute-done((bf16[64,2048]{1,0:T(8,128)(2,1)S(1)}, bf16[64,2048]{1,0:T(8,128)(2,1)S(1)}, u32[]{:S(2)}, u32[]{:S(2)}) %collective-permute-start.33) | collective-permute-done | bytes 262176 | tf_op jit(solution)/shard_map/ppermute | solution.py:44
  90.3 5.4 %collective-permute-done.34.refs_1_ = bf16[64,2048]{1,0:T(8,128)(2,1)S(1)} collective-permute-done((bf16[64,2048]{1,0:T(8,128)(2,1)S(1)}, bf16[64,2048]{1,0:T(8,128)(2,1)S(1)}, u32[]{:S(2)}, u32[]{:S(2)}) %collective-permute-start.34) | collective-permute-done | bytes 262176 | tf_op jit(solution)/shard_map/ppermute | solution.py:44
  95.7 0.7 add_rows.11
  (48 shorter events, 0.6 us)
Async XLA Ops:
  0.0 45.9 %collective-permute-start.11 = (bf16[384,4096]{1,0:T(8,128)(2,1)}, bf16[384,4096]{1,0:T(8,128)(2,1)S(1)}, u32[]{:S(2)}, u32[]{:S(2)}) collective-permute-start(bf16[384,4096]{1,0:T(8,128)(2,1)} %bitcast.7), channel_id=1, source_target_pairs={{0,1},{1,0},{2,3},{3,2},{4,5},{5,4},{6,7},{7,6},{8,9},{9,8},{10,11... | collective-permute-start | bytes 9437192 | tf_op jit(solution)/shard_map/ppermute | solution.py:44
  1.9 19.2 %collective-permute-start = (bf16[64,2176]{1,0:T(8,128)(2,1)}, bf16[64,2176]{1,0:T(8,128)(2,1)}, u32[]{:S(2)}, u32[]{:S(2)}) collective-permute-start(bf16[64,2176]{1,0:T(8,128)(2,1)} %scaled_tokens.1.near_ref), channel_id=1, source_target_pairs={{0,2},{1,5},{2,0},{3,7},{4,6},{5,1},{6,4},{7,3},{8,10},{9,13},{10,... | collective-permute-start | bytes 835592 | tf_op jit(solution)/shard_map/ppermute | solution.py:44
  3.4 12.9 %collective-permute-start.8 = (bf16[64,2176]{1,0:T(8,128)(2,1)}, bf16[64,2176]{1,0:T(8,128)(2,1)}, u32[]{:S(2)}, u32[]{:S(2)}) collective-permute-start(bf16[64,2176]{1,0:T(8,128)(2,1)} %scaled_tokens.1.near_ref), channel_id=1, source_target_pairs={{0,8},{1,9},{2,10},{3,11},{4,12},{5,13},{6,14},{7,15},{8,0},{9,1},... | collective-permute-start | bytes 835592 | tf_op jit(solution)/shard_map/ppermute | solution.py:44
  3.9 15.7 %collective-permute-start.4 = (bf16[64,2176]{1,0:T(8,128)(2,1)}, bf16[64,2176]{1,0:T(8,128)(2,1)S(1)}, u32[]{:S(2)}, u32[]{:S(2)}) collective-permute-start(bf16[64,2176]{1,0:T(8,128)(2,1)} %scaled_tokens.1.near_ref), channel_id=1, source_target_pairs={{0,16},{1,17},{2,18},{3,19},{4,20},{5,21},{6,22},{7,23},{8,24},{9,... | collective-permute-start | bytes 835592 | tf_op jit(solution)/shard_map/ppermute | solution.py:44
  16.4 9.6 %collective-permute-start.9 = (bf16[64,2176]{1,0:T(8,128)(2,1)}, bf16[64,2176]{1,0:T(8,128)(2,1)S(1)}, u32[]{:S(2)}, u32[]{:S(2)}) collective-permute-start(bf16[64,2176]{1,0:T(8,128)(2,1)} %collective-permute-done.8.near_ref), channel_id=1, source_target_pairs={{0,2},{1,5},{2,0},{3,7},{4,6},{5,1},{6,4},{7,3},{8,10},{9,13},{10,... | collective-permute-start | bytes 835592 | tf_op jit(solution)/shard_map/ppermute | solution.py:44
  19.5 8.0 %collective-permute-start.5 = (bf16[64,2176]{1,0:T(8,128)(2,1)S(1)}, bf16[64,2176]{1,0:T(8,128)(2,1)S(1)}, u32[]{:S(2)}, u32[]{:S(2)}) collective-permute-start(bf16[64,2176]{1,0:T(8,128)(2,1)S(1)} %collective-permute-done.4.near_ref), channel_id=1, source_target_pairs={{0,8},{1,9},{2,10},{3,11},{4,12},{5,13},{6,14},{7,15},{8,0},{9,1},... | collective-permute-start | bytes 835592 | tf_op jit(solution)/shard_map/ppermute | solution.py:44
  21.1 1.0 copy-start.3
  23.6 11.0 %collective-permute-start.2 = (bf16[80,2176]{1,0:T(8,128)(2,1)S(1)}, bf16[80,2176]{1,0:T(8,128)(2,1)S(1)}, u32[]{:S(2)}, u32[]{:S(2)}) collective-permute-start(bf16[80,2176]{1,0:T(8,128)(2,1)S(1)} %get-tuple-element.35), channel_id=1, source_target_pairs={{0,4},{1,3},{2,6},{3,1},{4,0},{5,7},{6,2},{7,5},{8,12},{9,11},{10,... | collective-permute-start | bytes 1044488 | tf_op jit(solution)/shard_map/ppermute | solution.py:44
  24.2 8.4 %collective-permute-start.7 = (bf16[64,2176]{1,0:T(8,128)(2,1)S(1)}, bf16[64,2176]{1,0:T(8,128)(2,1)S(1)}, u32[]{:S(2)}, u32[]{:S(2)}) collective-permute-start(bf16[64,2176]{1,0:T(8,128)(2,1)S(1)} %collective-permute-done.4.near_ref), channel_id=1, source_target_pairs={{0,2},{1,5},{2,0},{3,7},{4,6},{5,1},{6,4},{7,3},{8,10},{9,13},{10,... | collective-permute-start | bytes 835592 | tf_op jit(solution)/shard_map/ppermute | solution.py:44
  25.9 10.6 %collective-permute-start.1 = (bf16[80,2176]{1,0:T(8,128)(2,1)S(1)}, bf16[80,2176]{1,0:T(8,128)(2,1)S(1)}, u32[]{:S(2)}, u32[]{:S(2)}) collective-permute-start(bf16[80,2176]{1,0:T(8,128)(2,1)S(1)} %get-tuple-element.34.near_ref), channel_id=1, source_target_pairs={{0,1},{1,0},{2,3},{3,2},{4,5},{5,4},{6,7},{7,6},{8,9},{9,8},{10,11... | collective-permute-start | bytes 1044488 | tf_op jit(solution)/shard_map/ppermute | solution.py:44
  27.5 8.3 %collective-permute-start.6 = (bf16[64,2176]{1,0:T(8,128)(2,1)S(1)}, bf16[64,2176]{1,0:T(8,128)(2,1)S(1)}, u32[]{:S(2)}, u32[]{:S(2)}) collective-permute-start(bf16[64,2176]{1,0:T(8,128)(2,1)S(1)} %collective-permute-done.5.near_ref), channel_id=1, source_target_pairs={{0,2},{1,5},{2,0},{3,7},{4,6},{5,1},{6,4},{7,3},{8,10},{9,13},{10,... | collective-permute-start | bytes 835592 | tf_op jit(solution)/shard_map/ppermute | solution.py:44
  32.6 8.1 %collective-permute-start.20 = (bf16[80,2176]{1,0:T(8,128)(2,1)S(1)}, bf16[80,2176]{1,0:T(8,128)(2,1)S(1)}, u32[]{:S(2)}, u32[]{:S(2)}) collective-permute-start(bf16[80,2176]{1,0:T(8,128)(2,1)S(1)} %get-tuple-element.46), channel_id=1, source_target_pairs={{0,4},{1,3},{2,6},{3,1},{4,0},{5,7},{6,2},{7,5},{8,12},{9,11},{10,... | collective-permute-start | bytes 1044488 | tf_op jit(solution)/shard_map/ppermute | solution.py:44
  34.7 6.4 %collective-permute-start.3 = (bf16[80,2176]{1,0:T(8,128)(2,1)S(1)}, bf16[80,2176]{1,0:T(8,128)(2,1)S(1)}, u32[]{:S(2)}, u32[]{:S(2)}) collective-permute-start(bf16[80,2176]{1,0:T(8,128)(2,1)S(1)} %collective-permute-done.2.far_ref), channel_id=1, source_target_pairs={{0,1},{1,0},{2,3},{3,2},{4,5},{5,4},{6,7},{7,6},{8,9},{9,8},{10,11... | collective-permute-start | bytes 1044488 | tf_op jit(solution)/shard_map/ppermute | solution.py:44
  35.8 8.7 %collective-permute-start.17 = (bf16[80,2176]{1,0:T(8,128)(2,1)S(1)}, bf16[80,2176]{1,0:T(8,128)(2,1)S(1)}, u32[]{:S(2)}, u32[]{:S(2)}) collective-permute-start(bf16[80,2176]{1,0:T(8,128)(2,1)S(1)} %get-tuple-element.44), channel_id=1, source_target_pairs={{0,4},{1,3},{2,6},{3,1},{4,0},{5,7},{6,2},{7,5},{8,12},{9,11},{10,... | collective-permute-start | bytes 1044488 | tf_op jit(solution)/shard_map/ppermute | solution.py:44
  35.9 5.1 %copy-start.1 = (bf16[1,4096,384]{2,1,0:T(8,128)(2,1)S(1)}, bf16[1,4096,384]{2,1,0:T(8,128)(2,1)}, u32[]{:S(2)}) copy-start(bf16[1,4096,384]{2,1,0:T(8,128)(2,1)} %param.11) | copy-start | bytes 9437188
  35.9 5.1 %copy-start.2 = (bf16[1,4096,384]{2,1,0:T(8,128)(2,1)S(1)}, bf16[1,4096,384]{2,1,0:T(8,128)(2,1)}, u32[]{:S(2)}) copy-start(bf16[1,4096,384]{2,1,0:T(8,128)(2,1)} %param.12) | copy-start | bytes 9437188
  36.5 10.8 %collective-permute-start.19 = (bf16[80,2176]{1,0:T(8,128)(2,1)S(1)}, bf16[80,2176]{1,0:T(8,128)(2,1)S(1)}, u32[]{:S(2)}, u32[]{:S(2)}) collective-permute-start(bf16[80,2176]{1,0:T(8,128)(2,1)S(1)} %get-tuple-element.45.near_ref), channel_id=1, source_target_pairs={{0,1},{1,0},{2,3},{3,2},{4,5},{5,4},{6,7},{7,6},{8,9},{9,8},{10,11... | collective-permute-start | bytes 1044488 | tf_op jit(solution)/shard_map/ppermute | solution.py:44
  40.7 7.5 %collective-permute-start.14 = (bf16[80,2176]{1,0:T(8,128)(2,1)S(1)}, bf16[80,2176]{1,0:T(8,128)(2,1)S(1)}, u32[]{:S(2)}, u32[]{:S(2)}) collective-permute-start(bf16[80,2176]{1,0:T(8,128)(2,1)S(1)} %get-tuple-element.42), channel_id=1, source_target_pairs={{0,4},{1,3},{2,6},{3,1},{4,0},{5,7},{6,2},{7,5},{8,12},{9,11},{10,... | collective-permute-start | bytes 1044488 | tf_op jit(solution)/shard_map/ppermute | solution.py:44
  41.0 7.1 %collective-permute-start.21 = (bf16[80,2176]{1,0:T(8,128)(2,1)S(1)}, bf16[80,2176]{1,0:T(8,128)(2,1)S(1)}, u32[]{:S(2)}, u32[]{:S(2)}) collective-permute-start(bf16[80,2176]{1,0:T(8,128)(2,1)S(1)} %collective-permute-done.20.far_ref), channel_id=1, source_target_pairs={{0,1},{1,0},{2,3},{3,2},{4,5},{5,4},{6,7},{7,6},{8,9},{9,8},{10,11... | collective-permute-start | bytes 1044488 | tf_op jit(solution)/shard_map/ppermute | solution.py:44
  41.1 5.2 %copy-start = (bf16[1,384,4096]{2,1,0:T(8,128)(2,1)S(1)}, bf16[1,384,4096]{2,1,0:T(8,128)(2,1)}, u32[]{:S(2)}) copy-start(bf16[1,384,4096]{2,1,0:T(8,128)(2,1)} %param.13) | copy-start | bytes 9437188
  44.4 1.3 %collective-permute-start.10 = (bf16[160,384]{1,0:T(8,128)(2,1)S(1)}, bf16[160,384]{1,0:T(8,128)(2,1)S(1)}, u32[]{:S(2)}, u32[]{:S(2)}) collective-permute-start(bf16[160,384]{1,0:T(8,128)(2,1)S(1)} %hidden_units.4.mine_ref.after_ref), channel_id=1, source_target_pairs={{0,1},{1,0},{2,3},{3,2},{4,5},{5,4},{6,7},{7,6},{8,9},{9,8},{10,11... | collective-permute-start | bytes 368648 | tf_op jit(solution)/shard_map/ppermute | solution.py:44
  45.8 4.3 %collective-permute-start.16 = (bf16[80,2176]{1,0:T(8,128)(2,1)S(1)}, bf16[80,2176]{1,0:T(8,128)(2,1)S(1)}, u32[]{:S(2)}, u32[]{:S(2)}) collective-permute-start(bf16[80,2176]{1,0:T(8,128)(2,1)S(1)} %get-tuple-element.43.near_ref), channel_id=1, source_target_pairs={{0,1},{1,0},{2,3},{3,2},{4,5},{5,4},{6,7},{7,6},{8,9},{9,8},{10,11... | collective-permute-start | bytes 1044488 | tf_op jit(solution)/shard_map/ppermute | solution.py:44
  45.9 4.1 %collective-permute-start.18 = (bf16[80,2176]{1,0:T(8,128)(2,1)S(1)}, bf16[80,2176]{1,0:T(8,128)(2,1)S(1)}, u32[]{:S(2)}, u32[]{:S(2)}) collective-permute-start(bf16[80,2176]{1,0:T(8,128)(2,1)S(1)} %collective-permute-done.17.far_ref), channel_id=1, source_target_pairs={{0,1},{1,0},{2,3},{3,2},{4,5},{5,4},{6,7},{7,6},{8,9},{9,8},{10,11... | collective-permute-start | bytes 1044488 | tf_op jit(solution)/shard_map/ppermute | solution.py:44
  47.4 4.1 %collective-permute-start.13 = (bf16[80,2176]{1,0:T(8,128)(2,1)S(1)}, bf16[80,2176]{1,0:T(8,128)(2,1)S(1)}, u32[]{:S(2)}, u32[]{:S(2)}) collective-permute-start(bf16[80,2176]{1,0:T(8,128)(2,1)S(1)} %get-tuple-element.41.near_ref), channel_id=1, source_target_pairs={{0,1},{1,0},{2,3},{3,2},{4,5},{5,4},{6,7},{7,6},{8,9},{9,8},{10,11... | collective-permute-start | bytes 1044488 | tf_op jit(solution)/shard_map/ppermute | solution.py:44
  48.2 3.3 %collective-permute-start.15 = (bf16[80,2176]{1,0:T(8,128)(2,1)S(1)}, bf16[80,2176]{1,0:T(8,128)(2,1)S(1)}, u32[]{:S(2)}, u32[]{:S(2)}) collective-permute-start(bf16[80,2176]{1,0:T(8,128)(2,1)S(1)} %collective-permute-done.14.far_ref), channel_id=1, source_target_pairs={{0,1},{1,0},{2,3},{3,2},{4,5},{5,4},{6,7},{7,6},{8,9},{9,8},{10,11... | collective-permute-start | bytes 1044488 | tf_op jit(solution)/shard_map/ppermute | solution.py:44
  49.5 7.0 %collective-permute-start.23 = (bf16[160,384]{1,0:T(8,128)(2,1)S(1)}, bf16[160,384]{1,0:T(8,128)(2,1)S(1)}, u32[]{:S(2)}, u32[]{:S(2)}) collective-permute-start(bf16[160,384]{1,0:T(8,128)(2,1)S(1)} %hidden_units.5.after_ref.mine_ref), channel_id=1, source_target_pairs={{0,1},{1,0},{2,3},{3,2},{4,5},{5,4},{6,7},{7,6},{8,9},{9,8},{10,11... | collective-permute-start | bytes 368648 | tf_op jit(solution)/shard_map/ppermute | solution.py:44
  51.4 2.3 %collective-permute-start.24 = (bf16[160,384]{1,0:T(8,128)(2,1)S(1)}, bf16[160,384]{1,0:T(8,128)(2,1)S(1)}, u32[]{:S(2)}, u32[]{:S(2)}) collective-permute-start(bf16[160,384]{1,0:T(8,128)(2,1)S(1)} %hidden_units.6.after_ref.mine_ref), channel_id=1, source_target_pairs={{0,1},{1,0},{2,3},{3,2},{4,5},{5,4},{6,7},{7,6},{8,9},{9,8},{10,11... | collective-permute-start | bytes 368648 | tf_op jit(solution)/shard_map/ppermute | solution.py:44
  52.8 5.2 %collective-permute-start.22 = (bf16[160,384]{1,0:T(8,128)(2,1)S(1)}, bf16[160,384]{1,0:T(8,128)(2,1)S(1)}, u32[]{:S(2)}, u32[]{:S(2)}) collective-permute-start(bf16[160,384]{1,0:T(8,128)(2,1)S(1)} %hidden_units.7.after_ref.mine_ref), channel_id=1, source_target_pairs={{0,1},{1,0},{2,3},{3,2},{4,5},{5,4},{6,7},{7,6},{8,9},{9,8},{10,11... | collective-permute-start | bytes 368648 | tf_op jit(solution)/shard_map/ppermute | solution.py:44
  53.3 7.5 %collective-permute-start.12 = (bf16[80,2048]{1,0:T(8,128)(2,1)S(1)}, bf16[80,2048]{1,0:T(8,128)(2,1)S(1)}, u32[]{:S(2)}, u32[]{:S(2)}) collective-permute-start(bf16[80,2048]{1,0:T(8,128)(2,1)S(1)} %get-tuple-element.40), channel_id=1, source_target_pairs={{0,4},{1,3},{2,6},{3,1},{4,0},{5,7},{6,2},{7,5},{8,12},{9,11},{10,... | collective-permute-start | bytes 983048 | tf_op jit(solution)/shard_map/ppermute | solution.py:44
  54.7 9.2 %collective-permute-start.27 = (bf16[80,2048]{1,0:T(8,128)(2,1)S(1)}, bf16[80,2048]{1,0:T(8,128)(2,1)S(1)}, u32[]{:S(2)}, u32[]{:S(2)}) collective-permute-start(bf16[80,2048]{1,0:T(8,128)(2,1)S(1)} %get-tuple-element.53), channel_id=1, source_target_pairs={{0,4},{1,3},{2,6},{3,1},{4,0},{5,7},{6,2},{7,5},{8,12},{9,11},{10,... | collective-permute-start | bytes 983048 | tf_op jit(solution)/shard_map/ppermute | solution.py:44
  57.6 11.1 %collective-permute-start.29 = (bf16[80,2048]{1,0:T(8,128)(2,1)S(1)}, bf16[80,2048]{1,0:T(8,128)(2,1)S(1)}, u32[]{:S(2)}, u32[]{:S(2)}) collective-permute-start(bf16[80,2048]{1,0:T(8,128)(2,1)S(1)} %get-tuple-element.56), channel_id=1, source_target_pairs={{0,4},{1,3},{2,6},{3,1},{4,0},{5,7},{6,2},{7,5},{8,12},{9,11},{10,... | collective-permute-start | bytes 983048 | tf_op jit(solution)/shard_map/ppermute | solution.py:44
  59.1 16.6 %collective-permute-start.26 = (bf16[80,2048]{1,0:T(8,128)(2,1)S(1)}, bf16[80,2048]{1,0:T(8,128)(2,1)S(1)}, u32[]{:S(2)}, u32[]{:S(2)}) collective-permute-start(bf16[80,2048]{1,0:T(8,128)(2,1)S(1)} %get-tuple-element.52), channel_id=1, source_target_pairs={{0,4},{1,3},{2,6},{3,1},{4,0},{5,7},{6,2},{7,5},{8,12},{9,11},{10,... | collective-permute-start | bytes 983048 | tf_op jit(solution)/shard_map/ppermute | solution.py:44
  64.2 8.6 %collective-permute-start.28 = (bf16[64,2048]{1,0:T(8,128)(2,1)S(1)}, bf16[64,2048]{1,0:T(8,128)(2,1)S(1)}, u32[]{:S(2)}, u32[]{:S(2)}) collective-permute-start(bf16[64,2048]{1,0:T(8,128)(2,1)S(1)} %get-tuple-element.55), channel_id=1, source_target_pairs={{0,2},{1,5},{2,0},{3,7},{4,6},{5,1},{6,4},{7,3},{8,10},{9,13},{10,... | collective-permute-start | bytes 786440 | tf_op jit(solution)/shard_map/ppermute | solution.py:44
  69.0 9.5 %collective-permute-start.32 = (bf16[64,2048]{1,0:T(8,128)(2,1)S(1)}, bf16[64,2048]{1,0:T(8,128)(2,1)S(1)}, u32[]{:S(2)}, u32[]{:S(2)}) collective-permute-start(bf16[64,2048]{1,0:T(8,128)(2,1)S(1)} %get-tuple-element.60), channel_id=1, source_target_pairs={{0,2},{1,5},{2,0},{3,7},{4,6},{5,1},{6,4},{7,3},{8,10},{9,13},{10,... | collective-permute-start | bytes 786440 | tf_op jit(solution)/shard_map/ppermute | solution.py:44
  76.0 6.4 %collective-permute-start.30 = (bf16[64,2048]{1,0:T(8,128)(2,1)S(1)}, bf16[64,2048]{1,0:T(8,128)(2,1)S(1)}, u32[]{:S(2)}, u32[]{:S(2)}) collective-permute-start(bf16[64,2048]{1,0:T(8,128)(2,1)S(1)} %get-tuple-element.59), channel_id=1, source_target_pairs={{0,2},{1,5},{2,0},{3,7},{4,6},{5,1},{6,4},{7,3},{8,10},{9,13},{10,... | collective-permute-start | bytes 786440 | tf_op jit(solution)/shard_map/ppermute | solution.py:44
  77.2 9.2 %collective-permute-start.31 = (bf16[64,2048]{1,0:T(8,128)(2,1)S(1)}, bf16[64,2048]{1,0:T(8,128)(2,1)S(1)}, u32[]{:S(2)}, u32[]{:S(2)}) collective-permute-start(bf16[64,2048]{1,0:T(8,128)(2,1)S(1)} %add_rows.6.after_ref), channel_id=1, source_target_pairs={{0,8},{1,9},{2,10},{3,11},{4,12},{5,13},{6,14},{7,15},{8,0},{9,1},... | collective-permute-start | bytes 786440 | tf_op jit(solution)/shard_map/ppermute | solution.py:44
  78.0 10.1 %collective-permute-start.25 = (bf16[64,2048]{1,0:T(8,128)(2,1)S(1)}, bf16[64,2048]{1,0:T(8,128)(2,1)S(1)}, u32[]{:S(2)}, u32[]{:S(2)}) collective-permute-start(bf16[64,2048]{1,0:T(8,128)(2,1)S(1)} %get-tuple-element.51), channel_id=1, source_target_pairs={{0,2},{1,5},{2,0},{3,7},{4,6},{5,1},{6,4},{7,3},{8,10},{9,13},{10,... | collective-permute-start | bytes 786440 | tf_op jit(solution)/shard_map/ppermute | solution.py:44
  78.5 11.8 %collective-permute-start.33 = (bf16[64,2048]{1,0:T(8,128)(2,1)S(1)}, bf16[64,2048]{1,0:T(8,128)(2,1)S(1)}, u32[]{:S(2)}, u32[]{:S(2)}) collective-permute-start(bf16[64,2048]{1,0:T(8,128)(2,1)S(1)} %add_rows.7.refs_3_), channel_id=1, source_target_pairs={{0,8},{1,9},{2,10},{3,11},{4,12},{5,13},{6,14},{7,15},{8,0},{9,1},... | collective-permute-start | bytes 786440 | tf_op jit(solution)/shard_map/ppermute | solution.py:44
  86.5 9.2 %collective-permute-start.34 = (bf16[64,2048]{1,0:T(8,128)(2,1)S(1)}, bf16[64,2048]{1,0:T(8,128)(2,1)S(1)}, u32[]{:S(2)}, u32[]{:S(2)}) collective-permute-start(bf16[64,2048]{1,0:T(8,128)(2,1)S(1)} %add_rows.8.refs_2_), channel_id=1, source_target_pairs={{0,24},{1,25},{2,26},{3,27},{4,28},{5,29},{6,30},{7,31},{8,16},{9,... | collective-permute-start | bytes 786440 | tf_op jit(solution)/shard_map/ppermute | solution.py:44
